TPU v7x, 32 devices: a whole 2x2x4 slice. The times are simulated.
32 devices in a mesh: parts: 2 (over y), inner: 4 (over z), grp: 4 (over x, core).
Axes of the slice: x: 2, y: 2, z: 4, core: 2. Of those that a mesh axis runs over, the one named last changes fastest.
Arguments:
- cotangent: bfloat16 [1024, 8192], P(('parts', 'inner'), 'grp'), parts along dimension 0, may hold values from -1.5 to 1.5
- down_weight: bfloat16 [26624, 8192], P('inner', 'grp'), may hold values from -0.09375 to 0.09375
- pre_acts: bfloat16 [2, 26624, 1024], P(None, ('inner', 'grp'), 'parts'), parts along dimension 2, may hold values from -6 to 6
Outputs:
- grad_pre: bfloat16 [2, 26624, 1024], P(None, ('inner', 'grp'), 'parts'), parts along dimension 2
- grad_down: bfloat16 [53248, 8192], P(('parts', 'inner'), 'grp'), parts along dimension 0
There are 2 independent parts, one for each index of `parts`. A program takes and returns all parts, laid end to end along the dimension named above; an argument that names none is the same for every part. Nothing has to cross between parts.
All inputs are finite; a program needn't handle non-finite values.
Results may differ from a plain program's by a relative error of at most 0.005.
Values may be sent and summed in bfloat16 or wider, within the bound.
No kernel may reach another device: no remote copies, remote signals or barrier semaphores. Data moves between devices by JAX's collectives and lax.ppermute only.
A program may use at most 192 MiB of HBM per device.

v0:
```python
import jax
import jax.numpy as jnp
from jax import lax
from jax.sharding import PartitionSpec as P


def gated_step(hidden_grad, acts):
    gate = acts[0].astype(jnp.float32)
    upper = acts[1].astype(jnp.float32)
    sigm = jax.nn.sigmoid(gate)
    active = gate * sigm
    hidden = (active * upper).astype(jnp.bfloat16)
    grad_gate = hidden_grad * upper * sigm * (1.0 + gate * (1.0 - sigm))
    grad_upper = hidden_grad * active
    return (hidden, jnp.stack([grad_gate, grad_upper]).astype(jnp.bfloat16))


def on_device(cotangent, down_weight, pre_acts):
    all_rows = lax.all_gather(cotangent, "inner", axis=0, tiled=True)
    hidden_grad = lax.psum_scatter(
        jnp.einsum("fd,td->ft", down_weight, all_rows, preferred_element_type=jnp.float32),
        "grp",
        scatter_dimension=0,
        tiled=True,
    )
    hidden, grad_pre = gated_step(hidden_grad, pre_acts)
    grad_down = jnp.dot(
        lax.all_gather(hidden, "grp", axis=0, tiled=True),
        all_rows,
        preferred_element_type=jnp.float32,
    ).astype(jnp.bfloat16)
    return (grad_pre, grad_down)


def solution(mesh):
    return jax.shard_map(
        on_device,
        mesh=mesh,
        in_specs=(
            P(("parts", "inner"), "grp"),
            P("inner", "grp"),
            P(None, ("inner", "grp"), "parts"),
        ),
        out_specs=(P(None, ("inner", "grp"), "parts"), P(("parts", "inner"), "grp")),
        check_vma=False,
    )
```

profile of v0, /device:TPU:0, one launch (start us, length us, event | category | flops | bytes accessed | tf_op | source)
XLA Modules:
  0.0 267.5 jit_solution(2922200961141765230)
XLA Ops:
  7.2 0.0 all-gather.3.cloned.1.call-start
  7.2 0.7 all-gather.3.cloned.1.call-update
  7.9 0.0 reduce-scatter.2.cloned.1.call-start
  7.9 50.3 %all-gather.3.cloned.1.call-done = bf16[512,2048]{1,0:T(8,128)(2,1)} async-done(((bf16[128,2048]{1,0:T(8,128)(2,1)}), bf16[512,2048]{1,0:T(8,128)(2,1)}) %all-gather.3.cloned.1.call-update) | async-done | bytes 2097168 | tf_op jit(solution)/shard_map/all_gather | solution.py:19
  58.2 23.0 %fusion.10 = f32[6656,512]{1,0:T(8,128)} fusion(bf16[6656,2048]{1,0:T(8,128)(2,1)} %param.4, bf16[512,2048]{1,0:T(8,128)(2,1)} %all-gather.3.cloned.1.call-done), kind=kOutput, calls=%fused_computation.18 | convolution fusion | flops 13958643712 | bytes 42991616 | tf_op jit(solution)/shard_map/fd,td->ft/dot_general | solution.py:21
  81.2 0.0 reduce-scatter.2.cloned.1.call-update
  81.2 0.2 all-gather.5.cloned.1.call-start
  81.5 104.6 %reduce-scatter.2.cloned.1.call-done = f32[1664,512]{1,0:T(8,128)} async-done(((f32[6656,512]{1,0:T(8,128)}), f32[1664,512]{1,0:T(8,128)}) %reduce-scatter.2.cloned.1.call-update) | async-done | bytes 3407888 | tf_op jit(solution)/shard_map/reduce_scatter | solution.py:20
  186.0 4.8 %fusion.9 = (bf16[1,1664,512]{2,1,0:T(8,128)(2,1)S(1)}, bf16[1,1664,512]{2,1,0:T(8,128)(2,1)S(1)}, bf16[1664,512]{1,0:T(8,128)(2,1)}) fusion(f32[1664,512]{1,0:T(8,128)} %reduce-scatter.2.cloned.1.call-done, bf16[2,1664,512]{2,1,0:T(8,128)(2,1)} %param.5), kind=kLoop, calls=%fused_computation.17 | loop fusion | flops 14483456 | bytes 11927552 | tf_op jit(solution)/shard_map/stack | solution.py:15
  190.8 0.0 all-gather.5.cloned.1.call-update
  190.9 2.0 pad_maximum_fusion
  192.9 47.5 %all-gather.5.cloned.1.call-done = bf16[6656,512]{1,0:T(8,128)(2,1)} async-done(((bf16[1664,512]{1,0:T(8,128)(2,1)}), bf16[6656,512]{1,0:T(8,128)(2,1)}) %all-gather.5.cloned.1.call-update) | async-done | bytes 6815760 | tf_op jit(solution)/shard_map/all_gather | solution.py:28
  240.4 20.6 %convolution_convert_fusion = bf16[6656,2048]{1,0:T(8,128)(2,1)} fusion(bf16[6656,512]{1,0:T(8,128)(2,1)} %all-gather.5.cloned.1.call-done, bf16[512,2048]{1,0:T(8,128)(2,1)} %all-gather.3.cloned.1.call-done), kind=kOutput, calls=%fused_computation | convolution fusion | flops 13972275200 | bytes 36175872 | tf_op jit(solution)/shard_map/dot_general | solution.py:27
Async XLA Ops:
  7.2 51.1 %all-gather.3.cloned.1.call-start = ((), (), s32[]{:S(2)}) async-start(), calls=%async_computation.1 | async-start | bytes 2621440 | tf_op jit(solution)/shard_map/all_gather | solution.py:19
  7.9 178.1 %reduce-scatter.2.cloned.1.call-start = ((), (), s32[]{:S(2)}) async-start(), calls=%async_computation.2 | async-start | bytes 17039360 | tf_op jit(solution)/shard_map/reduce_scatter | solution.py:20
  81.2 159.2 %all-gather.5.cloned.1.call-start = ((), (), s32[]{:S(2)}) async-start(), calls=%async_computation.3 | async-start | bytes 8519680 | tf_op jit(solution)/shard_map/all_gather | solution.py:28
Sparse Core Ops, SparseCore 0:
  9.6 48.6 all-gather.2
  81.3 104.6 reduce-scatter.1
  191.0 49.3 all-gather.4
where the time goes:
time: 268 us
  waiting for transfers between devices  203 us (76%)
  matrix products  43.6 us (16%)
  between operations  13.7 us (5%)
  other arithmetic  6.84 us (3%)
    reduce_scatter x1, waiting for transfers between devices, on_device(): lax.psum_scatter(jnp.einsum('fd,td->ft', down_weight, all_rows, preferred...  105 us
    all_gather x1, waiting for transfers between devices, on_device(): all_rows = lax.all_gather(cotangent, 'inner', axis=0, tiled=True)  50.3 us
    all_gather x1, waiting for transfers between devices, on_device(): lax.all_gather(hidden, 'grp', axis=0, tiled=True)  47.5 us
    dot_general x1, matrix products, on_device(): jnp.einsum('fd,td->ft', down_weight, all_rows, preferred_element_type=jnp...  23 us
    dot_general x1, matrix products, on_device(): jnp.dot(lax.all_gather(hidden, 'grp', axis=0, tiled=True), all_rows, pref...  20.6 us
    another operation x2, other arithmetic, gated_step(): return (hidden, jnp.stack([grad_gate, grad_upper]).astype(jnp.bfloat16))  6.84 us
  transfers between devices with their start and end apart: 3, of which 3 were waited for; matrix products, arithmetic and copies ran while one was open for 1% of the time, Pallas kernels for 0%

commit v1 on v0

v1 whole, which is shorter than its diff:
```python
import functools
import math

import jax
import jax.numpy as jnp
import numpy as np
from jax import lax
from jax.experimental import pallas as pl
from jax.experimental.pallas import tpu as pltpu
from jax.sharding import PartitionSpec as P

LANES = 128
MIB = 1024 * 1024


def in_vmem(array):
    return pltpu.with_memory_space_constraint(array, pltpu.VMEM), pl.BlockSpec(memory_space=pltpu.VMEM)


def in_hbm(array):
    return pltpu.with_memory_space_constraint(array, pltpu.HBM), pl.BlockSpec(memory_space=pltpu.HBM)


def anywhere(array):
    return array, pl.BlockSpec(memory_space=pl.ANY)


def sigmoid(x):
    return 0.5 * jnp.tanh(0.5 * x) + 0.5


def hidden_of(acts):
    gate = acts[0].astype(jnp.float32)
    upper = acts[1].astype(jnp.float32)
    return (gate * sigmoid(gate) * upper).astype(jnp.bfloat16)


def tile_of(rows, most):
    return max(t for t in range(16, most + 1, 16) if rows % t == 0)


TOKEN = (jax.ShapeDtypeStruct((8, LANES), jnp.float32), pl.BlockSpec((8, LANES), lambda *_: (0, 0)))


def call(kernel, name, meta, grid, ins, outs, scratch=(), alias=None, after=(), weight=1, vmem=16):
    ins = list(ins) + [anywhere(a) for a in after]
    read = len(ins) - len(after)
    aliases = {}
    if alias is not None:
        aliases = {1 + len(ins): len(outs) - 1}
        ins.append(in_hbm(alias))
    outs = list(outs) + [TOKEN]

    def body(meta_ref, *refs):
        refs = list(refs)
        token = refs.pop(len(ins) + len(outs) - 1)
        token[...] = jnp.zeros_like(token)
        kernel(meta_ref, *refs[:read], *refs[len(ins) :])

    return pl.pallas_call(
        body,
        grid_spec=pltpu.PrefetchScalarGridSpec(
            num_scalar_prefetch=1, grid=grid, in_specs=[s for _, s in ins], out_specs=[s for _, s in outs], scratch_shapes=list(scratch)
        ),
        out_shape=[s for s, _ in outs],
        input_output_aliases=aliases,
        compiler_params=pltpu.CompilerParams(vmem_limit_bytes=vmem * MIB),
        cost_estimate=pl.CostEstimate(flops=weight, bytes_accessed=1, transcendentals=0),
        name=name,
    )(meta, *[a for a, _ in ins])


def hidden_rows(acts, pieces):
    _, rows, tokens = acts.shape
    tile = math.gcd(*pieces)
    starts = [sum(pieces[:p]) for p in range(len(pieces))]

    def kernel(acts_ref, *refs):
        out_refs, (buf, sems) = refs[: len(pieces)], refs[len(pieces) :]

        def load(p):
            here = pl.ds(starts[p], pieces[p])
            return pltpu.make_async_copy(acts_ref.at[:, here, :], buf.at[:, here, :], sems.at[p])

        for p in range(len(pieces)):
            load(p).start()
        for p, ref in enumerate(out_refs):
            load(p).wait()

            @pl.loop(0, pieces[p] // tile)
            def _(i):
                at = pl.multiple_of(i * tile, tile)
                ref[pl.ds(at, tile), :] = hidden_of(buf[:, pl.ds(starts[p] + at, tile), :])

    array, spec = in_hbm(acts)
    return pl.pallas_call(
        kernel,
        in_specs=[spec],
        out_specs=[pl.BlockSpec(memory_space=pltpu.VMEM)] * len(pieces),
        out_shape=[pltpu.VMEM((n, tokens), acts.dtype) for n in pieces],
        scratch_shapes=[pltpu.VMEM(acts.shape, acts.dtype), pltpu.SemaphoreType.DMA((len(pieces),))],
        compiler_params=pltpu.CompilerParams(vmem_limit_bytes=12 * MIB),
        cost_estimate=pl.CostEstimate(flops=1, bytes_accessed=1, transcendentals=0),
        name="hidden",
    )(array)


class Slot:
    def __init__(self, number, blocks):
        self.number, self.blocks = number, blocks

    def start(self, meta_ref, refs, target, sem):
        offset = meta_ref[1 + self.number] - meta_ref[1]
        for key, ref in zip(self.blocks, refs, strict=True):

            @pl.when(offset == key)
            def _():
                pltpu.make_async_copy(ref, target, sem).start()

    def wait(self, refs, target, sem):
        pltpu.make_async_copy(refs[0], target, sem).wait()


def fetch(slots, meta_ref, refs, targets, sems):
    waits = []
    for n, slot in enumerate(slots):
        mine, refs = refs[: len(slot.blocks)], refs[len(slot.blocks) :]
        slot.start(meta_ref, mine, targets[n], sems.at[n])
        waits.append(functools.partial(slot.wait, mine, targets[n], sems.at[n]))
    return lambda: [wait() for wait in waits]


def blocks_of(slots):
    return [(block, pl.BlockSpec(memory_space=pl.ANY)) for slot in slots for block in slot.blocks.values()]


def clamped(first, steps):
    return lambda k: jnp.clip(k - first, 0, steps - 1)


def partials(meta, masks, weight, rows, tokens, dtypes, splits, slots=None, turned=None, adds=None, after=()):
    feats = weight.shape[1]
    tile = rows // 4
    steps = rows // tile
    total = len(masks) * steps
    blocks = blocks_of(slots) if slots else [in_vmem(turned)]
    each = tokens // len(slots) if slots else 0
    extra = [a for group in adds or [] for a in group]
    per = len(extra) // len(masks)

    def kernel(meta_ref, w_ref, *refs):
        block_refs, refs = refs[: len(blocks)], refs[len(blocks) :]
        add_refs, refs = refs[: len(extra)], refs[len(extra) :]
        out_refs, refs = refs[: len(masks) * splits], refs[len(masks) * splits :]
        if slots:
            turned_ref, buf, w_sems, rows_buf, sems = refs
        else:
            turned_ref, (buf, w_sems) = block_refs[0], refs
        k = pl.program_id(0)

        def copy(step):
            block = meta_ref[0] ^ masks[step // steps]
            at = pl.multiple_of(block * rows + step % steps * tile, tile)
            return pltpu.make_async_copy(w_ref.at[pl.ds(at, tile), :], buf.at[pl.ds(step * tile, tile), :], w_sems.at[step])

        @pl.when(k == 0)
        def _():
            if slots:
                targets = [rows_buf.at[pl.ds(n * each, each), :] for n in range(len(slots))]
                wait = fetch(slots, meta_ref, block_refs, targets, sems)
            for step in range(total):
                copy(step).start()
            if slots:
                wait()
                turned_ref[...] = rows_buf[...].T

        for step in range(total):

            @pl.when(k == step)
            def _():
                copy(step).wait()

        w = buf[pl.ds(pl.multiple_of(k * tile, tile), tile), :]
        out = jnp.dot(w, turned_ref[...], preferred_element_type=jnp.float32)
        for step in range(total):
            j, i = step // steps, step % steps

            @pl.when(k == step)
            def _():
                value = out
                if extra:
                    value = value + add_refs[j * per + i * per // steps][...].astype(jnp.float32)
                out_refs[j * splits + i * splits // steps][...] = value.astype(dtypes[j])

    def spec(j, p, count):
        index = clamped(j * steps + p * steps // count, steps // count)
        return pl.BlockSpec((tile, tokens), lambda k, m: (index(k), 0))

    ins = [in_hbm(weight), *blocks]
    ins += [(piece, spec(n // per, n % per, per)) for n, piece in enumerate(extra)]
    outs = [
        (jax.ShapeDtypeStruct((rows // splits, tokens), dtype), spec(j, p, splits)) for j, dtype in enumerate(dtypes) for p in range(splits)
    ]
    scratch = [pltpu.VMEM((total * tile, feats), weight.dtype), pltpu.SemaphoreType.DMA((total,))]
    if slots:
        outs.append((pltpu.VMEM((feats, tokens), weight.dtype), pl.BlockSpec(memory_space=pltpu.VMEM)))
        scratch += [pltpu.VMEM((tokens, feats), weight.dtype), pltpu.SemaphoreType.DMA((len(slots),))]
    return call(kernel, "partials", meta, (total,), ins, outs, scratch, after=after, vmem=24)


def all_slots(meta, slots, each, feats, after=()):
    blocks = blocks_of(slots)

    def kernel(meta_ref, *refs):
        block_refs, (out_ref, sems) = refs[: len(blocks)], refs[len(blocks) :]
        starts = [pl.multiple_of(meta_ref[1 + slot.number] * each, each) for slot in slots]
        fetch(slots, meta_ref, block_refs, [out_ref.at[pl.ds(at, each), :] for at in starts], sems)()

    shape = pltpu.VMEM((len(slots) * each, feats), jnp.bfloat16)
    outs = [(shape, pl.BlockSpec(memory_space=pltpu.VMEM))]
    return call(kernel, "token_rows", meta, (1,), blocks, outs, [pltpu.SemaphoreType.DMA((len(slots),))], after=after, vmem=4)


def weight_grad(meta, masks, hiddens, cots, out, total_rows, after=(), weight=1):
    tokens, feats = cots.shape
    sizes = [p.shape[0] for p in hiddens[0]]
    rows = sum(sizes)
    tile = rows // 2
    steps = rows // tile
    flat = [p for pieces in hiddens for p in pieces]

    def kernel(meta_ref, cot_ref, *refs):
        piece_refs, (out_ref,) = refs[: len(flat)], refs[len(flat) :]
        for step in range(len(masks) * steps):

            @pl.when(pl.program_id(0) == step)
            def _():
                j, low = step // steps, step % steps * tile
                parts, at = [], 0
                for p, size in enumerate(sizes):
                    first, last = max(low, at), min(low + tile, at + size)
                    if first < last:
                        parts.append(piece_refs[j * len(sizes) + p][first - at : last - at, :])
                    at += size
                h = parts[0] if len(parts) == 1 else jnp.concatenate(parts)
                out_ref[...] = jnp.dot(h, cot_ref[...], preferred_element_type=jnp.float32).astype(out_ref.dtype)

    def place(k, m):
        block = m[0] ^ masks[0]
        for j in range(1, len(masks)):
            block = jnp.where(k // steps == j, m[0] ^ masks[j], block)
        return block * steps + k % steps, 0

    return call(
        kernel, "weight_grad", meta, (len(masks) * steps,),
        [in_vmem(cots), *[in_vmem(p) for p in flat]],
        [(jax.ShapeDtypeStruct((total_rows, feats), cots.dtype), pl.BlockSpec((tile, feats), place))],
        alias=out, after=after, weight=weight, vmem=18,
    )


def gate_grad(meta, first, start, acts, own, far, out, after=()):
    rows, tokens = far.shape
    tile = rows // 4

    def kernel(meta_ref, acts_ref, own_ref, far_ref, out_ref):
        i, j = pl.program_id(0), pl.program_id(1)
        columns = pl.ds(pl.multiple_of(meta_ref[1 + first + j] * LANES, LANES), LANES)
        lanes = pl.ds(pl.multiple_of(j * LANES, LANES), LANES)
        here = pl.ds(pl.multiple_of(i * tile, tile), tile)
        there = pl.ds(pl.multiple_of(start + i * tile, tile), tile)
        grad = own_ref[here, lanes] + far_ref[here, lanes].astype(jnp.float32)
        gate = acts_ref[0, there, columns].astype(jnp.float32)
        upper = acts_ref[1, there, columns].astype(jnp.float32)
        sigm = sigmoid(gate)
        out_ref[0] = (grad * upper * sigm * (1.0 + gate * (1.0 - sigm))).astype(out_ref.dtype)
        out_ref[1] = (grad * (gate * sigm)).astype(out_ref.dtype)

    spec = pl.BlockSpec((2, tile, LANES), lambda i, j, m: (0, start // tile + i, m[1 + first + j]))
    return call(
        kernel, "gate_grad", meta, (rows // tile, tokens // LANES),
        [in_vmem(acts), in_vmem(own), in_vmem(far)],
        [(jax.ShapeDtypeStruct(acts.shape, acts.dtype), spec)],
        alias=out, after=after, vmem=6,
    )


def arrivals(size):
    return [sorted((k for k in range(size) if k != z), key=lambda k: (abs(k - z), (k - z) * (1 if z % 2 else -1))) for z in range(size)]


def along(block, axis, size, step, first=0):
    left = lax.ppermute(block[0], axis, [(k, k + step) for k in range(first, size - step)])
    right = lax.ppermute(block[1], axis, [(k + step, k) for k in range(size - step - first)])
    return left, right


def slot_of(got, s, size):
    order = arrivals(size)
    offsets = {order[k][s - 1] - k for k in range(size)}
    return Slot(s, {offset: got[offset] for offset in sorted(offsets)})


def describe(me, z, size):
    order = arrivals(size)
    tables = [np.array([0, k, *order[k]], np.int32) for k in range(size)]
    meta = jnp.asarray(tables[0])
    for k in range(1, size):
        meta = jnp.where(z == k, tables[k], meta)
    return meta + me * np.array([1] + [0] * size, np.int32)


def two_level(inner, cotangent, down_weight, pre_acts):
    me, z = lax.axis_index("grp"), lax.axis_index("inner")
    total_rows = down_weight.shape[0]
    rows = pre_acts.shape[1]
    across_core = functools.partial(lax.ppermute, axis_name="grp", perm=[(k, k ^ 1) for k in range(4)])
    across_x = functools.partial(lax.ppermute, axis_name="grp", perm=[(k, k ^ 2) for k in range(4)])
    meta = describe(me, z, inner)
    bf16, f32 = jnp.bfloat16, jnp.float32

    unit = rows // 26
    hidden = hidden_rows(pre_acts, (12 * unit, 7 * unit, 7 * unit))
    hidden, cotangent = lax.optimization_barrier((hidden, cotangent))
    hidden_far = [across_x(h) for h in hidden]

    each, feats = cotangent.shape
    got = {}
    pair = (cotangent, cotangent)
    for step in range(1, inner):
        pair = along(pair, "inner", inner, 1, step - 1)
        got[-step], got[step] = pair
    slots = [Slot(0, {0: cotangent})] + [slot_of(got, s, inner) for s in range(1, inner)]
    hidden_core = [across_core(h) for h in hidden]

    half = inner // 2
    tokens = half * each

    *sent, turned, _ = partials(meta, (3, 1), down_weight, rows, tokens, (bf16, bf16), 2, slots[:half], after=(hidden_far[0],))
    back = [across_core(p) for p in sent]
    a_sum, a_own, done = partials(
        meta, (2, 0), down_weight, rows, tokens, (bf16, f32), 1, turned=turned, adds=(back[:2], back[2:]), after=(hidden_far[1],)
    )
    a_far = across_x(a_sum)

    *sent, turned, done = partials(
        meta, (3, 1), down_weight, rows, tokens, (bf16, bf16), 2, slots[half:], after=(done, hidden_far[2])
    )
    back = [across_core(p) for p in sent]
    cots, done = all_slots(meta, slots, each, feats, after=(done,))
    b_sum0, b_sum1, b_own0, b_own1, done = partials(
        meta, (2, 0), down_weight, rows, tokens, (bf16, f32), 2, turned=turned, adds=(back[:2], back[2:]), after=(done,)
    )
    b_far0, b_far1 = across_x(b_sum0), across_x(b_sum1)
    hidden_both = [across_core(h) for h in hidden_far]

    grad_down, done = weight_grad(meta, (0, 1), (hidden, hidden_core), cots, None, total_rows, after=(done,))
    grad_pre, done = gate_grad(meta, 0, 0, pre_acts, a_own, a_far, None, after=(done,))
    grad_down, done = weight_grad(
        meta, (2, 3), (hidden_far, hidden_both), cots, grad_down, total_rows, after=(done,), weight=100 * 10**9
    )
    grad_pre, done = gate_grad(meta, half, 0, pre_acts, b_own0, b_far0, grad_pre, after=(done,))
    grad_pre, _ = gate_grad(meta, half, rows // 2, pre_acts, b_own1, b_far1, grad_pre, after=(done,))
    return grad_pre, grad_down


def plain(cotangent, down_weight, pre_acts):
    all_rows = lax.all_gather(cotangent, "inner", axis=0, tiled=True)
    hidden = hidden_of(pre_acts)
    grad = lax.psum_scatter(
        jnp.einsum("fd,td->ft", down_weight, all_rows, preferred_element_type=jnp.float32),
        "grp",
        scatter_dimension=0,
        tiled=True,
    )
    gate = pre_acts[0].astype(jnp.float32)
    upper = pre_acts[1].astype(jnp.float32)
    sigm = jax.nn.sigmoid(gate)
    grad_gate = grad * upper * sigm * (1.0 + gate * (1.0 - sigm))
    grad_pre = jnp.stack([grad_gate, grad * (gate * sigm)]).astype(jnp.bfloat16)
    grad_down = jnp.dot(
        lax.all_gather(hidden, "grp", axis=0, tiled=True), all_rows, preferred_element_type=jnp.float32
    ).astype(jnp.bfloat16)
    return grad_pre, grad_down


def solution(mesh):
    inner, grp = mesh.shape["inner"], mesh.shape["grp"]

    def on_device(cotangent, down_weight, pre_acts):
        if grp == 4 and inner % 2 == 0 and cotangent.shape[0] == LANES:
            return two_level(inner, cotangent, down_weight, pre_acts)
        return plain(cotangent, down_weight, pre_acts)

    return jax.shard_map(
        on_device,
        mesh=mesh,
        in_specs=(
            P(("parts", "inner"), "grp"),
            P("inner", "grp"),
            P(None, ("inner", "grp"), "parts"),
        ),
        out_specs=(P(None, ("inner", "grp"), "parts"), P(("parts", "inner"), "grp")),
        check_vma=False,
    )
```

time: 268 us -> 111 us (0.41)
  waiting for transfers between devices: 203 us -> 19.2 us
  Pallas kernels: 0 us -> 69.7 us
  matrix products: 43.6 us -> 0 us
  starting transfers between devices: 0.3 us -> 18.9 us
  between operations: 13.7 us -> 0.94 us
  other arithmetic: 6.84 us -> 0.01 us
    reduce_scatter x1 -> x0, waiting for transfers between devices: 105 us -> none  [on_device(): lax.psum_scatter(jnp.einsum('fd,td->ft', down_weight, all_rows, preferred...]
    all_gather x2 -> x0, waiting for transfers between devices: 97.8 us -> none  [the longest x1 50.3 us: on_device(): all_rows = lax.all_gather(cotangent, 'inner', axis=0, tiled=True)]
    pallas_call x0 -> x11, Pallas kernels: none -> 69.7 us  [the longest x10 66.4 us: call(): pl.pallas_call(body, grid_spec=pltpu.PrefetchScalarGridSpec(num_scalar_pr...]
    dot_general x2 -> x0, matrix products: 43.6 us -> none  [the longest x1 23 us: on_device(): jnp.einsum('fd,td->ft', down_weight, all_rows, preferred_element_type=jnp...]
    ppermute x0 -> x26, waiting for transfers between devices: none -> 19.2 us  [the longest x3 12.3 us: along(): lax.ppermute(block[1], axis, [(k + step, k) for k in range(size - step -...]
    ppermute x0 -> x26, starting transfers between devices: none -> 18.9 us  [the longest x3 5.97 us: along(): lax.ppermute(block[0], axis, [(k, k + step) for k in range(first, size -...]
    another operation x2 -> x0, other arithmetic: 6.84 us -> none  [gated_step(): return (hidden, jnp.stack([grad_gate, grad_upper]).astype(jnp.bfloat16))]
  transfers between devices with their start and end apart: 3 -> 26, of which waited for: 3 -> 11; matrix products, arithmetic and copies ran while one was open for 1% -> 0% of each run, Pallas kernels for 0% -> 57%
where the time goes in v1:
time: 111 us; the launch traced here: 110 us
  Pallas kernels  69.7 us (63%)
  waiting for transfers between devices  19.2 us (17%)
  starting transfers between devices  18.9 us (17%)
    pallas_call x10, Pallas kernels, call(): pl.pallas_call(body, grid_spec=pltpu.PrefetchScalarGridSpec(num_scalar_pr...  66.4 us
    ppermute x3, waiting for transfers between devices, along(): lax.ppermute(block[1], axis, [(k + step, k) for k in range(size - step -...  12.3 us
    ppermute x3, starting transfers between devices, along(): lax.ppermute(block[0], axis, [(k, k + step) for k in range(first, size -...  5.97 us
    ppermute x3, waiting for transfers between devices, two_level(): hidden_far = [across_x(h) for h in hidden]  4.41 us
    ppermute x3, starting transfers between devices, two_level(): hidden_far = [across_x(h) for h in hidden]  3.86 us
    ppermute x3, starting transfers between devices, along(): lax.ppermute(block[1], axis, [(k + step, k) for k in range(size - step -...  3.84 us
    pallas_call x1, Pallas kernels, hidden_rows(): pl.pallas_call(kernel, in_specs=[spec], out_specs=[pl.BlockSpec(memory_sp...  3.33 us
    ppermute x8, waiting for transfers between devices, two_level(): back = [across_core(p) for p in sent]  2.44 us
  transfers between devices with their start and end apart: 26, of which 11 were waited for; matrix products, arithmetic and copies ran while one was open for 0% of the time, Pallas kernels for 57%

profile of v1, /device:TPU:0, one launch (start us, length us, event | category | flops | bytes accessed | tf_op | source)
XLA Modules:
  0.0 109.5 jit_solution(732413356018333813)
XLA Ops:
  0.7 3.3 %hidden.1 = (bf16[768,512]{1,0:T(8,128)(2,1)S(1)}, bf16[448,512]{1,0:T(8,128)(2,1)}, bf16[448,512]{1,0:T(8,128)(2,1)S(1)}) custom-call(bf16[2,1664,512]{2,1,0:T(8,128)(2,1)} %refs_0_.14), custom_call_target="tpu_custom_call" | custom-call | flops 1 | bytes 1 | tf_op jit(solution)/shard_map/hidden/pallas_call | solution.py:96
  4.0 0.8 copy-done.2
  4.8 2.9 %collective-permute-start.6 = (bf16[768,512]{1,0:T(8,128)(2,1)S(1)}, bf16[768,512]{1,0:T(8,128)(2,1)S(1)}, u32[]{:S(2)}, u32[]{:S(2)}) collective-permute-start(bf16[768,512]{1,0:T(8,128)(2,1)S(1)} %get-tuple-element.43.refs_1_), channel_id=1, source_target_pairs={{0,2},{1,3},{2,0},{3,1},{4,6},{5,7},{6,4},{7,5},{8,10},{9,11},{10,... | collective-permute-start | bytes 2359304 | tf_op jit(solution)/shard_map/ppermute | solution.py:325
  7.8 1.3 %collective-permute-start.2 = (bf16[128,2048]{1,0:T(8,128)(2,1)S(1)}, bf16[128,2048]{1,0:T(8,128)(2,1)S(1)}, u32[]{:S(2)}, u32[]{:S(2)}) collective-permute-start(bf16[128,2048]{1,0:T(8,128)(2,1)S(1)} %copy-done.1), channel_id=1, source_target_pairs={{4,0},{8,4},{12,8},{5,1},{9,5},{13,9},{6,2},{10,6},{14,10},{7,3},{... | collective-permute-start | bytes 1572872 | tf_op jit(solution)/shard_map/ppermute | solution.py:294
  9.0 4.6 %collective-permute-start = (bf16[128,2048]{1,0:T(8,128)(2,1)S(1)}, bf16[128,2048]{1,0:T(8,128)(2,1)S(1)}, u32[]{:S(2)}, u32[]{:S(2)}) collective-permute-start(bf16[128,2048]{1,0:T(8,128)(2,1)S(1)} %copy-done.1), channel_id=1, source_target_pairs={{0,4},{4,8},{8,12},{1,5},{5,9},{9,13},{2,6},{6,10},{10,14},{3,7},{... | collective-permute-start | bytes 1572872 | tf_op jit(solution)/shard_map/ppermute | solution.py:293
  13.8 9.2 %collective-permute-done.2.refs_3_.refs_2_.refs_5_ = bf16[128,2048]{1,0:T(8,128)(2,1)S(1)} collective-permute-done((bf16[128,2048]{1,0:T(8,128)(2,1)S(1)}, bf16[128,2048]{1,0:T(8,128)(2,1)S(1)}, u32[]{:S(2)}, u32[]{:S(2)}) %collective-permute-start.2) | collective-permute-done | bytes 524320 | tf_op jit(solution)/shard_map/ppermute | solution.py:294
  23.0 1.3 %collective-permute-start.3 = (bf16[128,2048]{1,0:T(8,128)(2,1)S(1)}, bf16[128,2048]{1,0:T(8,128)(2,1)S(1)}, u32[]{:S(2)}, u32[]{:S(2)}) collective-permute-start(bf16[128,2048]{1,0:T(8,128)(2,1)S(1)} %collective-permute-done.2.refs_3_.refs_2_.refs_5_), channel_id=1, source_target_pairs={{4,0},{8,4},{5,1},{9,5},{6,2},{10,6},{7,3},{11,7},{20,16},{24,20},... | collective-permute-start | bytes 1572872 | tf_op jit(solution)/shard_map/ppermute | solution.py:294
  24.3 0.7 collective-permute-start.1
  25.1 1.0 collective-permute-done.6.refs_4_.refs_1_
  26.1 8.3 %partials.4 = (bf16[832,256]{1,0:T(8,128)(2,1)S(1)}, bf16[832,256]{1,0:T(8,128)(2,1)S(1)}, bf16[832,256]{1,0:T(8,128)(2,1)S(1)}, bf16[832,256]{1,0:T(8,128)(2,1)...) custom-call(s32[5]{0:T(128)S(1)} %fusion.meta_ref, bf16[6656,2048]{1,0:T(8,128)(2,1)} %refs_0_.11, ...), custom_call_target="tpu_custom_call" | custom-call | flops 1 | bytes 1 | tf_op jit(solution)/shard_map/partials/pallas_call | solution.py:60
  34.5 0.5 collective-permute-start.8
  35.2 2.1 %collective-permute-done.3.refs_4_.refs_7_.refs_6_.refs_9_ = bf16[128,2048]{1,0:T(8,128)(2,1)S(1)} collective-permute-done((bf16[128,2048]{1,0:T(8,128)(2,1)S(1)}, bf16[128,2048]{1,0:T(8,128)(2,1)S(1)}, u32[]{:S(2)}, u32[]{:S(2)}) %collective-permute-start.3) | collective-permute-done | bytes 524320 | tf_op jit(solution)/shard_map/ppermute | solution.py:294
  37.4 1.3 %collective-permute-start.5 = (bf16[128,2048]{1,0:T(8,128)(2,1)S(1)}, bf16[128,2048]{1,0:T(8,128)(2,1)S(1)}, u32[]{:S(2)}, u32[]{:S(2)}) collective-permute-start(bf16[128,2048]{1,0:T(8,128)(2,1)S(1)} %collective-permute-done.3.refs_4_.refs_7_.refs_6_.refs_9_), channel_id=1, source_target_pairs={{4,0},{5,1},{6,2},{7,3},{20,16},{21,17},{22,18},{23,19}} | collective-permute-start | bytes 1572872 | tf_op jit(solution)/shard_map/ppermute | solution.py:294
  38.7 0.7 collective-permute-start.4
  39.5 0.8 collective-permute-start.12
  40.4 0.8 collective-permute-done.10.refs_5_
  41.4 7.9 %partials.5 = (bf16[1664,256]{1,0:T(8,128)(2,1)S(1)}, f32[1664,256]{1,0:T(8,128)S(1)}, f32[8,128]{1,0:T(8,128)S(1)}) custom-call(s32[5]{0:T(128)S(1)} %fusion.meta_ref, bf16[6656,2048]{1,0:T(8,128)(2,1)} %refs_0_.11, bf16[2048,256]{1,0:T(8,128)(2,1)S(1)} %get-tuple-element.44.refs_1_, bf16[832,256]{1,0:T(8,128)(2,1)S(1)} %collective-permute-done.7.refs_2_, ...), custom_call_target="tpu_custom_call" | custom-call | flops 1 | bytes 1 | tf_op jit(solution)/shard_map/partials/pallas_call | solution.py:60
  49.3 3.1 %collective-permute-done.12.refs_10_.refs_3_ = bf16[448,512]{1,0:T(8,128)(2,1)S(1)} collective-permute-done((bf16[448,512]{1,0:T(8,128)(2,1)S(1)}, bf16[448,512]{1,0:T(8,128)(2,1)S(1)}, u32[]{:S(2)}, u32[]{:S(2)}) %collective-permute-start.12) | collective-permute-done | bytes 458784 | tf_op jit(solution)/shard_map/ppermute | solution.py:325
  52.4 0.9 collective-permute-done.5.refs_8_.refs_10_
  53.3 7.7 %partials.6 = (bf16[832,256]{1,0:T(8,128)(2,1)S(1)}, bf16[832,256]{1,0:T(8,128)(2,1)S(1)}, bf16[832,256]{1,0:T(8,128)(2,1)S(1)}, bf16[832,256]{1,0:T(8,128)(2,1)...) custom-call(s32[5]{0:T(128)S(1)} %fusion.meta_ref, bf16[6656,2048]{1,0:T(8,128)(2,1)} %refs_0_.11, ...), custom_call_target="tpu_custom_call" | custom-call | flops 1 | bytes 1 | tf_op jit(solution)/shard_map/partials/pallas_call | solution.py:60
  61.1 0.5 collective-permute-start.14
  62.2 0.5 collective-permute-start.22
  63.0 0.5 collective-permute-done.14.refs_3_
  64.9 1.0 token_rows.1
  65.8 7.9 %partials.7 = (bf16[832,256]{1,0:T(8,128)(2,1)S(1)}, bf16[832,256]{1,0:T(8,128)(2,1)S(1)}, f32[832,256]{1,0:T(8,128)S(1)}, f32[832,256]{1,0:T(8,128)S(1)}, f32[8,128]{1,0:T(8,128)S(1)}) custom-call(s32[5]{0:T(128)S(1)} %fusion.meta_ref, bf16[6656,2048]{1,0:T(8,128)(2,1)} %refs_0_.11, bf16[2048,256]{1,0:T(8,128)(2,1)S(1)} %get-tuple-element.52.refs_1_, ...), custom_call_target="tpu_custom_call" | custom-call | flops 1 | bytes 1 | tf_op jit(solution)/shard_map/partials/pallas_call | solution.py:60
  73.8 0.6 collective-permute-start.17
  74.4 11.3 %weight_grad.2 = (bf16[6656,2048]{1,0:T(8,128)(2,1)}, f32[8,128]{1,0:T(8,128)S(1)}) custom-call(s32[5]{0:T(128)S(1)} %fusion.meta_ref, bf16[512,2048]{1,0:T(8,128)(2,1)S(1)} %get-tuple-element.63.refs_0_, bf16[768,512]{1,0:T(8,128)(2,1)S(1)} %get-tuple-element.43.refs_1_, bf16[448,512]{1,0:T(8,128)(2,1)} %get-tuple-element.49.refs_2_, ...), custom_call_target="tpu_custom_call" | custom-call | flops 1 | bytes 1 | tf_op jit(solution)/shard_map/weight_grad/pallas_call | solution.py:60
  85.7 1.5 %collective-permute-start.18 = (bf16[832,256]{1,0:T(8,128)(2,1)S(1)}, bf16[832,256]{1,0:T(8,128)(2,1)S(1)}, u32[]{:S(2)}, u32[]{:S(2)}) collective-permute-start(bf16[832,256]{1,0:T(8,128)(2,1)S(1)} %get-tuple-element.62), channel_id=1, source_target_pairs={{0,2},{1,3},{2,0},{3,1},{4,6},{5,7},{6,4},{7,5},{8,10},{9,11},{10,... | collective-permute-start | bytes 1277960 | tf_op jit(solution)/shard_map/ppermute | solution.py:354
  87.2 4.0 %gate_grad.3 = (bf16[2,1664,512]{2,1,0:T(8,128)(2,1)}, f32[8,128]{1,0:T(8,128)S(1)}) custom-call(s32[5]{0:T(128)S(1)} %fusion.meta_ref, bf16[2,1664,512]{2,1,0:T(8,128)(2,1)S(1)} %copy-done, f32[1664,256]{1,0:T(8,128)S(1)} %get-tuple-element.64.refs_1_, bf16[1664,256]{1,0:T(8,128)(2,1)S(1)} %collective-permute-done.22.refs_2_, ...), custom_call_target="tpu_custom_call" | custom-call | flops 1 | bytes 1 | tf_op jit(solution)/shard_map/gate_grad/pallas_call | solution.py:60
  91.2 11.3 %weight_grad.3 = (bf16[6656,2048]{1,0:T(8,128)(2,1)}, f32[8,128]{1,0:T(8,128)S(1)}) custom-call(s32[5]{0:T(128)S(1)} %fusion.meta_ref, bf16[512,2048]{1,0:T(8,128)(2,1)S(1)} %get-tuple-element.63.refs_0_, bf16[768,512]{1,0:T(8,128)(2,1)S(1)} %collective-permute-done.6.refs_4_.refs_1_, ...), custom_call_target="tpu_custom_call", output_to_operand_aliasing={{0}: (9, {})} | custom-call | flops 99999997952 | bytes 1 | tf_op jit(solution)/shard_map/weight_grad/pallas_call | solution.py:60
  102.5 3.5 %gate_grad.4 = (bf16[2,1664,512]{2,1,0:T(8,128)(2,1)}, f32[8,128]{1,0:T(8,128)S(1)}) custom-call(s32[5]{0:T(128)S(1)} %fusion.meta_ref, bf16[2,1664,512]{2,1,0:T(8,128)(2,1)S(1)} %copy-done, f32[832,256]{1,0:T(8,128)S(1)} %get-tuple-element.61.refs_1_, bf16[832,256]{1,0:T(8,128)(2,1)S(1)} %collective-permute-done.18.refs_2_, ...), custom_call_target="tpu_custom_call", output_to_operand_aliasing={{0}: (5, {})} | custom-call | flops 1 | bytes 1 | tf_op jit(solution)/shard_map/gate_grad/pallas_call | solution.py:60
  106.0 3.5 %gate_grad.5 = (bf16[2,1664,512]{2,1,0:T(8,128)(2,1)}, f32[8,128]{1,0:T(8,128)}) custom-call(s32[5]{0:T(128)S(1)} %fusion.meta_ref, bf16[2,1664,512]{2,1,0:T(8,128)(2,1)S(1)} %copy-done, f32[832,256]{1,0:T(8,128)S(1)} %get-tuple-element.59.refs_1_, bf16[832,256]{1,0:T(8,128)(2,1)S(1)} %collective-permute-done.17.refs_2_, ...), custom_call_target="tpu_custom_call", output_to_operand_aliasing={{0}: (5, {})} | custom-call | flops 1 | bytes 1 | tf_op jit(solution)/shard_map/gate_grad/pallas_call | solution.py:60
  (50 shorter events, 3.2 us)
Async XLA Ops:
  0.6 24.4 %copy-start.4 = (s32[5]{0:T(128)S(1)}, s32[5]{0:T(128)}, u32[]{:S(2)}) copy-start(s32[5]{0:T(128)} %constant.27.clone) | copy-start | bytes 64
  0.6 24.4 %copy-start.5 = (s32[5]{0:T(128)S(1)}, s32[5]{0:T(128)}, u32[]{:S(2)}) copy-start(s32[5]{0:T(128)} %constant.26.clone) | copy-start | bytes 64
  0.7 24.4 %copy-start.6 = (s32[5]{0:T(128)S(1)}, s32[5]{0:T(128)}, u32[]{:S(2)}) copy-start(s32[5]{0:T(128)} %constant.25.clone) | copy-start | bytes 64
  0.7 24.4 %copy-start.7 = (s32[5]{0:T(128)S(1)}, s32[5]{0:T(128)}, u32[]{:S(2)}) copy-start(s32[5]{0:T(128)} %constant.24.clone) | copy-start | bytes 64
  0.7 24.4 %copy-start.8 = (s32[5]{0:T(128)S(1)}, s32[5]{0:T(128)}, u32[]{:S(2)}) copy-start(s32[5]{0:T(128)} %constant.23.clone) | copy-start | bytes 64
  4.8 21.3 %collective-permute-start.6 = (bf16[768,512]{1,0:T(8,128)(2,1)S(1)}, bf16[768,512]{1,0:T(8,128)(2,1)S(1)}, u32[]{:S(2)}, u32[]{:S(2)}) collective-permute-start(bf16[768,512]{1,0:T(8,128)(2,1)S(1)} %get-tuple-element.43.refs_1_), channel_id=1, source_target_pairs={{0,2},{1,3},{2,0},{3,1},{4,6},{5,7},{6,4},{7,5},{8,10},{9,11},{10,... | collective-permute-start | bytes 2359304 | tf_op jit(solution)/shard_map/ppermute | solution.py:325
  7.8 15.3 %collective-permute-start.2 = (bf16[128,2048]{1,0:T(8,128)(2,1)S(1)}, bf16[128,2048]{1,0:T(8,128)(2,1)S(1)}, u32[]{:S(2)}, u32[]{:S(2)}) collective-permute-start(bf16[128,2048]{1,0:T(8,128)(2,1)S(1)} %copy-done.1), channel_id=1, source_target_pairs={{4,0},{8,4},{12,8},{5,1},{9,5},{13,9},{6,2},{10,6},{14,10},{7,3},{... | collective-permute-start | bytes 1572872 | tf_op jit(solution)/shard_map/ppermute | solution.py:294
  9.0 15.3 %collective-permute-start = (bf16[128,2048]{1,0:T(8,128)(2,1)S(1)}, bf16[128,2048]{1,0:T(8,128)(2,1)S(1)}, u32[]{:S(2)}, u32[]{:S(2)}) collective-permute-start(bf16[128,2048]{1,0:T(8,128)(2,1)S(1)} %copy-done.1), channel_id=1, source_target_pairs={{0,4},{4,8},{8,12},{1,5},{5,9},{9,13},{2,6},{6,10},{10,14},{3,7},{... | collective-permute-start | bytes 1572872 | tf_op jit(solution)/shard_map/ppermute | solution.py:293
  13.6 21.6 %collective-permute-start.11 = (bf16[448,512]{1,0:T(8,128)(2,1)}, bf16[448,512]{1,0:T(8,128)(2,1)}, u32[]{:S(2)}, u32[]{:S(2)}) collective-permute-start(bf16[448,512]{1,0:T(8,128)(2,1)} %get-tuple-element.49.refs_2_), channel_id=1, source_target_pairs={{0,2},{1,3},{2,0},{3,1},{4,6},{5,7},{6,4},{7,5},{8,10},{9,11},{10,... | collective-permute-start | bytes 1376264 | tf_op jit(solution)/shard_map/ppermute | solution.py:325
  23.0 14.4 %collective-permute-start.3 = (bf16[128,2048]{1,0:T(8,128)(2,1)S(1)}, bf16[128,2048]{1,0:T(8,128)(2,1)S(1)}, u32[]{:S(2)}, u32[]{:S(2)}) collective-permute-start(bf16[128,2048]{1,0:T(8,128)(2,1)S(1)} %collective-permute-done.2.refs_3_.refs_2_.refs_5_), channel_id=1, source_target_pairs={{4,0},{8,4},{5,1},{9,5},{6,2},{10,6},{7,3},{11,7},{20,16},{24,20},... | collective-permute-start | bytes 1572872 | tf_op jit(solution)/shard_map/ppermute | solution.py:294
  24.3 14.3 %collective-permute-start.1 = (bf16[128,2048]{1,0:T(8,128)(2,1)S(1)}, bf16[128,2048]{1,0:T(8,128)(2,1)S(1)}, u32[]{:S(2)}, u32[]{:S(2)}) collective-permute-start(bf16[128,2048]{1,0:T(8,128)(2,1)S(1)} %collective-permute-done.refs_2_.refs_1_.refs_4_), channel_id=1, source_target_pairs={{4,8},{8,12},{5,9},{9,13},{6,10},{10,14},{7,11},{11,15},{20,24},{2... | collective-permute-start | bytes 1572872 | tf_op jit(solution)/shard_map/ppermute | solution.py:293
  25.1 14.4 %copy-start.3 = (bf16[448,512]{1,0:T(8,128)(2,1)S(1)}, bf16[448,512]{1,0:T(8,128)(2,1)}, u32[]{:S(2)}) copy-start(bf16[448,512]{1,0:T(8,128)(2,1)} %copy-done.2) | copy-start | bytes 1376260
  34.4 5.0 %collective-permute-start.7 = (bf16[832,256]{1,0:T(8,128)(2,1)S(1)}, bf16[832,256]{1,0:T(8,128)(2,1)S(1)}, u32[]{:S(2)}, u32[]{:S(2)}) collective-permute-start(bf16[832,256]{1,0:T(8,128)(2,1)S(1)} %get-tuple-element.45), channel_id=1, source_target_pairs={{0,1},{1,0},{2,3},{3,2},{4,5},{5,4},{6,7},{7,6},{8,9},{9,8},{10,11... | collective-permute-start | bytes 1277960 | tf_op jit(solution)/shard_map/ppermute | solution.py:340
  34.5 5.0 %collective-permute-start.8 = (bf16[832,256]{1,0:T(8,128)(2,1)S(1)}, bf16[832,256]{1,0:T(8,128)(2,1)S(1)}, u32[]{:S(2)}, u32[]{:S(2)}) collective-permute-start(bf16[832,256]{1,0:T(8,128)(2,1)S(1)} %get-tuple-element.46), channel_id=1, source_target_pairs={{0,1},{1,0},{2,3},{3,2},{4,5},{5,4},{6,7},{7,6},{8,9},{9,8},{10,11... | collective-permute-start | bytes 1277960 | tf_op jit(solution)/shard_map/ppermute | solution.py:340
  35.2 5.0 %collective-permute-start.9 = (bf16[832,256]{1,0:T(8,128)(2,1)S(1)}, bf16[832,256]{1,0:T(8,128)(2,1)S(1)}, u32[]{:S(2)}, u32[]{:S(2)}) collective-permute-start(bf16[832,256]{1,0:T(8,128)(2,1)S(1)} %get-tuple-element.47), channel_id=1, source_target_pairs={{0,1},{1,0},{2,3},{3,2},{4,5},{5,4},{6,7},{7,6},{8,9},{9,8},{10,11... | collective-permute-start | bytes 1277960 | tf_op jit(solution)/shard_map/ppermute | solution.py:340
  37.4 16.0 %collective-permute-start.5 = (bf16[128,2048]{1,0:T(8,128)(2,1)S(1)}, bf16[128,2048]{1,0:T(8,128)(2,1)S(1)}, u32[]{:S(2)}, u32[]{:S(2)}) collective-permute-start(bf16[128,2048]{1,0:T(8,128)(2,1)S(1)} %collective-permute-done.3.refs_4_.refs_7_.refs_6_.refs_9_), channel_id=1, source_target_pairs={{4,0},{5,1},{6,2},{7,3},{20,16},{21,17},{22,18},{23,19}} | collective-permute-start | bytes 1572872 | tf_op jit(solution)/shard_map/ppermute | solution.py:294
  38.7 14.7 %collective-permute-start.4 = (bf16[128,2048]{1,0:T(8,128)(2,1)S(1)}, bf16[128,2048]{1,0:T(8,128)(2,1)S(1)}, u32[]{:S(2)}, u32[]{:S(2)}) collective-permute-start(bf16[128,2048]{1,0:T(8,128)(2,1)S(1)} %collective-permute-done.1.refs_1_.refs_6_.refs_3_.refs_8_), channel_id=1, source_target_pairs={{8,12},{9,13},{10,14},{11,15},{24,28},{25,29},{26,30},{27,31}} | collective-permute-start | bytes 1572872 | tf_op jit(solution)/shard_map/ppermute | solution.py:293
  39.4 1.8 %collective-permute-start.10 = (bf16[832,256]{1,0:T(8,128)(2,1)S(1)}, bf16[832,256]{1,0:T(8,128)(2,1)S(1)}, u32[]{:S(2)}, u32[]{:S(2)}) collective-permute-start(bf16[832,256]{1,0:T(8,128)(2,1)S(1)} %get-tuple-element.48), channel_id=1, source_target_pairs={{0,1},{1,0},{2,3},{3,2},{4,5},{5,4},{6,7},{7,6},{8,9},{9,8},{10,11... | collective-permute-start | bytes 1277960 | tf_op jit(solution)/shard_map/ppermute | solution.py:340
  39.5 12.9 %collective-permute-start.12 = (bf16[448,512]{1,0:T(8,128)(2,1)S(1)}, bf16[448,512]{1,0:T(8,128)(2,1)S(1)}, u32[]{:S(2)}, u32[]{:S(2)}) collective-permute-start(bf16[448,512]{1,0:T(8,128)(2,1)S(1)} %copy-done.3), channel_id=1, source_target_pairs={{0,2},{1,3},{2,0},{3,1},{4,6},{5,7},{6,4},{7,5},{8,10},{9,11},{10,... | collective-permute-start | bytes 1376264 | tf_op jit(solution)/shard_map/ppermute | solution.py:325
  40.2 21.5 %collective-permute-start.24 = (bf16[448,512]{1,0:T(8,128)(2,1)}, bf16[448,512]{1,0:T(8,128)(2,1)S(1)}, u32[]{:S(2)}, u32[]{:S(2)}) collective-permute-start(bf16[448,512]{1,0:T(8,128)(2,1)} %get-tuple-element.49.refs_2_), channel_id=1, source_target_pairs={{0,1},{1,0},{2,3},{3,2},{4,5},{5,4},{6,7},{7,6},{8,9},{9,8},{10,11... | collective-permute-start | bytes 1376264 | tf_op jit(solution)/shard_map/ppermute | solution.py:334
  41.2 20.9 %collective-permute-start.25 = (bf16[448,512]{1,0:T(8,128)(2,1)S(1)}, bf16[448,512]{1,0:T(8,128)(2,1)S(1)}, u32[]{:S(2)}, u32[]{:S(2)}) collective-permute-start(bf16[448,512]{1,0:T(8,128)(2,1)S(1)} %copy-done.3), channel_id=1, source_target_pairs={{0,1},{1,0},{2,3},{3,2},{4,5},{5,4},{6,7},{7,6},{8,9},{9,8},{10,11... | collective-permute-start | bytes 1376264 | tf_op jit(solution)/shard_map/ppermute | solution.py:334
  61.1 1.8 %collective-permute-start.13 = (bf16[832,256]{1,0:T(8,128)(2,1)S(1)}, bf16[832,256]{1,0:T(8,128)(2,1)S(1)}, u32[]{:S(2)}, u32[]{:S(2)}) collective-permute-start(bf16[832,256]{1,0:T(8,128)(2,1)S(1)} %get-tuple-element.53), channel_id=1, source_target_pairs={{0,1},{1,0},{2,3},{3,2},{4,5},{5,4},{6,7},{7,6},{8,9},{9,8},{10,11... | collective-permute-start | bytes 1277960 | tf_op jit(solution)/shard_map/ppermute | solution.py:349
  61.1 2.4 %collective-permute-start.14 = (bf16[832,256]{1,0:T(8,128)(2,1)S(1)}, bf16[832,256]{1,0:T(8,128)(2,1)S(1)}, u32[]{:S(2)}, u32[]{:S(2)}) collective-permute-start(bf16[832,256]{1,0:T(8,128)(2,1)S(1)} %get-tuple-element.54), channel_id=1, source_target_pairs={{0,1},{1,0},{2,3},{3,2},{4,5},{5,4},{6,7},{7,6},{8,9},{9,8},{10,11... | collective-permute-start | bytes 1277960 | tf_op jit(solution)/shard_map/ppermute | solution.py:349
  61.6 2.5 %collective-permute-start.15 = (bf16[832,256]{1,0:T(8,128)(2,1)S(1)}, bf16[832,256]{1,0:T(8,128)(2,1)S(1)}, u32[]{:S(2)}, u32[]{:S(2)}) collective-permute-start(bf16[832,256]{1,0:T(8,128)(2,1)S(1)} %get-tuple-element.55), channel_id=1, source_target_pairs={{0,1},{1,0},{2,3},{3,2},{4,5},{5,4},{6,7},{7,6},{8,9},{9,8},{10,11... | collective-permute-start | bytes 1277960 | tf_op jit(solution)/shard_map/ppermute | solution.py:349
  61.7 3.0 %collective-permute-start.16 = (bf16[832,256]{1,0:T(8,128)(2,1)S(1)}, bf16[832,256]{1,0:T(8,128)(2,1)S(1)}, u32[]{:S(2)}, u32[]{:S(2)}) collective-permute-start(bf16[832,256]{1,0:T(8,128)(2,1)S(1)} %get-tuple-element.56), channel_id=1, source_target_pairs={{0,1},{1,0},{2,3},{3,2},{4,5},{5,4},{6,7},{7,6},{8,9},{9,8},{10,11... | collective-permute-start | bytes 1277960 | tf_op jit(solution)/shard_map/ppermute | solution.py:349
  62.2 23.5 %collective-permute-start.22 = (bf16[1664,256]{1,0:T(8,128)(2,1)S(1)}, bf16[1664,256]{1,0:T(8,128)(2,1)S(1)}, u32[]{:S(2)}, u32[]{:S(2)}) collective-permute-start(bf16[1664,256]{1,0:T(8,128)(2,1)S(1)} %get-tuple-element.65), channel_id=1, source_target_pairs={{0,2},{1,3},{2,0},{3,1},{4,6},{5,7},{6,4},{7,5},{8,10},{9,11},{10,... | collective-permute-start | bytes 2555912 | tf_op jit(solution)/shard_map/ppermute | solution.py:344
  62.9 10.9 %collective-permute-start.23 = (bf16[768,512]{1,0:T(8,128)(2,1)S(1)}, bf16[768,512]{1,0:T(8,128)(2,1)S(1)}, u32[]{:S(2)}, u32[]{:S(2)}) collective-permute-start(bf16[768,512]{1,0:T(8,128)(2,1)S(1)} %get-tuple-element.43.refs_1_), channel_id=1, source_target_pairs={{0,1},{1,0},{2,3},{3,2},{4,5},{5,4},{6,7},{7,6},{8,9},{9,8},{10,11... | collective-permute-start | bytes 2359304 | tf_op jit(solution)/shard_map/ppermute | solution.py:334
  63.5 27.7 %collective-permute-start.19 = (bf16[768,512]{1,0:T(8,128)(2,1)S(1)}, bf16[768,512]{1,0:T(8,128)(2,1)S(1)}, u32[]{:S(2)}, u32[]{:S(2)}) collective-permute-start(bf16[768,512]{1,0:T(8,128)(2,1)S(1)} %collective-permute-done.6.refs_4_.refs_1_), channel_id=1, source_target_pairs={{0,1},{1,0},{2,3},{3,2},{4,5},{5,4},{6,7},{7,6},{8,9},{9,8},{10,11... | collective-permute-start | bytes 2359304 | tf_op jit(solution)/shard_map/ppermute | solution.py:355
  64.1 27.0 %collective-permute-start.20 = (bf16[448,512]{1,0:T(8,128)(2,1)}, bf16[448,512]{1,0:T(8,128)(2,1)S(1)}, u32[]{:S(2)}, u32[]{:S(2)}) collective-permute-start(bf16[448,512]{1,0:T(8,128)(2,1)} %collective-permute-done.11.refs_6_.refs_2_), channel_id=1, source_target_pairs={{0,1},{1,0},{2,3},{3,2},{4,5},{5,4},{6,7},{7,6},{8,9},{9,8},{10,11... | collective-permute-start | bytes 1376264 | tf_op jit(solution)/shard_map/ppermute | solution.py:355
  64.7 26.4 %collective-permute-start.21 = (bf16[448,512]{1,0:T(8,128)(2,1)S(1)}, bf16[448,512]{1,0:T(8,128)(2,1)S(1)}, u32[]{:S(2)}, u32[]{:S(2)}) collective-permute-start(bf16[448,512]{1,0:T(8,128)(2,1)S(1)} %collective-permute-done.12.refs_10_.refs_3_), channel_id=1, source_target_pairs={{0,1},{1,0},{2,3},{3,2},{4,5},{5,4},{6,7},{7,6},{8,9},{9,8},{10,11... | collective-permute-start | bytes 1376264 | tf_op jit(solution)/shard_map/ppermute | solution.py:355
  73.8 32.2 %collective-permute-start.17 = (bf16[832,256]{1,0:T(8,128)(2,1)S(1)}, bf16[832,256]{1,0:T(8,128)(2,1)S(1)}, u32[]{:S(2)}, u32[]{:S(2)}) collective-permute-start(bf16[832,256]{1,0:T(8,128)(2,1)S(1)} %get-tuple-element.60), channel_id=1, source_target_pairs={{0,2},{1,3},{2,0},{3,1},{4,6},{5,7},{6,4},{7,5},{8,10},{9,11},{10,... | collective-permute-start | bytes 1277960 | tf_op jit(solution)/shard_map/ppermute | solution.py:354
  85.7 16.8 %collective-permute-start.18 = (bf16[832,256]{1,0:T(8,128)(2,1)S(1)}, bf16[832,256]{1,0:T(8,128)(2,1)S(1)}, u32[]{:S(2)}, u32[]{:S(2)}) collective-permute-start(bf16[832,256]{1,0:T(8,128)(2,1)S(1)} %get-tuple-element.62), channel_id=1, source_target_pairs={{0,2},{1,3},{2,0},{3,1},{4,6},{5,7},{6,4},{7,5},{8,10},{9,11},{10,... | collective-permute-start | bytes 1277960 | tf_op jit(solution)/shard_map/ppermute | solution.py:354
  (3 other events, 21.3 us)

commit v2 on v1

v2 whole, which is shorter than its diff:
```python
import functools
import math

import jax
import jax.numpy as jnp
import numpy as np
from jax import lax
from jax.experimental import pallas as pl
from jax.experimental.pallas import tpu as pltpu
from jax.sharding import PartitionSpec as P

LANES = 128
LONG, SHORT, MIDDLE, BRIEF = 20 * 10**9, 4700 * 10**6, 4190 * 10**6, 790 * 10**6
MIB = 1024 * 1024


def in_vmem(array):
    return pltpu.with_memory_space_constraint(array, pltpu.VMEM), pl.BlockSpec(memory_space=pltpu.VMEM)


def in_hbm(array):
    return pltpu.with_memory_space_constraint(array, pltpu.HBM), pl.BlockSpec(memory_space=pltpu.HBM)


def anywhere(array):
    return array, pl.BlockSpec(memory_space=pl.ANY)


def sigmoid(x):
    return 0.5 * jnp.tanh(0.5 * x) + 0.5


def hidden_of(acts):
    gate = acts[0].astype(jnp.float32)
    upper = acts[1].astype(jnp.float32)
    return (gate * sigmoid(gate) * upper).astype(jnp.bfloat16)


def tile_of(rows, most):
    return max(t for t in range(16, most + 1, 16) if rows % t == 0)


TOKEN = (pltpu.VMEM((8, LANES), jnp.float32), pl.BlockSpec(memory_space=pltpu.VMEM))


def call(kernel, name, meta, grid, ins, outs, scratch=(), alias=None, after=(), weight=1, vmem=16):
    ins = list(ins) + [anywhere(a) for a in after]
    read = len(ins) - len(after)
    aliases = {}
    if alias is not None:
        aliases = {1 + len(ins): len(outs) - 1}
        ins.append(in_hbm(alias))
    outs = list(outs) + [TOKEN]

    def body(meta_ref, *refs):
        refs = list(refs)
        token = refs.pop(len(ins) + len(outs) - 1)
        token[...] = jnp.zeros_like(token)
        kernel(meta_ref, *refs[:read], *refs[len(ins) :])

    return pl.pallas_call(
        body,
        grid_spec=pltpu.PrefetchScalarGridSpec(
            num_scalar_prefetch=1, grid=grid, in_specs=[s for _, s in ins], out_specs=[s for _, s in outs], scratch_shapes=list(scratch)
        ),
        out_shape=[s for s, _ in outs],
        input_output_aliases=aliases,
        compiler_params=pltpu.CompilerParams(vmem_limit_bytes=vmem * MIB),
        cost_estimate=pl.CostEstimate(flops=weight, bytes_accessed=1, transcendentals=0),
        name=name,
    )(meta, *[a for a, _ in ins])


def hidden_rows(acts, start, pieces, after=()):
    _, _, tokens = acts.shape
    rows = sum(pieces)
    tile = math.gcd(*pieces)
    starts = [sum(pieces[:p]) for p in range(len(pieces))]

    def kernel(acts_ref, *refs):
        refs = refs[len(after) :]
        out_refs, (buf, sems) = refs[: len(pieces)], refs[len(pieces) :]

        def load(p):
            there, here = pl.ds(start + starts[p], pieces[p]), pl.ds(starts[p], pieces[p])
            return pltpu.make_async_copy(acts_ref.at[:, there, :], buf.at[:, here, :], sems.at[p])

        for p in range(len(pieces)):
            load(p).start()
        for p, ref in enumerate(out_refs):
            load(p).wait()
            for at in range(0, pieces[p], tile // 4):
                ref[pl.ds(at, tile // 4), :] = hidden_of(buf[:, pl.ds(starts[p] + at, tile // 4), :])

    array, spec = in_hbm(acts)
    return pl.pallas_call(
        kernel,
        in_specs=[spec, *[anywhere(a)[1] for a in after]],
        out_specs=[pl.BlockSpec(memory_space=pltpu.VMEM)] * len(pieces),
        out_shape=[pltpu.VMEM((n, tokens), acts.dtype) for n in pieces],
        scratch_shapes=[pltpu.VMEM((2, rows, tokens), acts.dtype), pltpu.SemaphoreType.DMA((len(pieces),))],
        compiler_params=pltpu.CompilerParams(vmem_limit_bytes=8 * MIB),
        cost_estimate=pl.CostEstimate(flops=1, bytes_accessed=1, transcendentals=0),
        name="hidden",
    )(array, *after)


class Slot:
    def __init__(self, number, blocks, places):
        self.number, self.blocks, self.places = number, blocks, places

    def start(self, meta_ref, refs, target, sem):
        for ref, places in zip(refs, self.places, strict=True):

            @pl.when(functools.reduce(jnp.logical_or, [meta_ref[1] == z for z in places]))
            def _():
                pltpu.make_async_copy(ref, target, sem).start()

    def wait(self, refs, target, sem):
        pltpu.make_async_copy(refs[0], target, sem).wait()


def fetch(slots, meta_ref, refs, targets, sems):
    waits = []
    for n, slot in enumerate(slots):
        mine, refs = refs[: len(slot.blocks)], refs[len(slot.blocks) :]
        slot.start(meta_ref, mine, targets[n], sems.at[n])
        waits.append(functools.partial(slot.wait, mine, targets[n], sems.at[n]))
    return lambda: [wait() for wait in waits]


def blocks_of(slots):
    return [anywhere(block) for slot in slots for block in slot.blocks]


def partials(meta, masks, weight, rows, tokens, dtypes, splits, slots=None, turned=None, adds=None, keep=True, after=(), weight_of=1):
    feats = weight.shape[1]
    tile = rows // (4 if keep else 2)
    steps = rows // tile
    total = len(masks) * steps
    depth = 3
    blocks = blocks_of(slots) if slots else [in_vmem(turned)]
    each = tokens // len(slots) if slots else 0
    extra = [a for group in adds or [] for a in group]
    per = len(extra) // len(masks)

    def kernel(meta_ref, w_ref, *refs):
        block_refs, refs = refs[: len(blocks)], refs[len(blocks) :]
        add_refs, refs = refs[: len(extra)], refs[len(extra) :]
        out_refs, refs = refs[: len(masks) * splits], list(refs[len(masks) * splits :])
        turned_ref = refs.pop(0) if slots else block_refs[0]
        kept_ref = refs.pop(0) if keep else w_ref
        k = pl.program_id(0)

        def copy(step):
            block = meta_ref[0] ^ masks[step // steps]
            at = pl.multiple_of(block * rows + step % steps * tile, tile)
            return pltpu.make_async_copy(w_ref.at[pl.ds(at, tile), :], kept_ref.at[pl.ds(step * tile, tile), :], refs[0].at[step])

        @pl.when(k == 0)
        def _():
            if slots:
                rows_buf, sems = refs[-2:]
                targets = [rows_buf.at[pl.ds(n * each, each), :] for n in range(len(slots))]
                wait = fetch(slots, meta_ref, block_refs, targets, sems)
            if keep:
                for step in range(depth - 1):
                    copy(step).start()
            if slots:
                wait()
                turned_ref[...] = rows_buf[...].T

        if keep:
            for step in range(total):

                @pl.when(k == step)
                def _():
                    if step + depth - 1 < total:
                        copy(step + depth - 1).start()
                    copy(step).wait()

        w = kept_ref[pl.ds(pl.multiple_of(k * tile, tile), tile), :]
        out = jnp.dot(w, turned_ref[...], preferred_element_type=jnp.float32)
        for step in range(total):
            j, i = step // steps, step % steps

            @pl.when(k == step)
            def _():
                value = out
                if extra:
                    add_ref, at = add_refs[j * per + i * per // steps], i % (steps // per) * tile
                    value = value + add_ref[at : at + tile, :].astype(jnp.float32)
                at = i % (steps // splits) * tile
                out_refs[j * splits + i * splits // steps][at : at + tile, :] = value.astype(dtypes[j])

    in_place = pl.BlockSpec(memory_space=pltpu.VMEM)
    ins = [in_hbm(weight) if keep else in_vmem(weight), *blocks, *[in_vmem(piece) for piece in extra]]
    outs = [(pltpu.VMEM((rows // splits, tokens), dtype), in_place) for dtype in dtypes for _ in range(splits)]
    scratch = []
    if slots:
        outs.append((pltpu.VMEM((feats, tokens), weight.dtype), in_place))
        scratch = [pltpu.VMEM((tokens, feats), weight.dtype), pltpu.SemaphoreType.DMA((len(slots),))]
    if keep:
        outs.append((pltpu.VMEM((total * tile, feats), weight.dtype), in_place))
        scratch = [pltpu.SemaphoreType.DMA((total,)), *scratch]
    return call(kernel, "partials", meta, (total,), ins, outs, scratch, after=after, weight=weight_of, vmem=8)


def turned_slots(meta, slots, each, feats, after=(), weight=1):
    blocks = blocks_of(slots)
    tokens = len(slots) * each

    def kernel(meta_ref, *refs):
        block_refs, (out_ref, buf, sems) = refs[: len(blocks)], refs[len(blocks) :]
        fetch(slots, meta_ref, block_refs, [buf.at[pl.ds(n * each, each), :] for n in range(len(slots))], sems)()
        out_ref[...] = buf[...].T

    outs = [(pltpu.VMEM((feats, tokens), jnp.bfloat16), pl.BlockSpec(memory_space=pltpu.VMEM))]
    scratch = [pltpu.VMEM((tokens, feats), jnp.bfloat16), pltpu.SemaphoreType.DMA((len(slots),))]
    return call(kernel, "turned", meta, (1,), blocks, outs, scratch, after=after, weight=weight, vmem=6)


def all_slots(meta, slots, each, feats, after=()):
    blocks = blocks_of(slots)

    def kernel(meta_ref, *refs):
        block_refs, (out_ref, sems) = refs[: len(blocks)], refs[len(blocks) :]
        starts = [pl.multiple_of(meta_ref[1 + slot.number] * each, each) for slot in slots]
        fetch(slots, meta_ref, block_refs, [out_ref.at[pl.ds(at, each), :] for at in starts], sems)()

    shape = pltpu.VMEM((len(slots) * each, feats), jnp.bfloat16)
    outs = [(shape, pl.BlockSpec(memory_space=pltpu.VMEM))]
    return call(kernel, "token_rows", meta, (1,), blocks, outs, [pltpu.SemaphoreType.DMA((len(slots),))], after=after, vmem=4)


def weight_grad(meta, masks, hiddens, cots, out, total_rows, after=(), weight=1):
    tokens, feats = cots.shape
    steps = len(hiddens[0])
    tile = hiddens[0][0].shape[0]
    flat = [p for pieces in hiddens for p in pieces]

    def kernel(meta_ref, cot_ref, *refs):
        piece_refs, (out_ref, buf, sems) = refs[: len(flat)], refs[len(flat) :]
        k = pl.program_id(0)

        def copy(step):
            return pltpu.make_async_copy(piece_refs[step], buf.at[step % 2], sems.at[step % 2])

        @pl.when(k == 0)
        def _():
            copy(0).start()

        for step in range(len(flat)):

            @pl.when(k == step)
            def _():
                copy(step).wait()
                if step + 1 < len(flat):
                    copy(step + 1).start()

        out_ref[...] = jnp.dot(buf[lax.rem(k, 2)], cot_ref[...], preferred_element_type=jnp.float32).astype(out_ref.dtype)

    def place(k, m):
        block = m[0] ^ masks[0]
        for j in range(1, len(masks)):
            block = jnp.where(k // steps == j, m[0] ^ masks[j], block)
        return block * steps + k % steps, 0

    return call(
        kernel, "weight_grad", meta, (len(flat),),
        [in_vmem(cots), *[anywhere(p) for p in flat]],
        [(jax.ShapeDtypeStruct((total_rows, feats), cots.dtype), pl.BlockSpec((tile, feats), place))],
        [pltpu.VMEM((2, tile, tokens), cots.dtype), pltpu.SemaphoreType.DMA((2,))],
        alias=out, after=after, weight=weight, vmem=20,
    )


def gate_grad(meta, acts, early, weight, turned, back, far, after=()):
    _, rows, tokens = acts.shape
    feats, half = turned.shape
    tile = rows // 4
    per = len(back)

    def kernel(meta_ref, acts_ref, mine_ref, theirs_ref, w_ref, turned_ref, *refs):
        back_refs, far_ref, out_ref = refs[:per], refs[per], refs[per + 1]
        i = pl.program_id(0)
        here = pl.ds(pl.multiple_of(i * tile, tile), tile)
        late = jnp.dot(w_ref[here, :], turned_ref[...], preferred_element_type=jnp.float32)
        late = late + far_ref[here, :].astype(jnp.float32)
        there = pl.ds(pl.multiple_of(i % (4 // per) * tile, tile), tile)
        added = back_refs[0][there, :]
        for p in range(1, per):
            added = jnp.where(i * per // 4 == p, back_refs[p][there, :], added)
        late = late + added.astype(jnp.float32)
        for slot in range(tokens // LANES):
            lanes = slice(slot * LANES % half, slot * LANES % half + LANES)
            if slot * LANES < half:
                grad = mine_ref[here, lanes] + theirs_ref[here, lanes].astype(jnp.float32)
            else:
                grad = late[:, lanes]
            columns = pl.ds(pl.multiple_of(meta_ref[1 + slot] * LANES, LANES), LANES)
            gate = acts_ref[0, here, columns].astype(jnp.float32)
            upper = acts_ref[1, here, columns].astype(jnp.float32)
            sigm = sigmoid(gate)
            out_ref[0, :, columns] = (grad * upper * sigm * (1.0 + gate * (1.0 - sigm))).astype(out_ref.dtype)
            out_ref[1, :, columns] = (grad * (gate * sigm)).astype(out_ref.dtype)

    ins = [in_vmem(a) for a in (acts, *early, weight, turned, *back, far)]
    outs = [(jax.ShapeDtypeStruct(acts.shape, acts.dtype), pl.BlockSpec((2, tile, tokens), lambda i, m: (0, i, 0)))]
    return call(kernel, "gate_grad", meta, (4,), ins, outs, after=after, vmem=12)


def wait_for(meta, after, weight):
    return call(lambda meta_ref: None, "arrived", meta, (1,), [], [], after=after, weight=weight, vmem=1)[0]


ARRIVALS = ((0, 1, 2, 3), (1, 0, 2, 3), (2, 3, 1, 0), (3, 2, 1, 0))


def describe(me, z):
    tables = [np.array([0, *order], np.int32) for order in ARRIVALS]
    meta = jnp.asarray(tables[0])
    for k in range(1, len(tables)):
        meta = jnp.where(z == k, tables[k], meta)
    return meta + me * np.array([1, 0, 0, 0, 0], np.int32)


def two_level(cotangent, down_weight, pre_acts):
    me, z = lax.axis_index("grp"), lax.axis_index("inner")
    total_rows = down_weight.shape[0]
    rows = pre_acts.shape[1]
    each, feats = cotangent.shape
    tokens = 2 * each
    across_core = functools.partial(lax.ppermute, axis_name="grp", perm=[(k, k ^ 1) for k in range(4)])
    across_x = functools.partial(lax.ppermute, axis_name="grp", perm=[(k, k ^ 2) for k in range(4)])
    in_pairs = functools.partial(lax.ppermute, axis_name="inner", perm=[(0, 1), (1, 0), (2, 3), (3, 2)])
    in_middle = functools.partial(lax.ppermute, axis_name="inner", perm=[(1, 2), (2, 1)])
    outwards = functools.partial(lax.ppermute, axis_name="inner", perm=[(1, 0), (2, 3)])
    meta = describe(me, z)
    bf16, f32 = jnp.bfloat16, jnp.float32

    hidden = hidden_rows(pre_acts, 0, (rows // 2,))
    hidden = [*hidden, *hidden_rows(pre_acts, rows // 2, (rows // 2,), after=hidden)]
    hidden[1], cotangent = lax.optimization_barrier((hidden[1], cotangent))
    hidden_far = [across_x(h) for h in hidden]
    hidden_core = [across_core(h) for h in hidden]

    near, second = in_pairs(cotangent), in_middle(cotangent)
    third, outer = in_middle(near), outwards(second)
    third, outer = lax.optimization_barrier((third, outer))
    outmost = outwards(third)
    slots = [
        Slot(0, [cotangent], [(0, 1, 2, 3)]),
        Slot(1, [near], [(0, 1, 2, 3)]),
        Slot(2, [second, outer], [(1, 2), (0, 3)]),
        Slot(3, [third, outmost], [(1, 2), (0, 3)]),
    ]

    sums = functools.partial(partials, meta, rows=rows, tokens=tokens)
    turned, done = turned_slots(meta, slots[:2], each, feats, after=(hidden_far[0],), weight=SHORT)
    *sent, kept_sent, _ = sums(
        (3, 1), down_weight, dtypes=(bf16, bf16), splits=2, turned=turned, after=(done, *hidden_core), weight_of=LONG
    )
    back = [across_core(p) for p in sent]
    a_sum, kept_sum, done = sums((2,), down_weight, dtypes=(bf16,), splits=1, turned=turned, adds=(back[:2],))
    a_far = across_x(a_sum)
    a_own, kept_own, done = sums(
        (0,), down_weight, dtypes=(f32,), splits=1, turned=turned, adds=(back[2:],), after=(done, hidden_far[1]), weight_of=MIDDLE
    )

    *sent, turned, done = sums((3, 1), kept_sent, dtypes=(bf16, bf16), splits=2, slots=slots[2:], keep=False, after=(done,))
    back = [across_core(p) for p in sent]
    cots, done = all_slots(meta, slots, each, feats, after=(done,))
    hidden_both = [across_core(h) for h in hidden_far]
    b_sum, done = sums((2,), kept_sum, dtypes=(bf16,), splits=1, turned=turned, adds=(back[:2],), keep=False, after=(done,))
    b_far = across_x(b_sum)
    done = wait_for(meta, (done, a_far), BRIEF)
    grad_down, done = weight_grad(
        meta, (0, 1, 2, 3), (hidden, hidden_core, hidden_far, hidden_both), cots, None, total_rows, after=(done,), weight=200 * 10**9
    )
    grad_pre, _ = gate_grad(meta, pre_acts, (a_own, a_far), kept_own, turned, back[2:], b_far, after=(done,))
    return grad_pre, grad_down


def plain(cotangent, down_weight, pre_acts):
    all_rows = lax.all_gather(cotangent, "inner", axis=0, tiled=True)
    hidden = hidden_of(pre_acts)
    grad = lax.psum_scatter(
        jnp.einsum("fd,td->ft", down_weight, all_rows, preferred_element_type=jnp.float32),
        "grp",
        scatter_dimension=0,
        tiled=True,
    )
    gate = pre_acts[0].astype(jnp.float32)
    upper = pre_acts[1].astype(jnp.float32)
    sigm = jax.nn.sigmoid(gate)
    grad_gate = grad * upper * sigm * (1.0 + gate * (1.0 - sigm))
    grad_pre = jnp.stack([grad_gate, grad * (gate * sigm)]).astype(jnp.bfloat16)
    grad_down = jnp.dot(
        lax.all_gather(hidden, "grp", axis=0, tiled=True), all_rows, preferred_element_type=jnp.float32
    ).astype(jnp.bfloat16)
    return grad_pre, grad_down


def solution(mesh):
    inner, grp = mesh.shape["inner"], mesh.shape["grp"]

    def on_device(cotangent, down_weight, pre_acts):
        if grp == 4 and inner == 4 and cotangent.shape[0] == LANES and pre_acts.shape[1] % 128 == 0:
            return two_level(cotangent, down_weight, pre_acts)
        return plain(cotangent, down_weight, pre_acts)

    return jax.shard_map(
        on_device,
        mesh=mesh,
        in_specs=(
            P(("parts", "inner"), "grp"),
            P("inner", "grp"),
            P(None, ("inner", "grp"), "parts"),
        ),
        out_specs=(P(None, ("inner", "grp"), "parts"), P(("parts", "inner"), "grp")),
        check_vma=False,
    )
```

time: 111 us -> 98.3 us (0.89); the launches traced: 110 us -> 97.9 us
  Pallas kernels: 69.7 us -> 61.3 us
  starting transfers between devices: 18.9 us -> 17 us
    pallas_call x10, Pallas kernels: 66.4 us -> 57.4 us  [call(): pl.pallas_call(body, grid_spec=pltpu.PrefetchScalarGridSpec(num_scalar_pr...]
    ppermute x8 -> x6, waiting for transfers between devices: 12.3 us -> 17.4 us  [the longest x2 10.2 us: two_level(): near, second = (in_pairs(cotangent), in_middle(cotangent))]
    ppermute x3 -> x2, waiting for transfers between devices: 4.41 us -> 0.15 us  [two_level(): hidden_far = [across_x(h) for h in hidden]]
    ppermute x8 -> x6, starting transfers between devices: 11.9 us -> 9.82 us  [the longest x2 5.13 us: two_level(): near, second = (in_pairs(cotangent), in_middle(cotangent))]
    ppermute x8, waiting for transfers between devices: 2.44 us -> 0.97 us  [two_level(): back = [across_core(p) for p in sent]]
    pallas_call x1 -> x2, Pallas kernels: 3.33 us -> 3.92 us  [hidden_rows(): pl.pallas_call(kernel, in_specs=[spec, *[anywhere(a)[1] for a in after]],...]
    ppermute x3 -> x2, starting transfers between devices: 3.86 us -> 3.6 us  [two_level(): hidden_far = [across_x(h) for h in hidden]]
  transfers between devices with their start and end apart: 26 -> 21, of which waited for: 11 -> 7; matrix products, arithmetic and copies ran while one was open for 0% -> 0% of each run, Pallas kernels for 57% -> 53%
where the time goes in v2:
time: 98.3 us; the launch traced here: 97.9 us
  Pallas kernels  61.3 us (62%)
  waiting for transfers between devices  18.5 us (19%)
  starting transfers between devices  17 us (17%)
    pallas_call x10, Pallas kernels, call(): pl.pallas_call(body, grid_spec=pltpu.PrefetchScalarGridSpec(num_scalar_pr...  57.4 us
    ppermute x2, waiting for transfers between devices, two_level(): near, second = (in_pairs(cotangent), in_middle(cotangent))  10.2 us
    ppermute x2, starting transfers between devices, two_level(): near, second = (in_pairs(cotangent), in_middle(cotangent))  5.13 us
    ppermute x1, waiting for transfers between devices, two_level(): outmost = outwards(third)  4.67 us
    pallas_call x2, Pallas kernels, hidden_rows(): pl.pallas_call(kernel, in_specs=[spec, *[anywhere(a)[1] for a in after]],...  3.92 us
    ppermute x2, starting transfers between devices, two_level(): hidden_far = [across_x(h) for h in hidden]  3.6 us
    ppermute x2, waiting for transfers between devices, two_level(): third, outer = (in_middle(near), outwards(second))  2.17 us
  transfers between devices with their start and end apart: 21, of which 7 were waited for; matrix products, arithmetic and copies ran while one was open for 0% of the time, Pallas kernels for 53%

profile of v2, /device:TPU:0, one launch (start us, length us, event | category | flops | bytes accessed | tf_op | source)
XLA Modules:
  0.0 97.9 jit_solution(1338373602054119798)
XLA Ops:
  0.7 2.0 %hidden.2.refs_0_.refs_1_ = bf16[832,512]{1,0:T(8,128)(2,1)S(1)} custom-call(bf16[2,1664,512]{2,1,0:T(8,128)(2,1)} %refs_0_.9), custom_call_target="tpu_custom_call" | custom-call | flops 1 | bytes 1 | tf_op jit(solution)/shard_map/hidden/pallas_call | solution.py:96
  2.7 3.0 %collective-permute-start.1 = (bf16[832,512]{1,0:T(8,128)(2,1)S(1)}, bf16[832,512]{1,0:T(8,128)(2,1)}, u32[]{:S(2)}, u32[]{:S(2)}) collective-permute-start(bf16[832,512]{1,0:T(8,128)(2,1)S(1)} %hidden.2.refs_0_.refs_1_), channel_id=1, source_target_pairs={{0,2},{1,3},{2,0},{3,1},{4,6},{5,7},{6,4},{7,5},{8,10},{9,11},{10,... | collective-permute-start | bytes 2555912 | tf_op jit(solution)/shard_map/ppermute | solution.py:345
  5.7 1.9 %hidden.3.refs_2_ = bf16[832,512]{1,0:T(8,128)(2,1)S(1)} custom-call(bf16[2,1664,512]{2,1,0:T(8,128)(2,1)} %refs_0_.9, bf16[832,512]{1,0:T(8,128)(2,1)S(1)} %hidden.2.refs_0_.refs_1_), custom_call_target="tpu_custom_call" | custom-call | flops 1 | bytes 1 | tf_op jit(solution)/shard_map/hidden/pallas_call | solution.py:96
  7.7 0.7 collective-permute-start.10
  8.4 4.4 %collective-permute-start = (bf16[128,2048]{1,0:T(8,128)(2,1)S(1)}, bf16[128,2048]{1,0:T(8,128)(2,1)S(1)}, u32[]{:S(2)}, u32[]{:S(2)}) collective-permute-start(bf16[128,2048]{1,0:T(8,128)(2,1)S(1)} %copy-done.5), channel_id=1, source_target_pairs={{0,4},{4,0},{8,12},{12,8},{1,5},{5,1},{9,13},{13,9},{2,6},{6,2},{1... | collective-permute-start | bytes 1572872 | tf_op jit(solution)/shard_map/ppermute | solution.py:348
  12.8 0.5 collective-permute-start.2
  13.3 0.6 collective-permute-start.8
  14.0 10.2 %collective-permute-done.refs_1_ = bf16[128,2048]{1,0:T(8,128)(2,1)S(1)} collective-permute-done((bf16[128,2048]{1,0:T(8,128)(2,1)S(1)}, bf16[128,2048]{1,0:T(8,128)(2,1)S(1)}, u32[]{:S(2)}, u32[]{:S(2)}) %collective-permute-start) | collective-permute-done | bytes 524320 | tf_op jit(solution)/shard_map/ppermute | solution.py:348
  24.2 1.3 %collective-permute-start.12 = (bf16[128,2048]{1,0:T(8,128)(2,1)S(1)}, bf16[128,2048]{1,0:T(8,128)(2,1)S(1)}, u32[]{:S(2)}, u32[]{:S(2)}) collective-permute-start(bf16[128,2048]{1,0:T(8,128)(2,1)S(1)} %collective-permute-done.10.refs_1_.refs_2_), channel_id=1, source_target_pairs={{4,0},{8,12},{5,1},{9,13},{6,2},{10,14},{7,3},{11,15},{20,16},{24,... | collective-permute-start | bytes 1572872 | tf_op jit(solution)/shard_map/ppermute | solution.py:349
  25.6 0.7 collective-permute-start.11
  26.3 1.0 turned.1
  27.3 8.6 %partials.5 = (bf16[832,256]{1,0:T(8,128)(2,1)S(1)}, bf16[832,256]{1,0:T(8,128)(2,1)S(1)}, bf16[832,256]{1,0:T(8,128)(2,1)S(1)}, bf16[832,256]{1,0:T(8,128)(2,1)...) custom-call(s32[5]{0:T(128)S(1)} %fusion.meta_ref, bf16[6656,2048]{1,0:T(8,128)(2,1)} %refs_0_.7, ...), custom_call_target="tpu_custom_call" | custom-call | flops 20000000000 | bytes 1 | tf_op jit(solution)/shard_map/partials/pallas_call | solution.py:61
  35.9 0.5 collective-permute-start.7
  36.4 2.2 %collective-permute-done.12.refs_2_.refs_3_ = bf16[128,2048]{1,0:T(8,128)(2,1)S(1)} collective-permute-done((bf16[128,2048]{1,0:T(8,128)(2,1)S(1)}, bf16[128,2048]{1,0:T(8,128)(2,1)S(1)}, u32[]{:S(2)}, u32[]{:S(2)}) %collective-permute-start.12) | collective-permute-done | bytes 524320 | tf_op jit(solution)/shard_map/ppermute | solution.py:349
  38.6 0.5 collective-permute-start.5
  39.1 1.3 %collective-permute-start.13 = (bf16[128,2048]{1,0:T(8,128)(2,1)S(1)}, bf16[128,2048]{1,0:T(8,128)(2,1)S(1)}, u32[]{:S(2)}, u32[]{:S(2)}) collective-permute-start(bf16[128,2048]{1,0:T(8,128)(2,1)S(1)} %collective-permute-done.11.refs_3_.refs_4_), channel_id=1, source_target_pairs={{4,0},{8,12},{5,1},{9,13},{6,2},{10,14},{7,3},{11,15},{20,16},{24,... | collective-permute-start | bytes 1572872 | tf_op jit(solution)/shard_map/ppermute | solution.py:351
  40.4 4.9 %partials.6 = (bf16[1664,256]{1,0:T(8,128)(2,1)S(1)}, bf16[1664,2048]{1,0:T(8,128)(2,1)S(1)}, f32[8,128]{1,0:T(8,128)S(1)}) custom-call(s32[5]{0:T(128)S(1)} %fusion.meta_ref, bf16[6656,2048]{1,0:T(8,128)(2,1)} %refs_0_.7, bf16[2048,256]{1,0:T(8,128)(2,1)S(1)} %get-tuple-element.33.refs_1_, bf16[832,256]{1,0:T(8,128)(2,1)S(1)} %collective-permute-done.6.refs_2_, ...), custom_call_target="tpu_custom_call" | custom-call | flops 1 | bytes 1 | tf_op jit(solution)/shard_map/partials/pallas_call | solution.py:61
  45.4 0.7 collective-permute-start.9
  46.1 0.5 collective-permute-start.20
  46.6 4.9 %partials.7 = (f32[1664,256]{1,0:T(8,128)S(1)}, bf16[1664,2048]{1,0:T(8,128)(2,1)S(1)}, f32[8,128]{1,0:T(8,128)S(1)}) custom-call(s32[5]{0:T(128)S(1)} %fusion.meta_ref, bf16[6656,2048]{1,0:T(8,128)(2,1)} %refs_0_.7, bf16[2048,256]{1,0:T(8,128)(2,1)S(1)} %get-tuple-element.33.refs_1_, bf16[832,256]{1,0:T(8,128)(2,1)S(1)} %collective-permute-done.4.refs_2_, ...), custom_call_target="tpu_custom_call" | custom-call | flops 4190000128 | bytes 1 | tf_op jit(solution)/shard_map/partials/pallas_call | solution.py:61
  51.5 4.7 %collective-permute-done.13.refs_4_.refs_5_ = bf16[128,2048]{1,0:T(8,128)(2,1)S(1)} collective-permute-done((bf16[128,2048]{1,0:T(8,128)(2,1)S(1)}, bf16[128,2048]{1,0:T(8,128)(2,1)S(1)}, u32[]{:S(2)}, u32[]{:S(2)}) %collective-permute-start.13) | collective-permute-done | bytes 524320 | tf_op jit(solution)/shard_map/ppermute | solution.py:351
  56.2 6.4 %partials.8 = (bf16[832,256]{1,0:T(8,128)(2,1)S(1)}, bf16[832,256]{1,0:T(8,128)(2,1)S(1)}, bf16[832,256]{1,0:T(8,128)(2,1)}, bf16[832,256]{1,0:T(8,128)(2,1)}, b...) custom-call(s32[5]{0:T(128)S(1)} %fusion.meta_ref, bf16[3328,2048]{1,0:T(8,128)(2,1)S(1)} %get-tuple-element.44.refs_0_, ...), custom_call_target="tpu_custom_call" | custom-call | flops 1 | bytes 1 | tf_op jit(solution)/shard_map/partials/pallas_call | solution.py:61
  62.7 0.5 collective-permute-start.17
  63.2 0.8 token_rows.1
  63.9 0.5 collective-permute-done.16.refs_2_
  64.6 0.5 collective-permute-done.17.refs_3_
  65.2 3.8 %partials.9 = (bf16[1664,256]{1,0:T(8,128)(2,1)}, f32[8,128]{1,0:T(8,128)S(1)}) custom-call(s32[5]{0:T(128)S(1)} %fusion.meta_ref, bf16[1664,2048]{1,0:T(8,128)(2,1)S(1)} %get-tuple-element.51.refs_0_, bf16[2048,256]{1,0:T(8,128)(2,1)S(1)} %get-tuple-element.48.refs_1_.refs_4_, bf16[832,256]{1,0:T(8,128)(2,1)S(1)} %collective-permute-done.16.refs_2_, ...), custom_call_target="tpu_custom_call" | custom-call | flops 1 | bytes 1 | tf_op jit(solution)/shard_map/partials/pallas_call | solution.py:61
  69.0 1.4 %collective-permute-start.18 = (bf16[1664,256]{1,0:T(8,128)(2,1)}, bf16[1664,256]{1,0:T(8,128)(2,1)}, u32[]{:S(2)}, u32[]{:S(2)}) collective-permute-start(bf16[1664,256]{1,0:T(8,128)(2,1)} %get-tuple-element.56), channel_id=1, source_target_pairs={{0,2},{1,3},{2,0},{3,1},{4,6},{5,7},{6,4},{7,5},{8,10},{9,11},{10,... | collective-permute-start | bytes 2555912 | tf_op jit(solution)/shard_map/ppermute | solution.py:376
  70.4 0.5 arrived.1.refs_9_
  71.0 19.1 %weight_grad.1 = (bf16[6656,2048]{1,0:T(8,128)(2,1)}, f32[8,128]{1,0:T(8,128)S(1)}) custom-call(s32[5]{0:T(128)S(1)} %fusion.meta_ref, bf16[512,2048]{1,0:T(8,128)(2,1)S(1)} %get-tuple-element.57.refs_0_, bf16[832,512]{1,0:T(8,128)(2,1)S(1)} %hidden.2.refs_0_.refs_1_, bf16[832,512]{1,0:T(8,128)(2,1)S(1)} %hidden.3.refs_2_, ...), custom_call_target="tpu_custom_call" | custom-call | flops 199999995904 | bytes 1 | tf_op jit(solution)/shard_map/weight_grad/pallas_call | solution.py:61
  90.1 0.4 collective-permute-done.18.refs_7_
  90.5 7.4 %gate_grad.1 = (bf16[2,1664,512]{2,1,0:T(8,128)(2,1)}, f32[8,128]{1,0:T(8,128)}) custom-call(s32[5]{0:T(128)S(1)} %fusion.meta_ref, bf16[2,1664,512]{2,1,0:T(8,128)(2,1)S(1)} %copy-done, f32[1664,256]{1,0:T(8,128)S(1)} %get-tuple-element.41.refs_1_, bf16[1664,256]{1,0:T(8,128)(2,1)S(1)} %copy-done.4, bf16[1664,2048]{1,0:T(8,128)(2,1)S(1)} %get-tuple-element.43.refs_3_, ...), custom_call_target="tpu_custom_call" | custom-call | flops 1 | bytes 1 | tf_op jit(solution)/shard_map/gate_grad/pallas_call | solution.py:61
  (45 shorter events, 0.7 us)
Async XLA Ops:
  0.6 12.7 %copy-start.6 = (s32[5]{0:T(128)S(1)}, s32[5]{0:T(128)}, u32[]{:S(2)}) copy-start(s32[5]{0:T(128)} %constant.27.clone) | copy-start | bytes 64
  0.6 12.7 %copy-start.7 = (s32[5]{0:T(128)S(1)}, s32[5]{0:T(128)}, u32[]{:S(2)}) copy-start(s32[5]{0:T(128)} %constant.26.clone) | copy-start | bytes 64
  0.7 12.7 %copy-start.8 = (s32[5]{0:T(128)S(1)}, s32[5]{0:T(128)}, u32[]{:S(2)}) copy-start(s32[5]{0:T(128)} %constant.25.clone) | copy-start | bytes 64
  0.7 12.6 %copy-start.9 = (s32[5]{0:T(128)S(1)}, s32[5]{0:T(128)}, u32[]{:S(2)}) copy-start(s32[5]{0:T(128)} %constant.24.clone) | copy-start | bytes 64
  0.7 12.6 %copy-start.10 = (s32[5]{0:T(128)S(1)}, s32[5]{0:T(128)}, u32[]{:S(2)}) copy-start(s32[5]{0:T(128)} %constant.23.clone) | copy-start | bytes 64
  0.7 7.0 %copy-start.5 = (bf16[128,2048]{1,0:T(8,128)(2,1)S(1)}, bf16[128,2048]{1,0:T(8,128)(2,1)}, u32[]{:S(2)}) copy-start(bf16[128,2048]{1,0:T(8,128)(2,1)} %refs_0_.8) | copy-start | bytes 1572868
  2.7 22.9 %collective-permute-start.1 = (bf16[832,512]{1,0:T(8,128)(2,1)S(1)}, bf16[832,512]{1,0:T(8,128)(2,1)}, u32[]{:S(2)}, u32[]{:S(2)}) collective-permute-start(bf16[832,512]{1,0:T(8,128)(2,1)S(1)} %hidden.2.refs_0_.refs_1_), channel_id=1, source_target_pairs={{0,2},{1,3},{2,0},{3,1},{4,6},{5,7},{6,4},{7,5},{8,10},{9,11},{10,... | collective-permute-start | bytes 2555912 | tf_op jit(solution)/shard_map/ppermute | solution.py:345
  7.7 5.7 %collective-permute-start.10 = (bf16[128,2048]{1,0:T(8,128)(2,1)S(1)}, bf16[128,2048]{1,0:T(8,128)(2,1)S(1)}, u32[]{:S(2)}, u32[]{:S(2)}) collective-permute-start(bf16[128,2048]{1,0:T(8,128)(2,1)S(1)} %copy-done.5), channel_id=1, source_target_pairs={{4,8},{8,4},{5,9},{9,5},{6,10},{10,6},{7,11},{11,7},{20,24},{24,20... | collective-permute-start | bytes 1572872 | tf_op jit(solution)/shard_map/ppermute | solution.py:348
  8.4 15.8 %collective-permute-start = (bf16[128,2048]{1,0:T(8,128)(2,1)S(1)}, bf16[128,2048]{1,0:T(8,128)(2,1)S(1)}, u32[]{:S(2)}, u32[]{:S(2)}) collective-permute-start(bf16[128,2048]{1,0:T(8,128)(2,1)S(1)} %copy-done.5), channel_id=1, source_target_pairs={{0,4},{4,0},{8,12},{12,8},{1,5},{5,1},{9,13},{13,9},{2,6},{6,2},{1... | collective-permute-start | bytes 1572872 | tf_op jit(solution)/shard_map/ppermute | solution.py:348
  12.8 14.5 %collective-permute-start.3 = (bf16[832,512]{1,0:T(8,128)(2,1)S(1)}, bf16[832,512]{1,0:T(8,128)(2,1)}, u32[]{:S(2)}, u32[]{:S(2)}) collective-permute-start(bf16[832,512]{1,0:T(8,128)(2,1)S(1)} %hidden.3.refs_2_), channel_id=1, source_target_pairs={{0,1},{1,0},{2,3},{3,2},{4,5},{5,4},{6,7},{7,6},{8,9},{9,8},{10,11... | collective-permute-start | bytes 2555912 | tf_op jit(solution)/shard_map/ppermute | solution.py:346
  12.8 14.5 %collective-permute-start.2 = (bf16[832,512]{1,0:T(8,128)(2,1)S(1)}, bf16[832,512]{1,0:T(8,128)(2,1)}, u32[]{:S(2)}, u32[]{:S(2)}) collective-permute-start(bf16[832,512]{1,0:T(8,128)(2,1)S(1)} %hidden.2.refs_0_.refs_1_), channel_id=1, source_target_pairs={{0,1},{1,0},{2,3},{3,2},{4,5},{5,4},{6,7},{7,6},{8,9},{9,8},{10,11... | collective-permute-start | bytes 2555912 | tf_op jit(solution)/shard_map/ppermute | solution.py:346
  13.3 32.7 %collective-permute-start.8 = (bf16[832,512]{1,0:T(8,128)(2,1)S(1)}, bf16[832,512]{1,0:T(8,128)(2,1)S(1)}, u32[]{:S(2)}, u32[]{:S(2)}) collective-permute-start(bf16[832,512]{1,0:T(8,128)(2,1)S(1)} %hidden.3.refs_2_), channel_id=1, source_target_pairs={{0,2},{1,3},{2,0},{3,1},{4,6},{5,7},{6,4},{7,5},{8,10},{9,11},{10,... | collective-permute-start | bytes 2555912 | tf_op jit(solution)/shard_map/ppermute | solution.py:345
  24.2 14.5 %collective-permute-start.12 = (bf16[128,2048]{1,0:T(8,128)(2,1)S(1)}, bf16[128,2048]{1,0:T(8,128)(2,1)S(1)}, u32[]{:S(2)}, u32[]{:S(2)}) collective-permute-start(bf16[128,2048]{1,0:T(8,128)(2,1)S(1)} %collective-permute-done.10.refs_1_.refs_2_), channel_id=1, source_target_pairs={{4,0},{8,12},{5,1},{9,13},{6,2},{10,14},{7,3},{11,15},{20,16},{24,... | collective-permute-start | bytes 1572872 | tf_op jit(solution)/shard_map/ppermute | solution.py:349
  25.6 13.0 %collective-permute-start.11 = (bf16[128,2048]{1,0:T(8,128)(2,1)S(1)}, bf16[128,2048]{1,0:T(8,128)(2,1)S(1)}, u32[]{:S(2)}, u32[]{:S(2)}) collective-permute-start(bf16[128,2048]{1,0:T(8,128)(2,1)S(1)} %collective-permute-done.refs_1_), channel_id=1, source_target_pairs={{4,8},{8,4},{5,9},{9,5},{6,10},{10,6},{7,11},{11,7},{20,24},{24,20... | collective-permute-start | bytes 1572872 | tf_op jit(solution)/shard_map/ppermute | solution.py:349
  35.9 3.3 %collective-permute-start.6 = (bf16[832,256]{1,0:T(8,128)(2,1)S(1)}, bf16[832,256]{1,0:T(8,128)(2,1)S(1)}, u32[]{:S(2)}, u32[]{:S(2)}) collective-permute-start(bf16[832,256]{1,0:T(8,128)(2,1)S(1)} %get-tuple-element.38), channel_id=1, source_target_pairs={{0,1},{1,0},{2,3},{3,2},{4,5},{5,4},{6,7},{7,6},{8,9},{9,8},{10,11... | collective-permute-start | bytes 1277960 | tf_op jit(solution)/shard_map/ppermute | solution.py:364
  35.9 4.5 %collective-permute-start.7 = (bf16[832,256]{1,0:T(8,128)(2,1)S(1)}, bf16[832,256]{1,0:T(8,128)(2,1)S(1)}, u32[]{:S(2)}, u32[]{:S(2)}) collective-permute-start(bf16[832,256]{1,0:T(8,128)(2,1)S(1)} %get-tuple-element.39), channel_id=1, source_target_pairs={{0,1},{1,0},{2,3},{3,2},{4,5},{5,4},{6,7},{7,6},{8,9},{9,8},{10,11... | collective-permute-start | bytes 1277960 | tf_op jit(solution)/shard_map/ppermute | solution.py:364
  38.6 7.5 %collective-permute-start.4 = (bf16[832,256]{1,0:T(8,128)(2,1)S(1)}, bf16[832,256]{1,0:T(8,128)(2,1)S(1)}, u32[]{:S(2)}, u32[]{:S(2)}) collective-permute-start(bf16[832,256]{1,0:T(8,128)(2,1)S(1)} %get-tuple-element.36), channel_id=1, source_target_pairs={{0,1},{1,0},{2,3},{3,2},{4,5},{5,4},{6,7},{7,6},{8,9},{9,8},{10,11... | collective-permute-start | bytes 1277960 | tf_op jit(solution)/shard_map/ppermute | solution.py:364
  38.6 8.0 %collective-permute-start.5 = (bf16[832,256]{1,0:T(8,128)(2,1)S(1)}, bf16[832,256]{1,0:T(8,128)(2,1)S(1)}, u32[]{:S(2)}, u32[]{:S(2)}) collective-permute-start(bf16[832,256]{1,0:T(8,128)(2,1)S(1)} %get-tuple-element.37), channel_id=1, source_target_pairs={{0,1},{1,0},{2,3},{3,2},{4,5},{5,4},{6,7},{7,6},{8,9},{9,8},{10,11... | collective-permute-start | bytes 1277960 | tf_op jit(solution)/shard_map/ppermute | solution.py:364
  39.1 17.0 %collective-permute-start.13 = (bf16[128,2048]{1,0:T(8,128)(2,1)S(1)}, bf16[128,2048]{1,0:T(8,128)(2,1)S(1)}, u32[]{:S(2)}, u32[]{:S(2)}) collective-permute-start(bf16[128,2048]{1,0:T(8,128)(2,1)S(1)} %collective-permute-done.11.refs_3_.refs_4_), channel_id=1, source_target_pairs={{4,0},{8,12},{5,1},{9,13},{6,2},{10,14},{7,3},{11,15},{20,16},{24,... | collective-permute-start | bytes 1572872 | tf_op jit(solution)/shard_map/ppermute | solution.py:351
  45.4 23.6 %collective-permute-start.9 = (bf16[1664,256]{1,0:T(8,128)(2,1)S(1)}, bf16[1664,256]{1,0:T(8,128)(2,1)S(1)}, u32[]{:S(2)}, u32[]{:S(2)}) collective-permute-start(bf16[1664,256]{1,0:T(8,128)(2,1)S(1)} %get-tuple-element.42), channel_id=1, source_target_pairs={{0,2},{1,3},{2,0},{3,1},{4,6},{5,7},{6,4},{7,5},{8,10},{9,11},{10,... | collective-permute-start | bytes 2555912 | tf_op jit(solution)/shard_map/ppermute | solution.py:366
  46.1 24.9 %collective-permute-start.19 = (bf16[832,512]{1,0:T(8,128)(2,1)}, bf16[832,512]{1,0:T(8,128)(2,1)S(1)}, u32[]{:S(2)}, u32[]{:S(2)}) collective-permute-start(bf16[832,512]{1,0:T(8,128)(2,1)} %collective-permute-done.1.refs_2_.refs_5_), channel_id=1, source_target_pairs={{0,1},{1,0},{2,3},{3,2},{4,5},{5,4},{6,7},{7,6},{8,9},{9,8},{10,11... | collective-permute-start | bytes 2555912 | tf_op jit(solution)/shard_map/ppermute | solution.py:374
  46.1 24.9 %collective-permute-start.20 = (bf16[832,512]{1,0:T(8,128)(2,1)S(1)}, bf16[832,512]{1,0:T(8,128)(2,1)S(1)}, u32[]{:S(2)}, u32[]{:S(2)}) collective-permute-start(bf16[832,512]{1,0:T(8,128)(2,1)S(1)} %collective-permute-done.8.refs_5_.refs_6_), channel_id=1, source_target_pairs={{0,1},{1,0},{2,3},{3,2},{4,5},{5,4},{6,7},{7,6},{8,9},{9,8},{10,11... | collective-permute-start | bytes 2555912 | tf_op jit(solution)/shard_map/ppermute | solution.py:374
  62.6 8.4 %copy-start.1 = (bf16[2048,256]{1,0:T(8,128)(2,1)}, bf16[2048,256]{1,0:T(8,128)(2,1)S(1)}, u32[]{:S(2)}) copy-start(bf16[2048,256]{1,0:T(8,128)(2,1)S(1)} %get-tuple-element.48.refs_1_.refs_4_) | copy-start | bytes 3145732
  62.6 1.8 %collective-permute-start.16 = (bf16[832,256]{1,0:T(8,128)(2,1)S(1)}, bf16[832,256]{1,0:T(8,128)(2,1)S(1)}, u32[]{:S(2)}, u32[]{:S(2)}) collective-permute-start(bf16[832,256]{1,0:T(8,128)(2,1)S(1)} %get-tuple-element.52), channel_id=1, source_target_pairs={{0,1},{1,0},{2,3},{3,2},{4,5},{5,4},{6,7},{7,6},{8,9},{9,8},{10,11... | collective-permute-start | bytes 1277960 | tf_op jit(solution)/shard_map/ppermute | solution.py:372
  62.7 2.4 %collective-permute-start.17 = (bf16[832,256]{1,0:T(8,128)(2,1)S(1)}, bf16[832,256]{1,0:T(8,128)(2,1)S(1)}, u32[]{:S(2)}, u32[]{:S(2)}) collective-permute-start(bf16[832,256]{1,0:T(8,128)(2,1)S(1)} %get-tuple-element.53), channel_id=1, source_target_pairs={{0,1},{1,0},{2,3},{3,2},{4,5},{5,4},{6,7},{7,6},{8,9},{9,8},{10,11... | collective-permute-start | bytes 1277960 | tf_op jit(solution)/shard_map/ppermute | solution.py:372
  64.4 25.7 %collective-permute-start.14 = (bf16[832,256]{1,0:T(8,128)(2,1)}, bf16[832,256]{1,0:T(8,128)(2,1)}, u32[]{:S(2)}, u32[]{:S(2)}) collective-permute-start(bf16[832,256]{1,0:T(8,128)(2,1)} %get-tuple-element.49), channel_id=1, source_target_pairs={{0,1},{1,0},{2,3},{3,2},{4,5},{5,4},{6,7},{7,6},{8,9},{9,8},{10,11... | collective-permute-start | bytes 1277960 | tf_op jit(solution)/shard_map/ppermute | solution.py:372
  65.0 25.1 %collective-permute-start.15 = (bf16[832,256]{1,0:T(8,128)(2,1)}, bf16[832,256]{1,0:T(8,128)(2,1)}, u32[]{:S(2)}, u32[]{:S(2)}) collective-permute-start(bf16[832,256]{1,0:T(8,128)(2,1)} %get-tuple-element.50), channel_id=1, source_target_pairs={{0,1},{1,0},{2,3},{3,2},{4,5},{5,4},{6,7},{7,6},{8,9},{9,8},{10,11... | collective-permute-start | bytes 1277960 | tf_op jit(solution)/shard_map/ppermute | solution.py:372
  68.9 2.0 %copy-start.3 = (bf16[1664,256]{1,0:T(8,128)(2,1)}, bf16[1664,256]{1,0:T(8,128)(2,1)S(1)}, u32[]{:S(2)}) copy-start(bf16[1664,256]{1,0:T(8,128)(2,1)S(1)} %collective-permute-done.9.refs_1_.refs_2_) | copy-start | bytes 2555908
  69.0 21.5 %collective-permute-start.18 = (bf16[1664,256]{1,0:T(8,128)(2,1)}, bf16[1664,256]{1,0:T(8,128)(2,1)}, u32[]{:S(2)}, u32[]{:S(2)}) collective-permute-start(bf16[1664,256]{1,0:T(8,128)(2,1)} %get-tuple-element.56), channel_id=1, source_target_pairs={{0,2},{1,3},{2,0},{3,1},{4,6},{5,7},{6,4},{7,5},{8,10},{9,11},{10,... | collective-permute-start | bytes 2555912 | tf_op jit(solution)/shard_map/ppermute | solution.py:376
  71.0 19.5 %copy-start = (bf16[2,1664,512]{2,1,0:T(8,128)(2,1)S(1)}, bf16[2,1664,512]{2,1,0:T(8,128)(2,1)}, u32[]{:S(2)}) copy-start(bf16[2,1664,512]{2,1,0:T(8,128)(2,1)} %refs_0_.9) | copy-start | bytes 10223620
  71.0 19.5 %copy-start.2 = (bf16[2048,256]{1,0:T(8,128)(2,1)S(1)}, bf16[2048,256]{1,0:T(8,128)(2,1)}, u32[]{:S(2)}) copy-start(bf16[2048,256]{1,0:T(8,128)(2,1)} %copy-done.1) | copy-start | bytes 3145732
  71.0 19.5 %copy-start.4 = (bf16[1664,256]{1,0:T(8,128)(2,1)S(1)}, bf16[1664,256]{1,0:T(8,128)(2,1)}, u32[]{:S(2)}) copy-start(bf16[1664,256]{1,0:T(8,128)(2,1)} %copy-done.3) | copy-start | bytes 2555908

commit v3 on v2

--- a/solution.py
+++ b/solution.py
@@ -10,7 +10,7 @@
 from jax.sharding import PartitionSpec as P
 
 LANES = 128
-LONG, SHORT, MIDDLE, BRIEF = 20 * 10**9, 4700 * 10**6, 4190 * 10**6, 790 * 10**6
+TURNED, ARRIVED = 7000 * 10**6, 9200 * 10**6
 MIB = 1024 * 1024
 
 
@@ -71,66 +71,51 @@
     )(meta, *[a for a, _ in ins])
 
 
-def hidden_rows(acts, start, pieces, after=()):
-    _, _, tokens = acts.shape
-    rows = sum(pieces)
-    tile = math.gcd(*pieces)
-    starts = [sum(pieces[:p]) for p in range(len(pieces))]
-
-    def kernel(acts_ref, *refs):
-        refs = refs[len(after) :]
-        out_refs, (buf, sems) = refs[: len(pieces)], refs[len(pieces) :]
-
+def hidden_rows(acts):
+    _, rows, tokens = acts.shape
+    parts = 4
+    tile = rows // parts
+
+    def kernel(acts_ref, out_ref, buf, sems):
         def load(p):
-            there, here = pl.ds(start + starts[p], pieces[p]), pl.ds(starts[p], pieces[p])
-            return pltpu.make_async_copy(acts_ref.at[:, there, :], buf.at[:, here, :], sems.at[p])
-
-        for p in range(len(pieces)):
+            here = pl.ds(p * tile, tile)
+            return pltpu.make_async_copy(acts_ref.at[:, here, :], buf.at[:, here, :], sems.at[p])
+
+        for p in range(2):
             load(p).start()
-        for p, ref in enumerate(out_refs):
+        for p in range(parts):
             load(p).wait()
-            for at in range(0, pieces[p], tile // 4):
-                ref[pl.ds(at, tile // 4), :] = hidden_of(buf[:, pl.ds(starts[p] + at, tile // 4), :])
+            if p + 2 < parts:
+                load(p + 2).start()
+            for at in range(p * tile, (p + 1) * tile, tile // 2):
+                out_ref[pl.ds(at, tile // 2), :] = hidden_of(buf[:, pl.ds(at, tile // 2), :])
 
     array, spec = in_hbm(acts)
     return pl.pallas_call(
         kernel,
-        in_specs=[spec, *[anywhere(a)[1] for a in after]],
-        out_specs=[pl.BlockSpec(memory_space=pltpu.VMEM)] * len(pieces),
-        out_shape=[pltpu.VMEM((n, tokens), acts.dtype) for n in pieces],
-        scratch_shapes=[pltpu.VMEM((2, rows, tokens), acts.dtype), pltpu.SemaphoreType.DMA((len(pieces),))],
+        in_specs=[spec],
+        out_specs=pl.BlockSpec(memory_space=pltpu.VMEM),
+        out_shape=pltpu.VMEM((rows, tokens), acts.dtype),
+        scratch_shapes=[pltpu.VMEM(acts.shape, acts.dtype), pltpu.SemaphoreType.DMA((parts,))],
         compiler_params=pltpu.CompilerParams(vmem_limit_bytes=8 * MIB),
         cost_estimate=pl.CostEstimate(flops=1, bytes_accessed=1, transcendentals=0),
         name="hidden",
-    )(array, *after)
-
-
-class Slot:
-    def __init__(self, number, blocks, places):
-        self.number, self.blocks, self.places = number, blocks, places
-
-    def start(self, meta_ref, refs, target, sem):
-        for ref, places in zip(refs, self.places, strict=True):
-
-            @pl.when(functools.reduce(jnp.logical_or, [meta_ref[1] == z for z in places]))
-            def _():
-                pltpu.make_async_copy(ref, target, sem).start()
-
-    def wait(self, refs, target, sem):
-        pltpu.make_async_copy(refs[0], target, sem).wait()
-
-
-def fetch(slots, meta_ref, refs, targets, sems):
-    waits = []
-    for n, slot in enumerate(slots):
-        mine, refs = refs[: len(slot.blocks)], refs[len(slot.blocks) :]
-        slot.start(meta_ref, mine, targets[n], sems.at[n])
-        waits.append(functools.partial(slot.wait, mine, targets[n], sems.at[n]))
-    return lambda: [wait() for wait in waits]
-
-
-def blocks_of(slots):
-    return [anywhere(block) for slot in slots for block in slot.blocks]
+    )(array)
+
+
+def slot_rows(refs):
+    rows = refs[0][...]
+    for ref in refs[1:]:
+        rows = rows + ref[...]
+    return rows
+
+
+def split(slots, refs):
+    groups = []
+    for slot in slots:
+        groups.append(refs[: len(slot)])
+        refs = refs[len(slot) :]
+    return groups, refs
 
 
 def partials(meta, masks, weight, rows, tokens, dtypes, splits, slots=None, turned=None, adds=None, keep=True, after=(), weight_of=1):
@@ -139,7 +124,7 @@
     steps = rows // tile
     total = len(masks) * steps
     depth = 3
-    blocks = blocks_of(slots) if slots else [in_vmem(turned)]
+    blocks = [in_vmem(block) for slot in slots for block in slot] if slots else [in_vmem(turned)]
     each = tokens // len(slots) if slots else 0
     extra = [a for group in adds or [] for a in group]
     per = len(extra) // len(masks)
@@ -159,34 +144,24 @@
 
         @pl.when(k == 0)
         def _():
-            if slots:
-                rows_buf, sems = refs[-2:]
-                targets = [rows_buf.at[pl.ds(n * each, each), :] for n in range(len(slots))]
-                wait = fetch(slots, meta_ref, block_refs, targets, sems)
             if keep:
                 for step in range(depth - 1):
                     copy(step).start()
             if slots:
-                wait()
-                turned_ref[...] = rows_buf[...].T
-
-        if keep:
-            for step in range(total):
-
-                @pl.when(k == step)
-                def _():
+                for n, group in enumerate(split(slots, block_refs)[0]):
+                    turned_ref[:, n * each : (n + 1) * each] = slot_rows(group).T
+
+        for step in range(total):
+            j, i = step // steps, step % steps
+
+            @pl.when(k == step)
+            def _():
+                if keep:
                     if step + depth - 1 < total:
                         copy(step + depth - 1).start()
                     copy(step).wait()
-
-        w = kept_ref[pl.ds(pl.multiple_of(k * tile, tile), tile), :]
-        out = jnp.dot(w, turned_ref[...], preferred_element_type=jnp.float32)
-        for step in range(total):
-            j, i = step // steps, step % steps
-
-            @pl.when(k == step)
-            def _():
-                value = out
+                w = kept_ref[step * tile : (step + 1) * tile, :]
+                value = jnp.dot(w, turned_ref[...], preferred_element_type=jnp.float32)
                 if extra:
                     add_ref, at = add_refs[j * per + i * per // steps], i % (steps // per) * tile
                     value = value + add_ref[at : at + tile, :].astype(jnp.float32)
@@ -199,66 +174,50 @@
     scratch = []
     if slots:
         outs.append((pltpu.VMEM((feats, tokens), weight.dtype), in_place))
-        scratch = [pltpu.VMEM((tokens, feats), weight.dtype), pltpu.SemaphoreType.DMA((len(slots),))]
     if keep:
         outs.append((pltpu.VMEM((total * tile, feats), weight.dtype), in_place))
-        scratch = [pltpu.SemaphoreType.DMA((total,)), *scratch]
+        scratch = [pltpu.SemaphoreType.DMA((total,))]
     return call(kernel, "partials", meta, (total,), ins, outs, scratch, after=after, weight=weight_of, vmem=8)
 
 
 def turned_slots(meta, slots, each, feats, after=(), weight=1):
-    blocks = blocks_of(slots)
-    tokens = len(slots) * each
-
     def kernel(meta_ref, *refs):
-        block_refs, (out_ref, buf, sems) = refs[: len(blocks)], refs[len(blocks) :]
-        fetch(slots, meta_ref, block_refs, [buf.at[pl.ds(n * each, each), :] for n in range(len(slots))], sems)()
-        out_ref[...] = buf[...].T
-
-    outs = [(pltpu.VMEM((feats, tokens), jnp.bfloat16), pl.BlockSpec(memory_space=pltpu.VMEM))]
-    scratch = [pltpu.VMEM((tokens, feats), jnp.bfloat16), pltpu.SemaphoreType.DMA((len(slots),))]
-    return call(kernel, "turned", meta, (1,), blocks, outs, scratch, after=after, weight=weight, vmem=6)
+        groups, (out_ref,) = split(slots, refs)
+        for n, group in enumerate(groups):
+            out_ref[:, n * each : (n + 1) * each] = slot_rows(group).T
+
+    outs = [(pltpu.VMEM((feats, len(slots) * each), jnp.bfloat16), pl.BlockSpec(memory_space=pltpu.VMEM))]
+    ins = [in_vmem(block) for slot in slots for block in slot]
+    return call(kernel, "turned", meta, (1,), ins, outs, after=after, weight=weight, vmem=6)
 
 
 def all_slots(meta, slots, each, feats, after=()):
-    blocks = blocks_of(slots)
-
     def kernel(meta_ref, *refs):
-        block_refs, (out_ref, sems) = refs[: len(blocks)], refs[len(blocks) :]
-        starts = [pl.multiple_of(meta_ref[1 + slot.number] * each, each) for slot in slots]
-        fetch(slots, meta_ref, block_refs, [out_ref.at[pl.ds(at, each), :] for at in starts], sems)()
-
-    shape = pltpu.VMEM((len(slots) * each, feats), jnp.bfloat16)
-    outs = [(shape, pl.BlockSpec(memory_space=pltpu.VMEM))]
-    return call(kernel, "token_rows", meta, (1,), blocks, outs, [pltpu.SemaphoreType.DMA((len(slots),))], after=after, vmem=4)
-
-
-def weight_grad(meta, masks, hiddens, cots, out, total_rows, after=(), weight=1):
+        groups, (out_ref,) = split(slots, refs)
+        for n, group in enumerate(groups):
+            out_ref[pl.ds(pl.multiple_of(meta_ref[1 + n] * each, each), each), :] = slot_rows(group)
+
+    outs = [(pltpu.VMEM((len(slots) * each, feats), jnp.bfloat16), pl.BlockSpec(memory_space=pltpu.VMEM))]
+    ins = [in_vmem(block) for slot in slots for block in slot]
+    return call(kernel, "token_rows", meta, (1,), ins, outs, after=after, vmem=6)
+
+
+def weight_grad(meta, masks, hiddens, cots, total_rows, after=(), weight=1):
     tokens, feats = cots.shape
-    steps = len(hiddens[0])
-    tile = hiddens[0][0].shape[0]
-    flat = [p for pieces in hiddens for p in pieces]
+    rows = hiddens[0].shape[0]
+    steps = 2
+    tile = rows // steps
+    total = len(masks) * steps
 
     def kernel(meta_ref, cot_ref, *refs):
-        piece_refs, (out_ref, buf, sems) = refs[: len(flat)], refs[len(flat) :]
+        hidden_refs, (out_ref,) = refs[: len(masks)], refs[len(masks) :]
         k = pl.program_id(0)
-
-        def copy(step):
-            return pltpu.make_async_copy(piece_refs[step], buf.at[step % 2], sems.at[step % 2])
-
-        @pl.when(k == 0)
-        def _():
-            copy(0).start()
-
-        for step in range(len(flat)):
-
-            @pl.when(k == step)
+        for j, ref in enumerate(hidden_refs):
+
+            @pl.when(k // steps == j)
             def _():
-                copy(step).wait()
-                if step + 1 < len(flat):
-                    copy(step + 1).start()
-
-        out_ref[...] = jnp.dot(buf[lax.rem(k, 2)], cot_ref[...], preferred_element_type=jnp.float32).astype(out_ref.dtype)
+                h = ref[pl.ds(pl.multiple_of(lax.rem(k, steps) * tile, tile), tile), :]
+                out_ref[...] = jnp.dot(h, cot_ref[...], preferred_element_type=jnp.float32).astype(out_ref.dtype)
 
     def place(k, m):
         block = m[0] ^ masks[0]
@@ -267,11 +226,10 @@
         return block * steps + k % steps, 0
 
     return call(
-        kernel, "weight_grad", meta, (len(flat),),
-        [in_vmem(cots), *[anywhere(p) for p in flat]],
+        kernel, "weight_grad", meta, (total,),
+        [in_vmem(cots), *[in_vmem(h) for h in hiddens]],
         [(jax.ShapeDtypeStruct((total_rows, feats), cots.dtype), pl.BlockSpec((tile, feats), place))],
-        [pltpu.VMEM((2, tile, tokens), cots.dtype), pltpu.SemaphoreType.DMA((2,))],
-        alias=out, after=after, weight=weight, vmem=20,
+        after=after, weight=weight, vmem=20,
     )
 
 
@@ -339,44 +297,35 @@
     meta = describe(me, z)
     bf16, f32 = jnp.bfloat16, jnp.float32
 
-    hidden = hidden_rows(pre_acts, 0, (rows // 2,))
-    hidden = [*hidden, *hidden_rows(pre_acts, rows // 2, (rows // 2,), after=hidden)]
-    hidden[1], cotangent = lax.optimization_barrier((hidden[1], cotangent))
-    hidden_far = [across_x(h) for h in hidden]
-    hidden_core = [across_core(h) for h in hidden]
+    hidden = hidden_rows(pre_acts)
+    hidden_far, hidden_core = across_x(hidden), across_core(hidden)
 
     near, second = in_pairs(cotangent), in_middle(cotangent)
     third, outer = in_middle(near), outwards(second)
     third, outer = lax.optimization_barrier((third, outer))
     outmost = outwards(third)
-    slots = [
-        Slot(0, [cotangent], [(0, 1, 2, 3)]),
-        Slot(1, [near], [(0, 1, 2, 3)]),
-        Slot(2, [second, outer], [(1, 2), (0, 3)]),
-        Slot(3, [third, outmost], [(1, 2), (0, 3)]),
-    ]
+    slots = [[cotangent], [near], [second, outer], [third, outmost]]
 
     sums = functools.partial(partials, meta, rows=rows, tokens=tokens)
-    turned, done = turned_slots(meta, slots[:2], each, feats, after=(hidden_far[0],), weight=SHORT)
-    *sent, kept_sent, _ = sums(
-        (3, 1), down_weight, dtypes=(bf16, bf16), splits=2, turned=turned, after=(done, *hidden_core), weight_of=LONG
-    )
+    turned, _ = turned_slots(meta, slots[:2], each, feats, weight=TURNED)
+    *sent, kept_sent, _ = sums((3, 1), down_weight, dtypes=(bf16, bf16), splits=2, turned=turned)
     back = [across_core(p) for p in sent]
-    a_sum, kept_sum, done = sums((2,), down_weight, dtypes=(bf16,), splits=1, turned=turned, adds=(back[:2],))
+    a_sum, kept_sum, done = sums((2,), down_weight, dtypes=(bf16,), splits=1, turned=turned, adds=(back[:2],), after=(hidden_core,))
     a_far = across_x(a_sum)
-    a_own, kept_own, done = sums(
-        (0,), down_weight, dtypes=(f32,), splits=1, turned=turned, adds=(back[2:],), after=(done, hidden_far[1]), weight_of=MIDDLE
-    )
-
-    *sent, turned, done = sums((3, 1), kept_sent, dtypes=(bf16, bf16), splits=2, slots=slots[2:], keep=False, after=(done,))
+    a_own, kept_own, done = sums((0,), down_weight, dtypes=(f32,), splits=1, turned=turned, adds=(back[2:],), after=(done,))
+
+    *sent, turned, done = sums(
+        (3, 1), kept_sent, dtypes=(bf16, bf16), splits=2, slots=slots[2:], keep=False, after=(done,)
+    )
     back = [across_core(p) for p in sent]
     cots, done = all_slots(meta, slots, each, feats, after=(done,))
-    hidden_both = [across_core(h) for h in hidden_far]
+    hidden_far, done = lax.optimization_barrier((hidden_far, done))
+    hidden_both = across_core(hidden_far)
     b_sum, done = sums((2,), kept_sum, dtypes=(bf16,), splits=1, turned=turned, adds=(back[:2],), keep=False, after=(done,))
     b_far = across_x(b_sum)
-    done = wait_for(meta, (done, a_far), BRIEF)
+    done = wait_for(meta, (done, a_far), ARRIVED)
     grad_down, done = weight_grad(
-        meta, (0, 1, 2, 3), (hidden, hidden_core, hidden_far, hidden_both), cots, None, total_rows, after=(done,), weight=200 * 10**9
+        meta, (0, 1, 2, 3), (hidden, hidden_core, hidden_far, hidden_both), cots, total_rows, after=(done,), weight=200 * 10**9
     )
     grad_pre, _ = gate_grad(meta, pre_acts, (a_own, a_far), kept_own, turned, back[2:], b_far, after=(done,))
     return grad_pre, grad_down

time: 98.3 us -> 96.4 us (0.981)
  the two profiles are of different devices: /device:TPU:0 before, /device:TPU:10 now
where the time goes in v3:
time: 96.4 us; the launch traced here: 96.1 us
  Pallas kernels  61.8 us (64%)
  starting transfers between devices  19.7 us (20%)
  waiting for transfers between devices  13.3 us (14%)
    pallas_call x10, Pallas kernels, call(): pl.pallas_call(body, grid_spec=pltpu.PrefetchScalarGridSpec(num_scalar_pr...  58.9 us
    ppermute x2, waiting for transfers between devices, two_level(): near, second = (in_pairs(cotangent), in_middle(cotangent))  5.27 us
    ppermute x2, starting transfers between devices, two_level(): near, second = (in_pairs(cotangent), in_middle(cotangent))  5.11 us
    ppermute x2, starting transfers between devices, two_level(): third, outer = (in_middle(near), outwards(second))  4.8 us
    ppermute x1, starting transfers between devices, two_level(): outmost = outwards(third)  4.53 us
    ppermute x1, waiting for transfers between devices, two_level(): a_far = across_x(a_sum)  4.35 us
    ppermute x8, waiting for transfers between devices, two_level(): back = [across_core(p) for p in sent]  3.68 us
    pallas_call x1, Pallas kernels, hidden_rows(): pl.pallas_call(kernel, in_specs=[spec], out_specs=pl.BlockSpec(memory_spa...  2.89 us
  transfers between devices with their start and end apart: 18, of which 4 were waited for; matrix products, arithmetic and copies ran while one was open for 0% of the time, Pallas kernels for 56%

profile of v3, /device:TPU:10, one launch (start us, length us, event | category | flops | bytes accessed | tf_op | source)
XLA Modules:
  0.0 96.1 jit_solution(12841696921185660749)
XLA Ops:
  0.7 0.5 collective-permute-start
  1.2 4.6 %collective-permute-start.7 = (bf16[128,2048]{1,0:T(8,128)(2,1)}, bf16[128,2048]{1,0:T(8,128)(2,1)S(1)}, u32[]{:S(2)}, u32[]{:S(2)}) collective-permute-start(bf16[128,2048]{1,0:T(8,128)(2,1)} %refs_0_.10), channel_id=1, source_target_pairs={{4,8},{8,4},{5,9},{9,5},{6,10},{10,6},{7,11},{11,7},{20,24},{24,20... | collective-permute-start | bytes 1572872 | tf_op jit(solution)/shard_map/ppermute | solution.py:303
  5.8 2.9 %hidden.1.refs_1_ = bf16[1664,512]{1,0:T(8,128)(2,1)S(1)} custom-call(bf16[2,1664,512]{2,1,0:T(8,128)(2,1)} %refs_0_.11), custom_call_target="tpu_custom_call" | custom-call | flops 1 | bytes 1 | tf_op jit(solution)/shard_map/hidden/pallas_call | solution.py:94
  8.7 0.6 collective-permute-start.15
  9.4 5.3 %collective-permute-done.refs_1_ = bf16[128,2048]{1,0:T(8,128)(2,1)S(1)} collective-permute-done((bf16[128,2048]{1,0:T(8,128)(2,1)}, bf16[128,2048]{1,0:T(8,128)(2,1)S(1)}, u32[]{:S(2)}, u32[]{:S(2)}) %collective-permute-start) | collective-permute-done | bytes 524320 | tf_op jit(solution)/shard_map/ppermute | solution.py:303
  14.6 3.5 %collective-permute-start.8 = (bf16[128,2048]{1,0:T(8,128)(2,1)S(1)}, bf16[128,2048]{1,0:T(8,128)(2,1)S(1)}, u32[]{:S(2)}, u32[]{:S(2)}) collective-permute-start(bf16[128,2048]{1,0:T(8,128)(2,1)S(1)} %collective-permute-done.refs_1_), channel_id=1, source_target_pairs={{4,8},{8,4},{5,9},{9,5},{6,10},{10,6},{7,11},{11,7},{20,24},{24,20... | collective-permute-start | bytes 1572872 | tf_op jit(solution)/shard_map/ppermute | solution.py:304
  18.1 1.3 %collective-permute-start.9 = (bf16[128,2048]{1,0:T(8,128)(2,1)S(1)}, bf16[128,2048]{1,0:T(8,128)(2,1)S(1)}, u32[]{:S(2)}, u32[]{:S(2)}) collective-permute-start(bf16[128,2048]{1,0:T(8,128)(2,1)S(1)} %collective-permute-done.7.refs_1_.refs_2_), channel_id=1, source_target_pairs={{4,0},{8,12},{5,1},{9,13},{6,2},{10,14},{7,3},{11,15},{20,16},{24,... | collective-permute-start | bytes 1572872 | tf_op jit(solution)/shard_map/ppermute | solution.py:304
  19.5 1.4 %turned.1 = (bf16[2048,256]{1,0:T(8,128)(2,1)S(1)}, f32[8,128]{1,0:T(8,128)}) custom-call(s32[5]{0:T(128)S(1)} %fusion.meta_ref, bf16[128,2048]{1,0:T(8,128)(2,1)S(1)} %copy-done.5, bf16[128,2048]{1,0:T(8,128)(2,1)S(1)} %collective-permute-done.refs_1_), custom_call_target="tpu_custom_call" | custom-call | flops 7000000000 | bytes 1 | tf_op jit(solution)/shard_map/turned/pallas_call | solution.py:61
  20.9 8.4 %partials.5 = (bf16[832,256]{1,0:T(8,128)(2,1)S(1)}, bf16[832,256]{1,0:T(8,128)(2,1)S(1)}, bf16[832,256]{1,0:T(8,128)(2,1)S(1)}, bf16[832,256]{1,0:T(8,128)(2,1)...) custom-call(s32[5]{0:T(128)S(1)} %fusion.meta_ref, bf16[6656,2048]{1,0:T(8,128)(2,1)} %refs_0_.9, ...), custom_call_target="tpu_custom_call" | custom-call | flops 1 | bytes 1 | tf_op jit(solution)/shard_map/partials/pallas_call | solution.py:61
  29.3 0.1 collective-permute-start.3
  29.4 0.5 collective-permute-start.4
  29.9 4.5 %collective-permute-start.10 = (bf16[128,2048]{1,0:T(8,128)(2,1)S(1)}, bf16[128,2048]{1,0:T(8,128)(2,1)S(1)}, u32[]{:S(2)}, u32[]{:S(2)}) collective-permute-start(bf16[128,2048]{1,0:T(8,128)(2,1)S(1)} %collective-permute-done.8.refs_3_.refs_4_), channel_id=1, source_target_pairs={{4,0},{8,12},{5,1},{9,13},{6,2},{10,14},{7,3},{11,15},{20,16},{24,... | collective-permute-start | bytes 1572872 | tf_op jit(solution)/shard_map/ppermute | solution.py:306
  34.4 0.1 collective-permute-start.1
  34.5 0.5 collective-permute-start.2
  35.0 4.9 %partials.6 = (bf16[1664,256]{1,0:T(8,128)(2,1)S(1)}, bf16[1664,2048]{1,0:T(8,128)(2,1)S(1)}, f32[8,128]{1,0:T(8,128)S(1)}) custom-call(s32[5]{0:T(128)S(1)} %fusion.meta_ref, bf16[6656,2048]{1,0:T(8,128)(2,1)} %refs_0_.9, bf16[2048,256]{1,0:T(8,128)(2,1)S(1)} %get-tuple-element.31.refs_1_, bf16[832,256]{1,0:T(8,128)(2,1)S(1)} %collective-permute-done.3.refs_2_, ...), custom_call_target="tpu_custom_call" | custom-call | flops 1 | bytes 1 | tf_op jit(solution)/shard_map/partials/pallas_call | solution.py:61
  39.9 0.6 collective-permute-start.6
  40.5 4.9 %partials.7 = (f32[1664,256]{1,0:T(8,128)S(1)}, bf16[1664,2048]{1,0:T(8,128)(2,1)S(1)}, f32[8,128]{1,0:T(8,128)S(1)}) custom-call(s32[5]{0:T(128)S(1)} %fusion.meta_ref, bf16[6656,2048]{1,0:T(8,128)(2,1)} %refs_0_.9, bf16[2048,256]{1,0:T(8,128)(2,1)S(1)} %get-tuple-element.31.refs_1_, bf16[832,256]{1,0:T(8,128)(2,1)S(1)} %collective-permute-done.1.refs_2_, ...), custom_call_target="tpu_custom_call" | custom-call | flops 1 | bytes 1 | tf_op jit(solution)/shard_map/partials/pallas_call | solution.py:61
  45.4 6.0 %partials.8 = (bf16[832,256]{1,0:T(8,128)(2,1)S(1)}, bf16[832,256]{1,0:T(8,128)(2,1)S(1)}, bf16[832,256]{1,0:T(8,128)(2,1)}, bf16[832,256]{1,0:T(8,128)(2,1)}, b...) custom-call(s32[5]{0:T(128)S(1)} %fusion.meta_ref, bf16[3328,2048]{1,0:T(8,128)(2,1)S(1)} %get-tuple-element.40.refs_0_, ...), custom_call_target="tpu_custom_call" | custom-call | flops 1 | bytes 1 | tf_op jit(solution)/shard_map/partials/pallas_call | solution.py:61
  51.4 0.7 token_rows.1
  52.2 0.5 collective-permute-start.13
  52.7 0.1 collective-permute-start.14
  52.8 0.4 collective-permute-start.11
  53.2 3.4 %collective-permute-done.13.refs_2_ = bf16[832,256]{1,0:T(8,128)(2,1)S(1)} collective-permute-done((bf16[832,256]{1,0:T(8,128)(2,1)S(1)}, bf16[832,256]{1,0:T(8,128)(2,1)S(1)}, u32[]{:S(2)}, u32[]{:S(2)}) %collective-permute-start.13) | collective-permute-done | bytes 426016 | tf_op jit(solution)/shard_map/ppermute | solution.py:320
  56.6 0.4 collective-permute-start.12
  57.0 0.2 collective-permute-done.14.refs_3_
  57.3 3.6 %partials.9 = (bf16[1664,256]{1,0:T(8,128)(2,1)}, f32[8,128]{1,0:T(8,128)S(1)}) custom-call(s32[5]{0:T(128)S(1)} %fusion.meta_ref, bf16[1664,2048]{1,0:T(8,128)(2,1)S(1)} %get-tuple-element.47.refs_0_, bf16[2048,256]{1,0:T(8,128)(2,1)S(1)} %get-tuple-element.44.refs_1_.refs_4_, bf16[832,256]{1,0:T(8,128)(2,1)S(1)} %collective-permute-done.13.refs_2_, ...), custom_call_target="tpu_custom_call" | custom-call | flops 1 | bytes 1 | tf_op jit(solution)/shard_map/partials/pallas_call | solution.py:61
  60.9 1.5 %collective-permute-start.16 = (bf16[1664,256]{1,0:T(8,128)(2,1)}, bf16[1664,256]{1,0:T(8,128)(2,1)}, u32[]{:S(2)}, u32[]{:S(2)}) collective-permute-start(bf16[1664,256]{1,0:T(8,128)(2,1)} %get-tuple-element.53), channel_id=1, source_target_pairs={{0,2},{1,3},{2,0},{3,1},{4,6},{5,7},{6,4},{7,5},{8,10},{9,11},{10,... | collective-permute-start | bytes 2555912 | tf_op jit(solution)/shard_map/ppermute | solution.py:325
  62.4 4.3 %collective-permute-done.6.refs_1_.refs_2_ = bf16[1664,256]{1,0:T(8,128)(2,1)S(1)} collective-permute-done((bf16[1664,256]{1,0:T(8,128)(2,1)S(1)}, bf16[1664,256]{1,0:T(8,128)(2,1)S(1)}, u32[]{:S(2)}, u32[]{:S(2)}) %collective-permute-start.6) | collective-permute-done | bytes 852000 | tf_op jit(solution)/shard_map/ppermute | solution.py:314
  66.7 0.5 arrived.1.refs_5_
  67.3 0.4 copy-done.3
  67.7 20.9 %weight_grad.1 = (bf16[6656,2048]{1,0:T(8,128)(2,1)}, f32[8,128]{1,0:T(8,128)S(1)}) custom-call(s32[5]{0:T(128)S(1)} %fusion.meta_ref, bf16[512,2048]{1,0:T(8,128)(2,1)S(1)} %get-tuple-element.54.refs_0_, bf16[1664,512]{1,0:T(8,128)(2,1)S(1)} %hidden.1.refs_1_, bf16[1664,512]{1,0:T(8,128)(2,1)} %collective-permute-done.5.refs_4_.refs_2_, ...), custom_call_target="tpu_custom_call" | custom-call | flops 199999995904 | bytes 1 | tf_op jit(solution)/shard_map/weight_grad/pallas_call | solution.py:61
  88.6 7.5 %gate_grad.1 = (bf16[2,1664,512]{2,1,0:T(8,128)(2,1)}, f32[8,128]{1,0:T(8,128)}) custom-call(s32[5]{0:T(128)S(1)} %fusion.meta_ref, bf16[2,1664,512]{2,1,0:T(8,128)(2,1)S(1)} %copy-done, f32[1664,256]{1,0:T(8,128)S(1)} %get-tuple-element.37.refs_1_, bf16[1664,256]{1,0:T(8,128)(2,1)S(1)} %copy-done.4, bf16[1664,2048]{1,0:T(8,128)(2,1)S(1)} %get-tuple-element.39.refs_3_, ...), custom_call_target="tpu_custom_call" | custom-call | flops 1 | bytes 1 | tf_op jit(solution)/shard_map/gate_grad/pallas_call | solution.py:61
  (38 shorter events, 0.2 us)
Async XLA Ops:
  0.6 8.7 %copy-start.6 = (s32[5]{0:T(128)S(1)}, s32[5]{0:T(128)}, u32[]{:S(2)}) copy-start(s32[5]{0:T(128)} %constant.27.clone) | copy-start | bytes 64
  0.6 8.7 %copy-start.7 = (s32[5]{0:T(128)S(1)}, s32[5]{0:T(128)}, u32[]{:S(2)}) copy-start(s32[5]{0:T(128)} %constant.26.clone) | copy-start | bytes 64
  0.7 8.7 %copy-start.8 = (s32[5]{0:T(128)S(1)}, s32[5]{0:T(128)}, u32[]{:S(2)}) copy-start(s32[5]{0:T(128)} %constant.25.clone) | copy-start | bytes 64
  0.7 8.7 %copy-start.9 = (s32[5]{0:T(128)S(1)}, s32[5]{0:T(128)}, u32[]{:S(2)}) copy-start(s32[5]{0:T(128)} %constant.24.clone) | copy-start | bytes 64
  0.7 8.7 %copy-start.10 = (s32[5]{0:T(128)S(1)}, s32[5]{0:T(128)}, u32[]{:S(2)}) copy-start(s32[5]{0:T(128)} %constant.23.clone) | copy-start | bytes 64
  0.7 18.8 %copy-start.5 = (bf16[128,2048]{1,0:T(8,128)(2,1)S(1)}, bf16[128,2048]{1,0:T(8,128)(2,1)}, u32[]{:S(2)}) copy-start(bf16[128,2048]{1,0:T(8,128)(2,1)} %refs_0_.10) | copy-start | bytes 1572868
  0.7 13.9 %collective-permute-start = (bf16[128,2048]{1,0:T(8,128)(2,1)}, bf16[128,2048]{1,0:T(8,128)(2,1)S(1)}, u32[]{:S(2)}, u32[]{:S(2)}) collective-permute-start(bf16[128,2048]{1,0:T(8,128)(2,1)} %refs_0_.10), channel_id=1, source_target_pairs={{0,4},{4,0},{8,12},{12,8},{1,5},{5,1},{9,13},{13,9},{2,6},{6,2},{1... | collective-permute-start | bytes 1572872 | tf_op jit(solution)/shard_map/ppermute | solution.py:303
  1.2 16.9 %collective-permute-start.7 = (bf16[128,2048]{1,0:T(8,128)(2,1)}, bf16[128,2048]{1,0:T(8,128)(2,1)S(1)}, u32[]{:S(2)}, u32[]{:S(2)}) collective-permute-start(bf16[128,2048]{1,0:T(8,128)(2,1)} %refs_0_.10), channel_id=1, source_target_pairs={{4,8},{8,4},{5,9},{9,5},{6,10},{10,6},{7,11},{11,7},{20,24},{24,20... | collective-permute-start | bytes 1572872 | tf_op jit(solution)/shard_map/ppermute | solution.py:303
  8.7 43.4 %collective-permute-start.15 = (bf16[1664,512]{1,0:T(8,128)(2,1)S(1)}, bf16[1664,512]{1,0:T(8,128)(2,1)}, u32[]{:S(2)}, u32[]{:S(2)}) collective-permute-start(bf16[1664,512]{1,0:T(8,128)(2,1)S(1)} %hidden.1.refs_1_), channel_id=1, source_target_pairs={{0,2},{1,3},{2,0},{3,1},{4,6},{5,7},{6,4},{7,5},{8,10},{9,11},{10,... | collective-permute-start | bytes 5111816 | tf_op jit(solution)/shard_map/ppermute | solution.py:301
  9.3 25.7 %collective-permute-start.5 = (bf16[1664,512]{1,0:T(8,128)(2,1)S(1)}, bf16[1664,512]{1,0:T(8,128)(2,1)}, u32[]{:S(2)}, u32[]{:S(2)}) collective-permute-start(bf16[1664,512]{1,0:T(8,128)(2,1)S(1)} %hidden.1.refs_1_), channel_id=1, source_target_pairs={{0,1},{1,0},{2,3},{3,2},{4,5},{5,4},{6,7},{7,6},{8,9},{9,8},{10,11... | collective-permute-start | bytes 5111816 | tf_op jit(solution)/shard_map/ppermute | solution.py:301
  14.6 14.8 %collective-permute-start.8 = (bf16[128,2048]{1,0:T(8,128)(2,1)S(1)}, bf16[128,2048]{1,0:T(8,128)(2,1)S(1)}, u32[]{:S(2)}, u32[]{:S(2)}) collective-permute-start(bf16[128,2048]{1,0:T(8,128)(2,1)S(1)} %collective-permute-done.refs_1_), channel_id=1, source_target_pairs={{4,8},{8,4},{5,9},{9,5},{6,10},{10,6},{7,11},{11,7},{20,24},{24,20... | collective-permute-start | bytes 1572872 | tf_op jit(solution)/shard_map/ppermute | solution.py:304
  18.1 11.8 %collective-permute-start.9 = (bf16[128,2048]{1,0:T(8,128)(2,1)S(1)}, bf16[128,2048]{1,0:T(8,128)(2,1)S(1)}, u32[]{:S(2)}, u32[]{:S(2)}) collective-permute-start(bf16[128,2048]{1,0:T(8,128)(2,1)S(1)} %collective-permute-done.7.refs_1_.refs_2_), channel_id=1, source_target_pairs={{4,0},{8,12},{5,1},{9,13},{6,2},{10,14},{7,3},{11,15},{20,16},{24,... | collective-permute-start | bytes 1572872 | tf_op jit(solution)/shard_map/ppermute | solution.py:304
  29.3 5.1 %collective-permute-start.3 = (bf16[832,256]{1,0:T(8,128)(2,1)S(1)}, bf16[832,256]{1,0:T(8,128)(2,1)S(1)}, u32[]{:S(2)}, u32[]{:S(2)}) collective-permute-start(bf16[832,256]{1,0:T(8,128)(2,1)S(1)} %get-tuple-element.34), channel_id=1, source_target_pairs={{0,1},{1,0},{2,3},{3,2},{4,5},{5,4},{6,7},{7,6},{8,9},{9,8},{10,11... | collective-permute-start | bytes 1277960 | tf_op jit(solution)/shard_map/ppermute | solution.py:312
  29.4 5.1 %collective-permute-start.4 = (bf16[832,256]{1,0:T(8,128)(2,1)S(1)}, bf16[832,256]{1,0:T(8,128)(2,1)S(1)}, u32[]{:S(2)}, u32[]{:S(2)}) collective-permute-start(bf16[832,256]{1,0:T(8,128)(2,1)S(1)} %get-tuple-element.35), channel_id=1, source_target_pairs={{0,1},{1,0},{2,3},{3,2},{4,5},{5,4},{6,7},{7,6},{8,9},{9,8},{10,11... | collective-permute-start | bytes 1277960 | tf_op jit(solution)/shard_map/ppermute | solution.py:312
  29.9 15.5 %collective-permute-start.10 = (bf16[128,2048]{1,0:T(8,128)(2,1)S(1)}, bf16[128,2048]{1,0:T(8,128)(2,1)S(1)}, u32[]{:S(2)}, u32[]{:S(2)}) collective-permute-start(bf16[128,2048]{1,0:T(8,128)(2,1)S(1)} %collective-permute-done.8.refs_3_.refs_4_), channel_id=1, source_target_pairs={{4,0},{8,12},{5,1},{9,13},{6,2},{10,14},{7,3},{11,15},{20,16},{24,... | collective-permute-start | bytes 1572872 | tf_op jit(solution)/shard_map/ppermute | solution.py:306
  34.4 6.1 %collective-permute-start.1 = (bf16[832,256]{1,0:T(8,128)(2,1)S(1)}, bf16[832,256]{1,0:T(8,128)(2,1)S(1)}, u32[]{:S(2)}, u32[]{:S(2)}) collective-permute-start(bf16[832,256]{1,0:T(8,128)(2,1)S(1)} %get-tuple-element.32), channel_id=1, source_target_pairs={{0,1},{1,0},{2,3},{3,2},{4,5},{5,4},{6,7},{7,6},{8,9},{9,8},{10,11... | collective-permute-start | bytes 1277960 | tf_op jit(solution)/shard_map/ppermute | solution.py:312
  34.5 6.0 %collective-permute-start.2 = (bf16[832,256]{1,0:T(8,128)(2,1)S(1)}, bf16[832,256]{1,0:T(8,128)(2,1)S(1)}, u32[]{:S(2)}, u32[]{:S(2)}) collective-permute-start(bf16[832,256]{1,0:T(8,128)(2,1)S(1)} %get-tuple-element.33), channel_id=1, source_target_pairs={{0,1},{1,0},{2,3},{3,2},{4,5},{5,4},{6,7},{7,6},{8,9},{9,8},{10,11... | collective-permute-start | bytes 1277960 | tf_op jit(solution)/shard_map/ppermute | solution.py:312
  39.9 26.8 %collective-permute-start.6 = (bf16[1664,256]{1,0:T(8,128)(2,1)S(1)}, bf16[1664,256]{1,0:T(8,128)(2,1)S(1)}, u32[]{:S(2)}, u32[]{:S(2)}) collective-permute-start(bf16[1664,256]{1,0:T(8,128)(2,1)S(1)} %get-tuple-element.38), channel_id=1, source_target_pairs={{0,2},{1,3},{2,0},{3,1},{4,6},{5,7},{6,4},{7,5},{8,10},{9,11},{10,... | collective-permute-start | bytes 2555912 | tf_op jit(solution)/shard_map/ppermute | solution.py:314
  51.4 9.5 %copy-start.1 = (bf16[2048,256]{1,0:T(8,128)(2,1)}, bf16[2048,256]{1,0:T(8,128)(2,1)S(1)}, u32[]{:S(2)}) copy-start(bf16[2048,256]{1,0:T(8,128)(2,1)S(1)} %get-tuple-element.44.refs_1_.refs_4_) | copy-start | bytes 3145732
  52.1 15.5 %collective-permute-start.17 = (bf16[1664,512]{1,0:T(8,128)(2,1)}, bf16[1664,512]{1,0:T(8,128)(2,1)S(1)}, u32[]{:S(2)}, u32[]{:S(2)}) collective-permute-start(bf16[1664,512]{1,0:T(8,128)(2,1)} %collective-permute-done.15.refs_3_), channel_id=1, source_target_pairs={{0,1},{1,0},{2,3},{3,2},{4,5},{5,4},{6,7},{7,6},{8,9},{9,8},{10,11... | collective-permute-start | bytes 5111816 | tf_op jit(solution)/shard_map/ppermute | solution.py:323
  52.2 4.4 %collective-permute-start.13 = (bf16[832,256]{1,0:T(8,128)(2,1)S(1)}, bf16[832,256]{1,0:T(8,128)(2,1)S(1)}, u32[]{:S(2)}, u32[]{:S(2)}) collective-permute-start(bf16[832,256]{1,0:T(8,128)(2,1)S(1)} %get-tuple-element.48), channel_id=1, source_target_pairs={{0,1},{1,0},{2,3},{3,2},{4,5},{5,4},{6,7},{7,6},{8,9},{9,8},{10,11... | collective-permute-start | bytes 1277960 | tf_op jit(solution)/shard_map/ppermute | solution.py:320
  52.7 4.5 %collective-permute-start.14 = (bf16[832,256]{1,0:T(8,128)(2,1)S(1)}, bf16[832,256]{1,0:T(8,128)(2,1)S(1)}, u32[]{:S(2)}, u32[]{:S(2)}) collective-permute-start(bf16[832,256]{1,0:T(8,128)(2,1)S(1)} %get-tuple-element.49), channel_id=1, source_target_pairs={{0,1},{1,0},{2,3},{3,2},{4,5},{5,4},{6,7},{7,6},{8,9},{9,8},{10,11... | collective-permute-start | bytes 1277960 | tf_op jit(solution)/shard_map/ppermute | solution.py:320
  52.8 35.8 %collective-permute-start.11 = (bf16[832,256]{1,0:T(8,128)(2,1)}, bf16[832,256]{1,0:T(8,128)(2,1)}, u32[]{:S(2)}, u32[]{:S(2)}) collective-permute-start(bf16[832,256]{1,0:T(8,128)(2,1)} %get-tuple-element.45), channel_id=1, source_target_pairs={{0,1},{1,0},{2,3},{3,2},{4,5},{5,4},{6,7},{7,6},{8,9},{9,8},{10,11... | collective-permute-start | bytes 1277960 | tf_op jit(solution)/shard_map/ppermute | solution.py:320
  56.6 32.0 %collective-permute-start.12 = (bf16[832,256]{1,0:T(8,128)(2,1)}, bf16[832,256]{1,0:T(8,128)(2,1)}, u32[]{:S(2)}, u32[]{:S(2)}) collective-permute-start(bf16[832,256]{1,0:T(8,128)(2,1)} %get-tuple-element.46), channel_id=1, source_target_pairs={{0,1},{1,0},{2,3},{3,2},{4,5},{5,4},{6,7},{7,6},{8,9},{9,8},{10,11... | collective-permute-start | bytes 1277960 | tf_op jit(solution)/shard_map/ppermute | solution.py:320
  60.9 27.7 %collective-permute-start.16 = (bf16[1664,256]{1,0:T(8,128)(2,1)}, bf16[1664,256]{1,0:T(8,128)(2,1)}, u32[]{:S(2)}, u32[]{:S(2)}) collective-permute-start(bf16[1664,256]{1,0:T(8,128)(2,1)} %get-tuple-element.53), channel_id=1, source_target_pairs={{0,2},{1,3},{2,0},{3,1},{4,6},{5,7},{6,4},{7,5},{8,10},{9,11},{10,... | collective-permute-start | bytes 2555912 | tf_op jit(solution)/shard_map/ppermute | solution.py:325
  66.7 0.9 copy-start.3
  67.6 21.0 %copy-start = (bf16[2,1664,512]{2,1,0:T(8,128)(2,1)S(1)}, bf16[2,1664,512]{2,1,0:T(8,128)(2,1)}, u32[]{:S(2)}) copy-start(bf16[2,1664,512]{2,1,0:T(8,128)(2,1)} %refs_0_.11) | copy-start | bytes 10223620
  67.6 21.0 %copy-start.2 = (bf16[2048,256]{1,0:T(8,128)(2,1)S(1)}, bf16[2048,256]{1,0:T(8,128)(2,1)}, u32[]{:S(2)}) copy-start(bf16[2048,256]{1,0:T(8,128)(2,1)} %copy-done.1) | copy-start | bytes 3145732
  67.7 21.0 %copy-start.4 = (bf16[1664,256]{1,0:T(8,128)(2,1)S(1)}, bf16[1664,256]{1,0:T(8,128)(2,1)}, u32[]{:S(2)}) copy-start(bf16[1664,256]{1,0:T(8,128)(2,1)} %copy-done.3) | copy-start | bytes 2555908

commit v4 on v3

--- a/solution.py
+++ b/solution.py
@@ -77,16 +77,16 @@
     tile = rows // parts
 
     def kernel(acts_ref, out_ref, buf, sems):
-        def load(p):
+        def loads(p):
             here = pl.ds(p * tile, tile)
-            return pltpu.make_async_copy(acts_ref.at[:, here, :], buf.at[:, here, :], sems.at[p])
-
-        for p in range(2):
-            load(p).start()
+            return [pltpu.make_async_copy(acts_ref.at[n, here, :], buf.at[n, here, :], sems.at[p, n]) for n in range(2)]
+
         for p in range(parts):
-            load(p).wait()
-            if p + 2 < parts:
-                load(p + 2).start()
+            for load in loads(p):
+                load.start()
+        for p in range(parts):
+            for load in loads(p):
+                load.wait()
             for at in range(p * tile, (p + 1) * tile, tile // 2):
                 out_ref[pl.ds(at, tile // 2), :] = hidden_of(buf[:, pl.ds(at, tile // 2), :])
 
@@ -96,7 +96,7 @@
         in_specs=[spec],
         out_specs=pl.BlockSpec(memory_space=pltpu.VMEM),
         out_shape=pltpu.VMEM((rows, tokens), acts.dtype),
-        scratch_shapes=[pltpu.VMEM(acts.shape, acts.dtype), pltpu.SemaphoreType.DMA((parts,))],
+        scratch_shapes=[pltpu.VMEM(acts.shape, acts.dtype), pltpu.SemaphoreType.DMA((parts, 2))],
         compiler_params=pltpu.CompilerParams(vmem_limit_bytes=8 * MIB),
         cost_estimate=pl.CostEstimate(flops=1, bytes_accessed=1, transcendentals=0),
         name="hidden",
@@ -127,12 +127,18 @@
     blocks = [in_vmem(block) for slot in slots for block in slot] if slots else [in_vmem(turned)]
     each = tokens // len(slots) if slots else 0
     extra = [a for group in adds or [] for a in group]
-    per = len(extra) // len(masks)
+
+    def overlaps(low, count):
+        size = rows // count
+        for p in range(count):
+            first, last = max(low, p * size), min(low + tile, (p + 1) * size)
+            if first < last:
+                yield p, slice(first - p * size, last - p * size), slice(first - low, last - low)
 
     def kernel(meta_ref, w_ref, *refs):
         block_refs, refs = refs[: len(blocks)], refs[len(blocks) :]
         add_refs, refs = refs[: len(extra)], refs[len(extra) :]
-        out_refs, refs = refs[: len(masks) * splits], list(refs[len(masks) * splits :])
+        out_refs, refs = refs[: sum(splits)], list(refs[sum(splits) :])
         turned_ref = refs.pop(0) if slots else block_refs[0]
         kept_ref = refs.pop(0) if keep else w_ref
         k = pl.program_id(0)
@@ -163,14 +169,15 @@
                 w = kept_ref[step * tile : (step + 1) * tile, :]
                 value = jnp.dot(w, turned_ref[...], preferred_element_type=jnp.float32)
                 if extra:
-                    add_ref, at = add_refs[j * per + i * per // steps], i % (steps // per) * tile
-                    value = value + add_ref[at : at + tile, :].astype(jnp.float32)
-                at = i % (steps // splits) * tile
-                out_refs[j * splits + i * splits // steps][at : at + tile, :] = value.astype(dtypes[j])
+                    base = sum(len(group) for group in adds[:j])
+                    added = [add_refs[base + p][there, :] for p, there, _ in overlaps(i * tile, len(adds[j]))]
+                    value = value + jnp.concatenate(added).astype(jnp.float32)
+                for p, there, here in overlaps(i * tile, splits[j]):
+                    out_refs[sum(splits[:j]) + p][there, :] = value[here, :].astype(dtypes[j])
 
     in_place = pl.BlockSpec(memory_space=pltpu.VMEM)
     ins = [in_hbm(weight) if keep else in_vmem(weight), *blocks, *[in_vmem(piece) for piece in extra]]
-    outs = [(pltpu.VMEM((rows // splits, tokens), dtype), in_place) for dtype in dtypes for _ in range(splits)]
+    outs = [(pltpu.VMEM((rows // n, tokens), dtype), in_place) for dtype, n in zip(dtypes, splits, strict=True) for _ in range(n)]
     scratch = []
     if slots:
         outs.append((pltpu.VMEM((feats, tokens), weight.dtype), in_place))
@@ -233,39 +240,29 @@
     )
 
 
-def gate_grad(meta, acts, early, weight, turned, back, far, after=()):
+def gate_grad(meta, acts, early, late, after=()):
     _, rows, tokens = acts.shape
-    feats, half = turned.shape
+    half = tokens // 2
     tile = rows // 4
-    per = len(back)
-
-    def kernel(meta_ref, acts_ref, mine_ref, theirs_ref, w_ref, turned_ref, *refs):
-        back_refs, far_ref, out_ref = refs[:per], refs[per], refs[per + 1]
-        i = pl.program_id(0)
-        here = pl.ds(pl.multiple_of(i * tile, tile), tile)
-        late = jnp.dot(w_ref[here, :], turned_ref[...], preferred_element_type=jnp.float32)
-        late = late + far_ref[here, :].astype(jnp.float32)
-        there = pl.ds(pl.multiple_of(i % (4 // per) * tile, tile), tile)
-        added = back_refs[0][there, :]
-        for p in range(1, per):
-            added = jnp.where(i * per // 4 == p, back_refs[p][there, :], added)
-        late = late + added.astype(jnp.float32)
+
+    def kernel(meta_ref, acts_ref, *refs):
+        pairs, out_ref = (refs[:2], refs[2:4]), refs[4]
+        here = pl.ds(pl.multiple_of(pl.program_id(0) * tile, tile), tile)
         for slot in range(tokens // LANES):
+            mine_ref, theirs_ref = pairs[slot * LANES // half]
             lanes = slice(slot * LANES % half, slot * LANES % half + LANES)
-            if slot * LANES < half:
-                grad = mine_ref[here, lanes] + theirs_ref[here, lanes].astype(jnp.float32)
-            else:
-                grad = late[:, lanes]
             columns = pl.ds(pl.multiple_of(meta_ref[1 + slot] * LANES, LANES), LANES)
+            grad = mine_ref[here, lanes] + theirs_ref[here, lanes].astype(jnp.float32)
             gate = acts_ref[0, here, columns].astype(jnp.float32)
             upper = acts_ref[1, here, columns].astype(jnp.float32)
             sigm = sigmoid(gate)
-            out_ref[0, :, columns] = (grad * upper * sigm * (1.0 + gate * (1.0 - sigm))).astype(out_ref.dtype)
-            out_ref[1, :, columns] = (grad * (gate * sigm)).astype(out_ref.dtype)
-
-    ins = [in_vmem(a) for a in (acts, *early, weight, turned, *back, far)]
+            active = gate * sigm
+            out_ref[0, :, columns] = (grad * upper * (sigm + active * (1.0 - sigm))).astype(out_ref.dtype)
+            out_ref[1, :, columns] = (grad * active).astype(out_ref.dtype)
+
+    ins = [in_vmem(a) for a in (acts, *early, *late)]
     outs = [(jax.ShapeDtypeStruct(acts.shape, acts.dtype), pl.BlockSpec((2, tile, tokens), lambda i, m: (0, i, 0)))]
-    return call(kernel, "gate_grad", meta, (4,), ins, outs, after=after, vmem=12)
+    return call(kernel, "gate_grad", meta, (4,), ins, outs, after=after, vmem=8)
 
 
 def wait_for(meta, after, weight):
@@ -308,26 +305,27 @@
 
     sums = functools.partial(partials, meta, rows=rows, tokens=tokens)
     turned, _ = turned_slots(meta, slots[:2], each, feats, weight=TURNED)
-    *sent, kept_sent, _ = sums((3, 1), down_weight, dtypes=(bf16, bf16), splits=2, turned=turned)
+    *sent, kept_sent, _ = sums((3, 1), down_weight, dtypes=(bf16, bf16), splits=(2, 2), turned=turned)
     back = [across_core(p) for p in sent]
-    a_sum, kept_sum, done = sums((2,), down_weight, dtypes=(bf16,), splits=1, turned=turned, adds=(back[:2],), after=(hidden_core,))
+    a_sum, kept_sum, done = sums((2,), down_weight, dtypes=(bf16,), splits=(1,), turned=turned, adds=(back[:2],), after=(hidden_core,))
     a_far = across_x(a_sum)
-    a_own, kept_own, done = sums((0,), down_weight, dtypes=(f32,), splits=1, turned=turned, adds=(back[2:],), after=(done,))
+    a_own, kept_own, done = sums((0,), down_weight, dtypes=(f32,), splits=(1,), turned=turned, adds=(back[2:],), after=(done,))
 
     *sent, turned, done = sums(
-        (3, 1), kept_sent, dtypes=(bf16, bf16), splits=2, slots=slots[2:], keep=False, after=(done,)
+        (3, 1), kept_sent, dtypes=(bf16, bf16), splits=(2, 4), slots=slots[2:], keep=False, after=(done,)
     )
     back = [across_core(p) for p in sent]
     cots, done = all_slots(meta, slots, each, feats, after=(done,))
     hidden_far, done = lax.optimization_barrier((hidden_far, done))
     hidden_both = across_core(hidden_far)
-    b_sum, done = sums((2,), kept_sum, dtypes=(bf16,), splits=1, turned=turned, adds=(back[:2],), keep=False, after=(done,))
+    b_sum, done = sums((2,), kept_sum, dtypes=(bf16,), splits=(1,), turned=turned, adds=(back[:2],), keep=False, after=(done,))
     b_far = across_x(b_sum)
+    b_own, done = sums((0,), kept_own, dtypes=(f32,), splits=(1,), turned=turned, adds=(back[2:],), keep=False, after=(done,))
     done = wait_for(meta, (done, a_far), ARRIVED)
     grad_down, done = weight_grad(
         meta, (0, 1, 2, 3), (hidden, hidden_core, hidden_far, hidden_both), cots, total_rows, after=(done,), weight=200 * 10**9
     )
-    grad_pre, _ = gate_grad(meta, pre_acts, (a_own, a_far), kept_own, turned, back[2:], b_far, after=(done,))
+    grad_pre, _ = gate_grad(meta, pre_acts, (a_own, a_far), (b_own, b_far), after=(done,))
     return grad_pre, grad_down
 
 

time: 96.4 us -> 93.8 us (0.973)
  the two profiles are of different devices: /device:TPU:10 before, /device:TPU:0 now
where the time goes in v4:
time: 93.8 us; the launch traced here: 93.5 us
  Pallas kernels  60.4 us (64%)
  waiting for transfers between devices  17.2 us (18%)
  starting transfers between devices  14.7 us (16%)
    pallas_call x11, Pallas kernels, call(): pl.pallas_call(body, grid_spec=pltpu.PrefetchScalarGridSpec(num_scalar_pr...  58.1 us
    ppermute x2, waiting for transfers between devices, two_level(): near, second = (in_pairs(cotangent), in_middle(cotangent))  7.61 us
    ppermute x2, waiting for transfers between devices, two_level(): third, outer = (in_middle(near), outwards(second))  4.96 us
    ppermute x10, waiting for transfers between devices, two_level(): back = [across_core(p) for p in sent]  3.99 us
    ppermute x2, starting transfers between devices, two_level(): near, second = (in_pairs(cotangent), in_middle(cotangent))  3.77 us
    ppermute x10, starting transfers between devices, two_level(): back = [across_core(p) for p in sent]  2.78 us
    pallas_call x1, Pallas kernels, hidden_rows(): pl.pallas_call(kernel, in_specs=[spec], out_specs=pl.BlockSpec(memory_spa...  2.22 us
    ppermute x2, starting transfers between devices, two_level(): third, outer = (in_middle(near), outwards(second))  1.97 us
  transfers between devices with their start and end apart: 20, of which 4 were waited for; matrix products, arithmetic and copies ran while one was open for 0% of the time, Pallas kernels for 59%

profile of v4, /device:TPU:0, one launch (start us, length us, event | category | flops | bytes accessed | tf_op | source)
XLA Modules:
  0.0 93.5 jit_solution(15454173759772462218)
XLA Ops:
  0.7 3.1 %collective-permute-start = (bf16[128,2048]{1,0:T(8,128)(2,1)}, bf16[128,2048]{1,0:T(8,128)(2,1)S(1)}, u32[]{:S(2)}, u32[]{:S(2)}) collective-permute-start(bf16[128,2048]{1,0:T(8,128)(2,1)} %refs_0_.10), channel_id=1, source_target_pairs={{0,4},{4,0},{8,12},{12,8},{1,5},{5,1},{9,13},{13,9},{2,6},{6,2},{1... | collective-permute-start | bytes 1572872 | tf_op jit(solution)/shard_map/ppermute | solution.py:300
  3.8 0.7 collective-permute-start.7
  4.5 2.2 %hidden.1.refs_1_ = bf16[1664,512]{1,0:T(8,128)(2,1)S(1)} custom-call(bf16[2,1664,512]{2,1,0:T(8,128)(2,1)} %refs_0_.11), custom_call_target="tpu_custom_call" | custom-call | flops 1 | bytes 1 | tf_op jit(solution)/shard_map/hidden/pallas_call | solution.py:94
  6.7 1.6 %collective-permute-start.17 = (bf16[1664,512]{1,0:T(8,128)(2,1)S(1)}, bf16[1664,512]{1,0:T(8,128)(2,1)}, u32[]{:S(2)}, u32[]{:S(2)}) collective-permute-start(bf16[1664,512]{1,0:T(8,128)(2,1)S(1)} %hidden.1.refs_1_), channel_id=1, source_target_pairs={{0,2},{1,3},{2,0},{3,1},{4,6},{5,7},{6,4},{7,5},{8,10},{9,11},{10,... | collective-permute-start | bytes 5111816 | tf_op jit(solution)/shard_map/ppermute | solution.py:298
  8.3 7.6 %collective-permute-done.refs_1_ = bf16[128,2048]{1,0:T(8,128)(2,1)S(1)} collective-permute-done((bf16[128,2048]{1,0:T(8,128)(2,1)}, bf16[128,2048]{1,0:T(8,128)(2,1)S(1)}, u32[]{:S(2)}, u32[]{:S(2)}) %collective-permute-start) | collective-permute-done | bytes 524320 | tf_op jit(solution)/shard_map/ppermute | solution.py:300
  15.9 0.7 collective-permute-start.8
  16.6 1.3 %collective-permute-start.9 = (bf16[128,2048]{1,0:T(8,128)(2,1)S(1)}, bf16[128,2048]{1,0:T(8,128)(2,1)S(1)}, u32[]{:S(2)}, u32[]{:S(2)}) collective-permute-start(bf16[128,2048]{1,0:T(8,128)(2,1)S(1)} %collective-permute-done.7.refs_1_.refs_2_), channel_id=1, source_target_pairs={{4,0},{8,12},{5,1},{9,13},{6,2},{10,14},{7,3},{11,15},{20,16},{24,... | collective-permute-start | bytes 1572872 | tf_op jit(solution)/shard_map/ppermute | solution.py:301
  17.9 1.4 %turned.1 = (bf16[2048,256]{1,0:T(8,128)(2,1)S(1)}, f32[8,128]{1,0:T(8,128)}) custom-call(s32[5]{0:T(128)S(1)} %fusion.meta_ref, bf16[128,2048]{1,0:T(8,128)(2,1)S(1)} %copy-done.3, bf16[128,2048]{1,0:T(8,128)(2,1)S(1)} %collective-permute-done.refs_1_), custom_call_target="tpu_custom_call" | custom-call | flops 7000000000 | bytes 1 | tf_op jit(solution)/shard_map/turned/pallas_call | solution.py:61
  19.3 8.4 %partials.6 = (bf16[832,256]{1,0:T(8,128)(2,1)S(1)}, bf16[832,256]{1,0:T(8,128)(2,1)S(1)}, bf16[832,256]{1,0:T(8,128)(2,1)S(1)}, bf16[832,256]{1,0:T(8,128)(2,1)...) custom-call(s32[5]{0:T(128)S(1)} %fusion.meta_ref, bf16[6656,2048]{1,0:T(8,128)(2,1)} %refs_0_.9, ...), custom_call_target="tpu_custom_call" | custom-call | flops 1 | bytes 1 | tf_op jit(solution)/shard_map/partials/pallas_call | solution.py:61
  27.9 0.5 collective-permute-start.4
  28.4 5.0 %collective-permute-done.9.refs_2_.refs_3_ = bf16[128,2048]{1,0:T(8,128)(2,1)S(1)} collective-permute-done((bf16[128,2048]{1,0:T(8,128)(2,1)S(1)}, bf16[128,2048]{1,0:T(8,128)(2,1)S(1)}, u32[]{:S(2)}, u32[]{:S(2)}) %collective-permute-start.9) | collective-permute-done | bytes 524320 | tf_op jit(solution)/shard_map/ppermute | solution.py:301
  33.3 1.5 %collective-permute-start.10 = (bf16[128,2048]{1,0:T(8,128)(2,1)S(1)}, bf16[128,2048]{1,0:T(8,128)(2,1)S(1)}, u32[]{:S(2)}, u32[]{:S(2)}) collective-permute-start(bf16[128,2048]{1,0:T(8,128)(2,1)S(1)} %collective-permute-done.8.refs_3_.refs_4_), channel_id=1, source_target_pairs={{4,0},{8,12},{5,1},{9,13},{6,2},{10,14},{7,3},{11,15},{20,16},{24,... | collective-permute-start | bytes 1572872 | tf_op jit(solution)/shard_map/ppermute | solution.py:303
  34.9 0.5 collective-permute-start.2
  35.4 4.9 %partials.7 = (bf16[1664,256]{1,0:T(8,128)(2,1)S(1)}, bf16[1664,2048]{1,0:T(8,128)(2,1)S(1)}, f32[8,128]{1,0:T(8,128)S(1)}) custom-call(s32[5]{0:T(128)S(1)} %fusion.meta_ref, bf16[6656,2048]{1,0:T(8,128)(2,1)} %refs_0_.9, bf16[2048,256]{1,0:T(8,128)(2,1)S(1)} %get-tuple-element.35.refs_1_, bf16[832,256]{1,0:T(8,128)(2,1)S(1)} %collective-permute-done.3.refs_2_, ...), custom_call_target="tpu_custom_call" | custom-call | flops 1 | bytes 1 | tf_op jit(solution)/shard_map/partials/pallas_call | solution.py:61
  40.2 1.6 %collective-permute-start.6 = (bf16[1664,256]{1,0:T(8,128)(2,1)S(1)}, bf16[1664,256]{1,0:T(8,128)(2,1)S(1)}, u32[]{:S(2)}, u32[]{:S(2)}) collective-permute-start(bf16[1664,256]{1,0:T(8,128)(2,1)S(1)} %get-tuple-element.42), channel_id=1, source_target_pairs={{0,2},{1,3},{2,0},{3,1},{4,6},{5,7},{6,4},{7,5},{8,10},{9,11},{10,... | collective-permute-start | bytes 2555912 | tf_op jit(solution)/shard_map/ppermute | solution.py:311
  41.8 4.9 %partials.8 = (f32[1664,256]{1,0:T(8,128)S(1)}, bf16[1664,2048]{1,0:T(8,128)(2,1)S(1)}, f32[8,128]{1,0:T(8,128)S(1)}) custom-call(s32[5]{0:T(128)S(1)} %fusion.meta_ref, bf16[6656,2048]{1,0:T(8,128)(2,1)} %refs_0_.9, bf16[2048,256]{1,0:T(8,128)(2,1)S(1)} %get-tuple-element.35.refs_1_, bf16[832,256]{1,0:T(8,128)(2,1)S(1)} %collective-permute-done.1.refs_2_, ...), custom_call_target="tpu_custom_call" | custom-call | flops 1 | bytes 1 | tf_op jit(solution)/shard_map/partials/pallas_call | solution.py:61
  46.7 0.6 collective-permute-done.10.refs_4_.refs_5_
  47.3 5.1 %partials.9 = (bf16[832,256]{1,0:T(8,128)(2,1)S(1)}, bf16[832,256]{1,0:T(8,128)(2,1)S(1)}, bf16[416,256]{1,0:T(8,128)(2,1)S(1)}, bf16[416,256]{1,0:T(8,128)(2,1)...) custom-call(s32[5]{0:T(128)S(1)} %fusion.meta_ref, ...), custom_call_target="tpu_custom_call" | custom-call | flops 1 | bytes 1 | tf_op jit(solution)/shard_map/partials/pallas_call | solution.py:61
  52.4 0.7 token_rows.1
  53.2 0.5 collective-permute-start.15
  53.8 0.4 collective-permute-start.11
  54.2 4.0 %collective-permute-done.11.refs_2_ = bf16[416,256]{1,0:T(8,128)(2,1)S(1)} collective-permute-done((bf16[416,256]{1,0:T(8,128)(2,1)S(1)}, bf16[416,256]{1,0:T(8,128)(2,1)S(1)}, u32[]{:S(2)}, u32[]{:S(2)}) %collective-permute-start.11) | collective-permute-done | bytes 213024 | tf_op jit(solution)/shard_map/ppermute | solution.py:317
  58.2 0.1 collective-permute-start.12
  58.3 0.4 collective-permute-start.13
  58.7 0.1 collective-permute-start.14
  58.8 3.6 %partials.10 = (bf16[1664,256]{1,0:T(8,128)(2,1)}, f32[8,128]{1,0:T(8,128)S(1)}) custom-call(s32[5]{0:T(128)S(1)} %fusion.meta_ref, bf16[1664,2048]{1,0:T(8,128)(2,1)S(1)} %get-tuple-element.53.refs_0_, bf16[2048,256]{1,0:T(8,128)(2,1)S(1)} %get-tuple-element.48.refs_1_, bf16[832,256]{1,0:T(8,128)(2,1)S(1)} %collective-permute-done.15.refs_2_, ...), custom_call_target="tpu_custom_call" | custom-call | flops 1 | bytes 1 | tf_op jit(solution)/shard_map/partials/pallas_call | solution.py:61
  62.5 1.5 %collective-permute-start.18 = (bf16[1664,256]{1,0:T(8,128)(2,1)}, bf16[1664,256]{1,0:T(8,128)(2,1)}, u32[]{:S(2)}, u32[]{:S(2)}) collective-permute-start(bf16[1664,256]{1,0:T(8,128)(2,1)} %get-tuple-element.61), channel_id=1, source_target_pairs={{0,2},{1,3},{2,0},{3,1},{4,6},{5,7},{6,4},{7,5},{8,10},{9,11},{10,... | collective-permute-start | bytes 2555912 | tf_op jit(solution)/shard_map/ppermute | solution.py:322
  64.0 2.7 %partials.11 = (f32[1664,256]{1,0:T(8,128)S(1)}, f32[8,128]{1,0:T(8,128)S(1)}) custom-call(s32[5]{0:T(128)S(1)} %fusion.meta_ref, bf16[1664,2048]{1,0:T(8,128)(2,1)S(1)} %get-tuple-element.43.refs_0_, bf16[2048,256]{1,0:T(8,128)(2,1)S(1)} %get-tuple-element.48.refs_1_, bf16[416,256]{1,0:T(8,128)(2,1)S(1)} %collective-permute-done.11.refs_2_, ...), custom_call_target="tpu_custom_call" | custom-call | flops 1 | bytes 1 | tf_op jit(solution)/shard_map/partials/pallas_call | solution.py:61
  66.7 0.5 arrived.1.refs_5_
  67.2 0.3 copy-done.1
  67.6 20.8 %weight_grad.1 = (bf16[6656,2048]{1,0:T(8,128)(2,1)}, f32[8,128]{1,0:T(8,128)S(1)}) custom-call(s32[5]{0:T(128)S(1)} %fusion.meta_ref, bf16[512,2048]{1,0:T(8,128)(2,1)S(1)} %get-tuple-element.62.refs_0_, bf16[1664,512]{1,0:T(8,128)(2,1)S(1)} %hidden.1.refs_1_, bf16[1664,512]{1,0:T(8,128)(2,1)} %collective-permute-done.5.refs_4_.refs_2_, ...), custom_call_target="tpu_custom_call" | custom-call | flops 199999995904 | bytes 1 | tf_op jit(solution)/shard_map/weight_grad/pallas_call | solution.py:61
  88.4 5.1 %gate_grad.1 = (bf16[2,1664,512]{2,1,0:T(8,128)(2,1)}, f32[8,128]{1,0:T(8,128)}) custom-call(s32[5]{0:T(128)S(1)} %fusion.meta_ref, bf16[2,1664,512]{2,1,0:T(8,128)(2,1)S(1)} %copy-done, f32[1664,256]{1,0:T(8,128)S(1)} %get-tuple-element.41.refs_1_, bf16[1664,256]{1,0:T(8,128)(2,1)S(1)} %copy-done.2, f32[1664,256]{1,0:T(8,128)S(1)} %get-tuple-element.60.refs_3_, ...), custom_call_target="tpu_custom_call" | custom-call | flops 1 | bytes 1 | tf_op jit(solution)/shard_map/gate_grad/pallas_call | solution.py:61
  (39 shorter events, 0.4 us)
Async XLA Ops:
  0.6 7.6 %copy-start.4 = (s32[5]{0:T(128)S(1)}, s32[5]{0:T(128)}, u32[]{:S(2)}) copy-start(s32[5]{0:T(128)} %constant.27.clone) | copy-start | bytes 64
  0.6 7.6 %copy-start.5 = (s32[5]{0:T(128)S(1)}, s32[5]{0:T(128)}, u32[]{:S(2)}) copy-start(s32[5]{0:T(128)} %constant.26.clone) | copy-start | bytes 64
  0.7 7.6 %copy-start.6 = (s32[5]{0:T(128)S(1)}, s32[5]{0:T(128)}, u32[]{:S(2)}) copy-start(s32[5]{0:T(128)} %constant.25.clone) | copy-start | bytes 64
  0.7 7.6 %copy-start.7 = (s32[5]{0:T(128)S(1)}, s32[5]{0:T(128)}, u32[]{:S(2)}) copy-start(s32[5]{0:T(128)} %constant.24.clone) | copy-start | bytes 64
  0.7 7.6 %copy-start.8 = (s32[5]{0:T(128)S(1)}, s32[5]{0:T(128)}, u32[]{:S(2)}) copy-start(s32[5]{0:T(128)} %constant.23.clone) | copy-start | bytes 64
  0.7 17.2 %copy-start.3 = (bf16[128,2048]{1,0:T(8,128)(2,1)S(1)}, bf16[128,2048]{1,0:T(8,128)(2,1)}, u32[]{:S(2)}) copy-start(bf16[128,2048]{1,0:T(8,128)(2,1)} %refs_0_.10) | copy-start | bytes 1572868
  0.7 15.2 %collective-permute-start = (bf16[128,2048]{1,0:T(8,128)(2,1)}, bf16[128,2048]{1,0:T(8,128)(2,1)S(1)}, u32[]{:S(2)}, u32[]{:S(2)}) collective-permute-start(bf16[128,2048]{1,0:T(8,128)(2,1)} %refs_0_.10), channel_id=1, source_target_pairs={{0,4},{4,0},{8,12},{12,8},{1,5},{5,1},{9,13},{13,9},{2,6},{6,2},{1... | collective-permute-start | bytes 1572872 | tf_op jit(solution)/shard_map/ppermute | solution.py:300
  3.8 12.8 %collective-permute-start.7 = (bf16[128,2048]{1,0:T(8,128)(2,1)}, bf16[128,2048]{1,0:T(8,128)(2,1)S(1)}, u32[]{:S(2)}, u32[]{:S(2)}) collective-permute-start(bf16[128,2048]{1,0:T(8,128)(2,1)} %refs_0_.10), channel_id=1, source_target_pairs={{4,8},{8,4},{5,9},{9,5},{6,10},{10,6},{7,11},{11,7},{20,24},{24,20... | collective-permute-start | bytes 1572872 | tf_op jit(solution)/shard_map/ppermute | solution.py:300
  6.7 46.4 %collective-permute-start.17 = (bf16[1664,512]{1,0:T(8,128)(2,1)S(1)}, bf16[1664,512]{1,0:T(8,128)(2,1)}, u32[]{:S(2)}, u32[]{:S(2)}) collective-permute-start(bf16[1664,512]{1,0:T(8,128)(2,1)S(1)} %hidden.1.refs_1_), channel_id=1, source_target_pairs={{0,2},{1,3},{2,0},{3,1},{4,6},{5,7},{6,4},{7,5},{8,10},{9,11},{10,... | collective-permute-start | bytes 5111816 | tf_op jit(solution)/shard_map/ppermute | solution.py:298
  8.3 27.1 %collective-permute-start.5 = (bf16[1664,512]{1,0:T(8,128)(2,1)S(1)}, bf16[1664,512]{1,0:T(8,128)(2,1)}, u32[]{:S(2)}, u32[]{:S(2)}) collective-permute-start(bf16[1664,512]{1,0:T(8,128)(2,1)S(1)} %hidden.1.refs_1_), channel_id=1, source_target_pairs={{0,1},{1,0},{2,3},{3,2},{4,5},{5,4},{6,7},{7,6},{8,9},{9,8},{10,11... | collective-permute-start | bytes 5111816 | tf_op jit(solution)/shard_map/ppermute | solution.py:298
  15.9 11.9 %collective-permute-start.8 = (bf16[128,2048]{1,0:T(8,128)(2,1)S(1)}, bf16[128,2048]{1,0:T(8,128)(2,1)S(1)}, u32[]{:S(2)}, u32[]{:S(2)}) collective-permute-start(bf16[128,2048]{1,0:T(8,128)(2,1)S(1)} %collective-permute-done.refs_1_), channel_id=1, source_target_pairs={{4,8},{8,4},{5,9},{9,5},{6,10},{10,6},{7,11},{11,7},{20,24},{24,20... | collective-permute-start | bytes 1572872 | tf_op jit(solution)/shard_map/ppermute | solution.py:301
  16.6 16.7 %collective-permute-start.9 = (bf16[128,2048]{1,0:T(8,128)(2,1)S(1)}, bf16[128,2048]{1,0:T(8,128)(2,1)S(1)}, u32[]{:S(2)}, u32[]{:S(2)}) collective-permute-start(bf16[128,2048]{1,0:T(8,128)(2,1)S(1)} %collective-permute-done.7.refs_1_.refs_2_), channel_id=1, source_target_pairs={{4,0},{8,12},{5,1},{9,13},{6,2},{10,14},{7,3},{11,15},{20,16},{24,... | collective-permute-start | bytes 1572872 | tf_op jit(solution)/shard_map/ppermute | solution.py:301
  27.8 7.0 %collective-permute-start.3 = (bf16[832,256]{1,0:T(8,128)(2,1)S(1)}, bf16[832,256]{1,0:T(8,128)(2,1)S(1)}, u32[]{:S(2)}, u32[]{:S(2)}) collective-permute-start(bf16[832,256]{1,0:T(8,128)(2,1)S(1)} %get-tuple-element.38), channel_id=1, source_target_pairs={{0,1},{1,0},{2,3},{3,2},{4,5},{5,4},{6,7},{7,6},{8,9},{9,8},{10,11... | collective-permute-start | bytes 1277960 | tf_op jit(solution)/shard_map/ppermute | solution.py:309
  27.9 7.0 %collective-permute-start.4 = (bf16[832,256]{1,0:T(8,128)(2,1)S(1)}, bf16[832,256]{1,0:T(8,128)(2,1)S(1)}, u32[]{:S(2)}, u32[]{:S(2)}) collective-permute-start(bf16[832,256]{1,0:T(8,128)(2,1)S(1)} %get-tuple-element.39), channel_id=1, source_target_pairs={{0,1},{1,0},{2,3},{3,2},{4,5},{5,4},{6,7},{7,6},{8,9},{9,8},{10,11... | collective-permute-start | bytes 1277960 | tf_op jit(solution)/shard_map/ppermute | solution.py:309
  33.3 14.0 %collective-permute-start.10 = (bf16[128,2048]{1,0:T(8,128)(2,1)S(1)}, bf16[128,2048]{1,0:T(8,128)(2,1)S(1)}, u32[]{:S(2)}, u32[]{:S(2)}) collective-permute-start(bf16[128,2048]{1,0:T(8,128)(2,1)S(1)} %collective-permute-done.8.refs_3_.refs_4_), channel_id=1, source_target_pairs={{4,0},{8,12},{5,1},{9,13},{6,2},{10,14},{7,3},{11,15},{20,16},{24,... | collective-permute-start | bytes 1572872 | tf_op jit(solution)/shard_map/ppermute | solution.py:303
  34.8 7.0 %collective-permute-start.1 = (bf16[832,256]{1,0:T(8,128)(2,1)S(1)}, bf16[832,256]{1,0:T(8,128)(2,1)S(1)}, u32[]{:S(2)}, u32[]{:S(2)}) collective-permute-start(bf16[832,256]{1,0:T(8,128)(2,1)S(1)} %get-tuple-element.36), channel_id=1, source_target_pairs={{0,1},{1,0},{2,3},{3,2},{4,5},{5,4},{6,7},{7,6},{8,9},{9,8},{10,11... | collective-permute-start | bytes 1277960 | tf_op jit(solution)/shard_map/ppermute | solution.py:309
  34.9 6.9 %collective-permute-start.2 = (bf16[832,256]{1,0:T(8,128)(2,1)S(1)}, bf16[832,256]{1,0:T(8,128)(2,1)S(1)}, u32[]{:S(2)}, u32[]{:S(2)}) collective-permute-start(bf16[832,256]{1,0:T(8,128)(2,1)S(1)} %get-tuple-element.37), channel_id=1, source_target_pairs={{0,1},{1,0},{2,3},{3,2},{4,5},{5,4},{6,7},{7,6},{8,9},{9,8},{10,11... | collective-permute-start | bytes 1277960 | tf_op jit(solution)/shard_map/ppermute | solution.py:309
  40.2 26.4 %collective-permute-start.6 = (bf16[1664,256]{1,0:T(8,128)(2,1)S(1)}, bf16[1664,256]{1,0:T(8,128)(2,1)S(1)}, u32[]{:S(2)}, u32[]{:S(2)}) collective-permute-start(bf16[1664,256]{1,0:T(8,128)(2,1)S(1)} %get-tuple-element.42), channel_id=1, source_target_pairs={{0,2},{1,3},{2,0},{3,1},{4,6},{5,7},{6,4},{7,5},{8,10},{9,11},{10,... | collective-permute-start | bytes 2555912 | tf_op jit(solution)/shard_map/ppermute | solution.py:311
  53.1 14.5 %collective-permute-start.19 = (bf16[1664,512]{1,0:T(8,128)(2,1)}, bf16[1664,512]{1,0:T(8,128)(2,1)S(1)}, u32[]{:S(2)}, u32[]{:S(2)}) collective-permute-start(bf16[1664,512]{1,0:T(8,128)(2,1)} %collective-permute-done.17.refs_3_), channel_id=1, source_target_pairs={{0,1},{1,0},{2,3},{3,2},{4,5},{5,4},{6,7},{7,6},{8,9},{9,8},{10,11... | collective-permute-start | bytes 5111816 | tf_op jit(solution)/shard_map/ppermute | solution.py:320
  53.2 5.1 %collective-permute-start.15 = (bf16[832,256]{1,0:T(8,128)(2,1)S(1)}, bf16[832,256]{1,0:T(8,128)(2,1)S(1)}, u32[]{:S(2)}, u32[]{:S(2)}) collective-permute-start(bf16[832,256]{1,0:T(8,128)(2,1)S(1)} %get-tuple-element.54), channel_id=1, source_target_pairs={{0,1},{1,0},{2,3},{3,2},{4,5},{5,4},{6,7},{7,6},{8,9},{9,8},{10,11... | collective-permute-start | bytes 1277960 | tf_op jit(solution)/shard_map/ppermute | solution.py:317
  53.7 5.0 %collective-permute-start.16 = (bf16[832,256]{1,0:T(8,128)(2,1)S(1)}, bf16[832,256]{1,0:T(8,128)(2,1)S(1)}, u32[]{:S(2)}, u32[]{:S(2)}) collective-permute-start(bf16[832,256]{1,0:T(8,128)(2,1)S(1)} %get-tuple-element.55), channel_id=1, source_target_pairs={{0,1},{1,0},{2,3},{3,2},{4,5},{5,4},{6,7},{7,6},{8,9},{9,8},{10,11... | collective-permute-start | bytes 1277960 | tf_op jit(solution)/shard_map/ppermute | solution.py:317
  53.8 4.4 %collective-permute-start.11 = (bf16[416,256]{1,0:T(8,128)(2,1)S(1)}, bf16[416,256]{1,0:T(8,128)(2,1)S(1)}, u32[]{:S(2)}, u32[]{:S(2)}) collective-permute-start(bf16[416,256]{1,0:T(8,128)(2,1)S(1)} %get-tuple-element.49), channel_id=1, source_target_pairs={{0,1},{1,0},{2,3},{3,2},{4,5},{5,4},{6,7},{7,6},{8,9},{9,8},{10,11... | collective-permute-start | bytes 638984 | tf_op jit(solution)/shard_map/ppermute | solution.py:317
  58.2 4.3 %collective-permute-start.12 = (bf16[416,256]{1,0:T(8,128)(2,1)S(1)}, bf16[416,256]{1,0:T(8,128)(2,1)S(1)}, u32[]{:S(2)}, u32[]{:S(2)}) collective-permute-start(bf16[416,256]{1,0:T(8,128)(2,1)S(1)} %get-tuple-element.50), channel_id=1, source_target_pairs={{0,1},{1,0},{2,3},{3,2},{4,5},{5,4},{6,7},{7,6},{8,9},{9,8},{10,11... | collective-permute-start | bytes 638984 | tf_op jit(solution)/shard_map/ppermute | solution.py:317
  58.3 5.6 %collective-permute-start.13 = (bf16[416,256]{1,0:T(8,128)(2,1)S(1)}, bf16[416,256]{1,0:T(8,128)(2,1)S(1)}, u32[]{:S(2)}, u32[]{:S(2)}) collective-permute-start(bf16[416,256]{1,0:T(8,128)(2,1)S(1)} %get-tuple-element.51), channel_id=1, source_target_pairs={{0,1},{1,0},{2,3},{3,2},{4,5},{5,4},{6,7},{7,6},{8,9},{9,8},{10,11... | collective-permute-start | bytes 638984 | tf_op jit(solution)/shard_map/ppermute | solution.py:317
  58.7 5.3 %collective-permute-start.14 = (bf16[416,256]{1,0:T(8,128)(2,1)S(1)}, bf16[416,256]{1,0:T(8,128)(2,1)S(1)}, u32[]{:S(2)}, u32[]{:S(2)}) collective-permute-start(bf16[416,256]{1,0:T(8,128)(2,1)S(1)} %get-tuple-element.52), channel_id=1, source_target_pairs={{0,1},{1,0},{2,3},{3,2},{4,5},{5,4},{6,7},{7,6},{8,9},{9,8},{10,11... | collective-permute-start | bytes 638984 | tf_op jit(solution)/shard_map/ppermute | solution.py:317
  62.5 26.0 %collective-permute-start.18 = (bf16[1664,256]{1,0:T(8,128)(2,1)}, bf16[1664,256]{1,0:T(8,128)(2,1)}, u32[]{:S(2)}, u32[]{:S(2)}) collective-permute-start(bf16[1664,256]{1,0:T(8,128)(2,1)} %get-tuple-element.61), channel_id=1, source_target_pairs={{0,2},{1,3},{2,0},{3,1},{4,6},{5,7},{6,4},{7,5},{8,10},{9,11},{10,... | collective-permute-start | bytes 2555912 | tf_op jit(solution)/shard_map/ppermute | solution.py:322
  66.7 0.9 copy-start.1
  67.6 20.8 %copy-start = (bf16[2,1664,512]{2,1,0:T(8,128)(2,1)S(1)}, bf16[2,1664,512]{2,1,0:T(8,128)(2,1)}, u32[]{:S(2)}) copy-start(bf16[2,1664,512]{2,1,0:T(8,128)(2,1)} %refs_0_.11) | copy-start | bytes 10223620
  67.6 20.8 %copy-start.2 = (bf16[1664,256]{1,0:T(8,128)(2,1)S(1)}, bf16[1664,256]{1,0:T(8,128)(2,1)}, u32[]{:S(2)}) copy-start(bf16[1664,256]{1,0:T(8,128)(2,1)} %copy-done.1) | copy-start | bytes 2555908

commit v5 on v4

--- a/solution.py
+++ b/solution.py
@@ -10,7 +10,7 @@
 from jax.sharding import PartitionSpec as P
 
 LANES = 128
-TURNED, ARRIVED = 7000 * 10**6, 9200 * 10**6
+TURNED, ARRIVED = 7000 * 10**6, 14200 * 10**6
 MIB = 1024 * 1024
 
 
@@ -243,7 +243,7 @@
 def gate_grad(meta, acts, early, late, after=()):
     _, rows, tokens = acts.shape
     half = tokens // 2
-    tile = rows // 4
+    tile = rows // 2
 
     def kernel(meta_ref, acts_ref, *refs):
         pairs, out_ref = (refs[:2], refs[2:4]), refs[4]
@@ -262,7 +262,7 @@
 
     ins = [in_vmem(a) for a in (acts, *early, *late)]
     outs = [(jax.ShapeDtypeStruct(acts.shape, acts.dtype), pl.BlockSpec((2, tile, tokens), lambda i, m: (0, i, 0)))]
-    return call(kernel, "gate_grad", meta, (4,), ins, outs, after=after, vmem=8)
+    return call(kernel, "gate_grad", meta, (2,), ins, outs, after=after, vmem=8)
 
 
 def wait_for(meta, after, weight):
@@ -316,7 +316,7 @@
     )
     back = [across_core(p) for p in sent]
     cots, done = all_slots(meta, slots, each, feats, after=(done,))
-    hidden_far, done = lax.optimization_barrier((hidden_far, done))
+    hidden_far, back[0], back[1] = lax.optimization_barrier((hidden_far, back[0], back[1]))
     hidden_both = across_core(hidden_far)
     b_sum, done = sums((2,), kept_sum, dtypes=(bf16,), splits=(1,), turned=turned, adds=(back[:2],), keep=False, after=(done,))
     b_far = across_x(b_sum)

time: 93.8 us -> 93.5 us (level); the launches traced: 93.5 us -> 91.9 us
  waiting for transfers between devices: 17.2 us -> 15.6 us
    ppermute x10, waiting for transfers between devices: 3.99 us -> 1.81 us  [two_level(): back = [across_core(p) for p in sent]]
  transfers between devices with their start and end apart: 20 -> 20, of which waited for: 4 -> 6; matrix products, arithmetic and copies ran while one was open for 0% -> 0% of each run, Pallas kernels for 59% -> 60%
where the time goes in v5:
time: 93.5 us; the launch traced here: 91.9 us
  Pallas kernels  60.3 us (64%)
  waiting for transfers between devices  15.6 us (17%)
  starting transfers between devices  14.7 us (16%)
    pallas_call x11, Pallas kernels, call(): pl.pallas_call(body, grid_spec=pltpu.PrefetchScalarGridSpec(num_scalar_pr...  58.1 us
    ppermute x2, waiting for transfers between devices, two_level(): near, second = (in_pairs(cotangent), in_middle(cotangent))  7.55 us
    ppermute x2, waiting for transfers between devices, two_level(): third, outer = (in_middle(near), outwards(second))  4.96 us
    ppermute x2, starting transfers between devices, two_level(): near, second = (in_pairs(cotangent), in_middle(cotangent))  3.77 us
    ppermute x10, starting transfers between devices, two_level(): back = [across_core(p) for p in sent]  2.65 us
    pallas_call x1, Pallas kernels, hidden_rows(): pl.pallas_call(kernel, in_specs=[spec], out_specs=pl.BlockSpec(memory_spa...  2.22 us
    ppermute x2, starting transfers between devices, two_level(): third, outer = (in_middle(near), outwards(second))  1.97 us
  transfers between devices with their start and end apart: 20, of which 6 were waited for; matrix products, arithmetic and copies ran while one was open for 0% of the time, Pallas kernels for 60%

profile of v5, /device:TPU:0, one launch (start us, length us, event | category | flops | bytes accessed | tf_op | source)
XLA Modules:
  0.0 91.9 jit_solution(9561825531462464116)
XLA Ops:
  0.7 3.1 %collective-permute-start = (bf16[128,2048]{1,0:T(8,128)(2,1)}, bf16[128,2048]{1,0:T(8,128)(2,1)S(1)}, u32[]{:S(2)}, u32[]{:S(2)}) collective-permute-start(bf16[128,2048]{1,0:T(8,128)(2,1)} %refs_0_.10), channel_id=1, source_target_pairs={{0,4},{4,0},{8,12},{12,8},{1,5},{5,1},{9,13},{13,9},{2,6},{6,2},{1... | collective-permute-start | bytes 1572872 | tf_op jit(solution)/shard_map/ppermute | solution.py:300
  3.8 0.7 collective-permute-start.7
  4.5 2.2 %hidden.1.refs_1_ = bf16[1664,512]{1,0:T(8,128)(2,1)S(1)} custom-call(bf16[2,1664,512]{2,1,0:T(8,128)(2,1)} %refs_0_.11), custom_call_target="tpu_custom_call" | custom-call | flops 1 | bytes 1 | tf_op jit(solution)/shard_map/hidden/pallas_call | solution.py:94
  6.8 1.6 %collective-permute-start.15 = (bf16[1664,512]{1,0:T(8,128)(2,1)S(1)}, bf16[1664,512]{1,0:T(8,128)(2,1)}, u32[]{:S(2)}, u32[]{:S(2)}) collective-permute-start(bf16[1664,512]{1,0:T(8,128)(2,1)S(1)} %hidden.1.refs_1_), channel_id=1, source_target_pairs={{0,2},{1,3},{2,0},{3,1},{4,6},{5,7},{6,4},{7,5},{8,10},{9,11},{10,... | collective-permute-start | bytes 5111816 | tf_op jit(solution)/shard_map/ppermute | solution.py:298
  8.4 7.5 %collective-permute-done.refs_1_ = bf16[128,2048]{1,0:T(8,128)(2,1)S(1)} collective-permute-done((bf16[128,2048]{1,0:T(8,128)(2,1)}, bf16[128,2048]{1,0:T(8,128)(2,1)S(1)}, u32[]{:S(2)}, u32[]{:S(2)}) %collective-permute-start) | collective-permute-done | bytes 524320 | tf_op jit(solution)/shard_map/ppermute | solution.py:300
  15.9 0.7 collective-permute-start.8
  16.6 1.3 %collective-permute-start.9 = (bf16[128,2048]{1,0:T(8,128)(2,1)S(1)}, bf16[128,2048]{1,0:T(8,128)(2,1)S(1)}, u32[]{:S(2)}, u32[]{:S(2)}) collective-permute-start(bf16[128,2048]{1,0:T(8,128)(2,1)S(1)} %collective-permute-done.7.refs_1_.refs_2_), channel_id=1, source_target_pairs={{4,0},{8,12},{5,1},{9,13},{6,2},{10,14},{7,3},{11,15},{20,16},{24,... | collective-permute-start | bytes 1572872 | tf_op jit(solution)/shard_map/ppermute | solution.py:301
  17.9 1.4 %turned.1 = (bf16[2048,256]{1,0:T(8,128)(2,1)S(1)}, f32[8,128]{1,0:T(8,128)}) custom-call(s32[5]{0:T(128)S(1)} %fusion.meta_ref, bf16[128,2048]{1,0:T(8,128)(2,1)S(1)} %copy-done.3, bf16[128,2048]{1,0:T(8,128)(2,1)S(1)} %collective-permute-done.refs_1_), custom_call_target="tpu_custom_call" | custom-call | flops 7000000000 | bytes 1 | tf_op jit(solution)/shard_map/turned/pallas_call | solution.py:61
  19.3 8.4 %partials.6 = (bf16[832,256]{1,0:T(8,128)(2,1)S(1)}, bf16[832,256]{1,0:T(8,128)(2,1)S(1)}, bf16[832,256]{1,0:T(8,128)(2,1)S(1)}, bf16[832,256]{1,0:T(8,128)(2,1)...) custom-call(s32[5]{0:T(128)S(1)} %fusion.meta_ref, bf16[6656,2048]{1,0:T(8,128)(2,1)} %refs_0_.9, ...), custom_call_target="tpu_custom_call" | custom-call | flops 1 | bytes 1 | tf_op jit(solution)/shard_map/partials/pallas_call | solution.py:61
  27.9 0.5 collective-permute-start.4
  28.4 5.0 %collective-permute-done.9.refs_2_.refs_3_ = bf16[128,2048]{1,0:T(8,128)(2,1)S(1)} collective-permute-done((bf16[128,2048]{1,0:T(8,128)(2,1)S(1)}, bf16[128,2048]{1,0:T(8,128)(2,1)S(1)}, u32[]{:S(2)}, u32[]{:S(2)}) %collective-permute-start.9) | collective-permute-done | bytes 524320 | tf_op jit(solution)/shard_map/ppermute | solution.py:301
  33.3 1.5 %collective-permute-start.10 = (bf16[128,2048]{1,0:T(8,128)(2,1)S(1)}, bf16[128,2048]{1,0:T(8,128)(2,1)S(1)}, u32[]{:S(2)}, u32[]{:S(2)}) collective-permute-start(bf16[128,2048]{1,0:T(8,128)(2,1)S(1)} %collective-permute-done.8.refs_3_.refs_4_), channel_id=1, source_target_pairs={{4,0},{8,12},{5,1},{9,13},{6,2},{10,14},{7,3},{11,15},{20,16},{24,... | collective-permute-start | bytes 1572872 | tf_op jit(solution)/shard_map/ppermute | solution.py:303
  34.9 0.5 collective-permute-start.2
  35.4 4.9 %partials.7 = (bf16[1664,256]{1,0:T(8,128)(2,1)S(1)}, bf16[1664,2048]{1,0:T(8,128)(2,1)S(1)}, f32[8,128]{1,0:T(8,128)S(1)}) custom-call(s32[5]{0:T(128)S(1)} %fusion.meta_ref, bf16[6656,2048]{1,0:T(8,128)(2,1)} %refs_0_.9, bf16[2048,256]{1,0:T(8,128)(2,1)S(1)} %get-tuple-element.36.refs_1_, bf16[832,256]{1,0:T(8,128)(2,1)S(1)} %collective-permute-done.3.refs_2_, ...), custom_call_target="tpu_custom_call" | custom-call | flops 1 | bytes 1 | tf_op jit(solution)/shard_map/partials/pallas_call | solution.py:61
  40.2 1.6 %collective-permute-start.6 = (bf16[1664,256]{1,0:T(8,128)(2,1)S(1)}, bf16[1664,256]{1,0:T(8,128)(2,1)S(1)}, u32[]{:S(2)}, u32[]{:S(2)}) collective-permute-start(bf16[1664,256]{1,0:T(8,128)(2,1)S(1)} %get-tuple-element.43), channel_id=1, source_target_pairs={{0,2},{1,3},{2,0},{3,1},{4,6},{5,7},{6,4},{7,5},{8,10},{9,11},{10,... | collective-permute-start | bytes 2555912 | tf_op jit(solution)/shard_map/ppermute | solution.py:311
  41.8 4.9 %partials.8 = (f32[1664,256]{1,0:T(8,128)S(1)}, bf16[1664,2048]{1,0:T(8,128)(2,1)S(1)}, f32[8,128]{1,0:T(8,128)S(1)}) custom-call(s32[5]{0:T(128)S(1)} %fusion.meta_ref, bf16[6656,2048]{1,0:T(8,128)(2,1)} %refs_0_.9, bf16[2048,256]{1,0:T(8,128)(2,1)S(1)} %get-tuple-element.36.refs_1_, bf16[832,256]{1,0:T(8,128)(2,1)S(1)} %collective-permute-done.1.refs_2_, ...), custom_call_target="tpu_custom_call" | custom-call | flops 1 | bytes 1 | tf_op jit(solution)/shard_map/partials/pallas_call | solution.py:61
  46.7 0.6 collective-permute-done.10.refs_4_.refs_5_
  47.3 5.1 %partials.9 = (bf16[832,256]{1,0:T(8,128)(2,1)S(1)}, bf16[832,256]{1,0:T(8,128)(2,1)S(1)}, bf16[416,256]{1,0:T(8,128)(2,1)S(1)}, bf16[416,256]{1,0:T(8,128)(2,1)...) custom-call(s32[5]{0:T(128)S(1)} %fusion.meta_ref, ...), custom_call_target="tpu_custom_call" | custom-call | flops 1 | bytes 1 | tf_op jit(solution)/shard_map/partials/pallas_call | solution.py:61
  52.5 0.5 collective-permute-start.17
  53.0 1.2 %collective-permute-done.16.refs_2_ = bf16[832,256]{1,0:T(8,128)(2,1)S(1)} collective-permute-done((bf16[832,256]{1,0:T(8,128)(2,1)S(1)}, bf16[832,256]{1,0:T(8,128)(2,1)S(1)}, u32[]{:S(2)}, u32[]{:S(2)}) %collective-permute-start.16) | collective-permute-done | bytes 426016 | tf_op jit(solution)/shard_map/ppermute | solution.py:317
  54.2 0.6 collective-permute-done.17.refs_3_
  55.0 0.4 collective-permute-start.12
  55.5 0.4 collective-permute-start.14
  55.9 0.7 token_rows.1
  56.6 3.6 %partials.10 = (bf16[1664,256]{1,0:T(8,128)(2,1)}, f32[8,128]{1,0:T(8,128)S(1)}) custom-call(s32[5]{0:T(128)S(1)} %fusion.meta_ref, bf16[1664,2048]{1,0:T(8,128)(2,1)S(1)} %get-tuple-element.54.refs_0_, bf16[2048,256]{1,0:T(8,128)(2,1)S(1)} %get-tuple-element.49.refs_1_, bf16[832,256]{1,0:T(8,128)(2,1)S(1)} %collective-permute-done.16.refs_2_, ...), custom_call_target="tpu_custom_call" | custom-call | flops 1 | bytes 1 | tf_op jit(solution)/shard_map/partials/pallas_call | solution.py:61
  60.2 1.5 %collective-permute-start.18 = (bf16[1664,256]{1,0:T(8,128)(2,1)}, bf16[1664,256]{1,0:T(8,128)(2,1)}, u32[]{:S(2)}, u32[]{:S(2)}) collective-permute-start(bf16[1664,256]{1,0:T(8,128)(2,1)} %get-tuple-element.63), channel_id=1, source_target_pairs={{0,2},{1,3},{2,0},{3,1},{4,6},{5,7},{6,4},{7,5},{8,10},{9,11},{10,... | collective-permute-start | bytes 2555912 | tf_op jit(solution)/shard_map/ppermute | solution.py:322
  61.7 2.7 %partials.11 = (f32[1664,256]{1,0:T(8,128)S(1)}, f32[8,128]{1,0:T(8,128)S(1)}) custom-call(s32[5]{0:T(128)S(1)} %fusion.meta_ref, bf16[1664,2048]{1,0:T(8,128)(2,1)S(1)} %get-tuple-element.44.refs_0_, bf16[2048,256]{1,0:T(8,128)(2,1)S(1)} %get-tuple-element.49.refs_1_, bf16[416,256]{1,0:T(8,128)(2,1)S(1)} %collective-permute-done.11.refs_2_, ...), custom_call_target="tpu_custom_call" | custom-call | flops 1 | bytes 1 | tf_op jit(solution)/shard_map/partials/pallas_call | solution.py:61
  64.4 0.7 collective-permute-done.6.refs_1_.refs_2_
  65.1 0.5 arrived.1.refs_5_
  65.7 0.4 copy-done.1
  66.0 20.8 %weight_grad.1 = (bf16[6656,2048]{1,0:T(8,128)(2,1)}, f32[8,128]{1,0:T(8,128)S(1)}) custom-call(s32[5]{0:T(128)S(1)} %fusion.meta_ref, bf16[512,2048]{1,0:T(8,128)(2,1)S(1)} %get-tuple-element.64.refs_0_, bf16[1664,512]{1,0:T(8,128)(2,1)S(1)} %hidden.1.refs_1_, bf16[1664,512]{1,0:T(8,128)(2,1)} %collective-permute-done.5.refs_4_.refs_2_, ...), custom_call_target="tpu_custom_call" | custom-call | flops 199999995904 | bytes 1 | tf_op jit(solution)/shard_map/weight_grad/pallas_call | solution.py:61
  86.9 5.0 %gate_grad.1 = (bf16[2,1664,512]{2,1,0:T(8,128)(2,1)}, f32[8,128]{1,0:T(8,128)}) custom-call(s32[5]{0:T(128)S(1)} %fusion.meta_ref, bf16[2,1664,512]{2,1,0:T(8,128)(2,1)S(1)} %copy-done, f32[1664,256]{1,0:T(8,128)S(1)} %get-tuple-element.42.refs_1_, bf16[1664,256]{1,0:T(8,128)(2,1)S(1)} %copy-done.2, f32[1664,256]{1,0:T(8,128)S(1)} %get-tuple-element.62.refs_3_, ...), custom_call_target="tpu_custom_call" | custom-call | flops 1 | bytes 1 | tf_op jit(solution)/shard_map/gate_grad/pallas_call | solution.py:61
  (39 shorter events, 0.7 us)
Async XLA Ops:
  0.6 7.7 %copy-start.4 = (s32[5]{0:T(128)S(1)}, s32[5]{0:T(128)}, u32[]{:S(2)}) copy-start(s32[5]{0:T(128)} %constant.27.clone) | copy-start | bytes 64
  0.6 7.7 %copy-start.5 = (s32[5]{0:T(128)S(1)}, s32[5]{0:T(128)}, u32[]{:S(2)}) copy-start(s32[5]{0:T(128)} %constant.26.clone) | copy-start | bytes 64
  0.7 7.7 %copy-start.6 = (s32[5]{0:T(128)S(1)}, s32[5]{0:T(128)}, u32[]{:S(2)}) copy-start(s32[5]{0:T(128)} %constant.25.clone) | copy-start | bytes 64
  0.7 7.7 %copy-start.7 = (s32[5]{0:T(128)S(1)}, s32[5]{0:T(128)}, u32[]{:S(2)}) copy-start(s32[5]{0:T(128)} %constant.24.clone) | copy-start | bytes 64
  0.7 7.7 %copy-start.8 = (s32[5]{0:T(128)S(1)}, s32[5]{0:T(128)}, u32[]{:S(2)}) copy-start(s32[5]{0:T(128)} %constant.23.clone) | copy-start | bytes 64
  0.7 17.2 %copy-start.3 = (bf16[128,2048]{1,0:T(8,128)(2,1)S(1)}, bf16[128,2048]{1,0:T(8,128)(2,1)}, u32[]{:S(2)}) copy-start(bf16[128,2048]{1,0:T(8,128)(2,1)} %refs_0_.10) | copy-start | bytes 1572868
  0.7 15.2 %collective-permute-start = (bf16[128,2048]{1,0:T(8,128)(2,1)}, bf16[128,2048]{1,0:T(8,128)(2,1)S(1)}, u32[]{:S(2)}, u32[]{:S(2)}) collective-permute-start(bf16[128,2048]{1,0:T(8,128)(2,1)} %refs_0_.10), channel_id=1, source_target_pairs={{0,4},{4,0},{8,12},{12,8},{1,5},{5,1},{9,13},{13,9},{2,6},{6,2},{1... | collective-permute-start | bytes 1572872 | tf_op jit(solution)/shard_map/ppermute | solution.py:300
  3.8 12.8 %collective-permute-start.7 = (bf16[128,2048]{1,0:T(8,128)(2,1)}, bf16[128,2048]{1,0:T(8,128)(2,1)S(1)}, u32[]{:S(2)}, u32[]{:S(2)}) collective-permute-start(bf16[128,2048]{1,0:T(8,128)(2,1)} %refs_0_.10), channel_id=1, source_target_pairs={{4,8},{8,4},{5,9},{9,5},{6,10},{10,6},{7,11},{11,7},{20,24},{24,20... | collective-permute-start | bytes 1572872 | tf_op jit(solution)/shard_map/ppermute | solution.py:300
  6.7 28.7 %collective-permute-start.5 = (bf16[1664,512]{1,0:T(8,128)(2,1)S(1)}, bf16[1664,512]{1,0:T(8,128)(2,1)}, u32[]{:S(2)}, u32[]{:S(2)}) collective-permute-start(bf16[1664,512]{1,0:T(8,128)(2,1)S(1)} %hidden.1.refs_1_), channel_id=1, source_target_pairs={{0,1},{1,0},{2,3},{3,2},{4,5},{5,4},{6,7},{7,6},{8,9},{9,8},{10,11... | collective-permute-start | bytes 5111816 | tf_op jit(solution)/shard_map/ppermute | solution.py:298
  6.8 46.3 %collective-permute-start.15 = (bf16[1664,512]{1,0:T(8,128)(2,1)S(1)}, bf16[1664,512]{1,0:T(8,128)(2,1)}, u32[]{:S(2)}, u32[]{:S(2)}) collective-permute-start(bf16[1664,512]{1,0:T(8,128)(2,1)S(1)} %hidden.1.refs_1_), channel_id=1, source_target_pairs={{0,2},{1,3},{2,0},{3,1},{4,6},{5,7},{6,4},{7,5},{8,10},{9,11},{10,... | collective-permute-start | bytes 5111816 | tf_op jit(solution)/shard_map/ppermute | solution.py:298
  15.9 11.9 %collective-permute-start.8 = (bf16[128,2048]{1,0:T(8,128)(2,1)S(1)}, bf16[128,2048]{1,0:T(8,128)(2,1)S(1)}, u32[]{:S(2)}, u32[]{:S(2)}) collective-permute-start(bf16[128,2048]{1,0:T(8,128)(2,1)S(1)} %collective-permute-done.refs_1_), channel_id=1, source_target_pairs={{4,8},{8,4},{5,9},{9,5},{6,10},{10,6},{7,11},{11,7},{20,24},{24,20... | collective-permute-start | bytes 1572872 | tf_op jit(solution)/shard_map/ppermute | solution.py:301
  16.6 16.7 %collective-permute-start.9 = (bf16[128,2048]{1,0:T(8,128)(2,1)S(1)}, bf16[128,2048]{1,0:T(8,128)(2,1)S(1)}, u32[]{:S(2)}, u32[]{:S(2)}) collective-permute-start(bf16[128,2048]{1,0:T(8,128)(2,1)S(1)} %collective-permute-done.7.refs_1_.refs_2_), channel_id=1, source_target_pairs={{4,0},{8,12},{5,1},{9,13},{6,2},{10,14},{7,3},{11,15},{20,16},{24,... | collective-permute-start | bytes 1572872 | tf_op jit(solution)/shard_map/ppermute | solution.py:301
  27.8 7.0 %collective-permute-start.3 = (bf16[832,256]{1,0:T(8,128)(2,1)S(1)}, bf16[832,256]{1,0:T(8,128)(2,1)S(1)}, u32[]{:S(2)}, u32[]{:S(2)}) collective-permute-start(bf16[832,256]{1,0:T(8,128)(2,1)S(1)} %get-tuple-element.39), channel_id=1, source_target_pairs={{0,1},{1,0},{2,3},{3,2},{4,5},{5,4},{6,7},{7,6},{8,9},{9,8},{10,11... | collective-permute-start | bytes 1277960 | tf_op jit(solution)/shard_map/ppermute | solution.py:309
  27.9 7.0 %collective-permute-start.4 = (bf16[832,256]{1,0:T(8,128)(2,1)S(1)}, bf16[832,256]{1,0:T(8,128)(2,1)S(1)}, u32[]{:S(2)}, u32[]{:S(2)}) collective-permute-start(bf16[832,256]{1,0:T(8,128)(2,1)S(1)} %get-tuple-element.40), channel_id=1, source_target_pairs={{0,1},{1,0},{2,3},{3,2},{4,5},{5,4},{6,7},{7,6},{8,9},{9,8},{10,11... | collective-permute-start | bytes 1277960 | tf_op jit(solution)/shard_map/ppermute | solution.py:309
  33.3 14.0 %collective-permute-start.10 = (bf16[128,2048]{1,0:T(8,128)(2,1)S(1)}, bf16[128,2048]{1,0:T(8,128)(2,1)S(1)}, u32[]{:S(2)}, u32[]{:S(2)}) collective-permute-start(bf16[128,2048]{1,0:T(8,128)(2,1)S(1)} %collective-permute-done.8.refs_3_.refs_4_), channel_id=1, source_target_pairs={{4,0},{8,12},{5,1},{9,13},{6,2},{10,14},{7,3},{11,15},{20,16},{24,... | collective-permute-start | bytes 1572872 | tf_op jit(solution)/shard_map/ppermute | solution.py:303
  34.8 7.0 %collective-permute-start.1 = (bf16[832,256]{1,0:T(8,128)(2,1)S(1)}, bf16[832,256]{1,0:T(8,128)(2,1)S(1)}, u32[]{:S(2)}, u32[]{:S(2)}) collective-permute-start(bf16[832,256]{1,0:T(8,128)(2,1)S(1)} %get-tuple-element.37), channel_id=1, source_target_pairs={{0,1},{1,0},{2,3},{3,2},{4,5},{5,4},{6,7},{7,6},{8,9},{9,8},{10,11... | collective-permute-start | bytes 1277960 | tf_op jit(solution)/shard_map/ppermute | solution.py:309
  34.9 6.9 %collective-permute-start.2 = (bf16[832,256]{1,0:T(8,128)(2,1)S(1)}, bf16[832,256]{1,0:T(8,128)(2,1)S(1)}, u32[]{:S(2)}, u32[]{:S(2)}) collective-permute-start(bf16[832,256]{1,0:T(8,128)(2,1)S(1)} %get-tuple-element.38), channel_id=1, source_target_pairs={{0,1},{1,0},{2,3},{3,2},{4,5},{5,4},{6,7},{7,6},{8,9},{9,8},{10,11... | collective-permute-start | bytes 1277960 | tf_op jit(solution)/shard_map/ppermute | solution.py:309
  40.2 24.9 %collective-permute-start.6 = (bf16[1664,256]{1,0:T(8,128)(2,1)S(1)}, bf16[1664,256]{1,0:T(8,128)(2,1)S(1)}, u32[]{:S(2)}, u32[]{:S(2)}) collective-permute-start(bf16[1664,256]{1,0:T(8,128)(2,1)S(1)} %get-tuple-element.43), channel_id=1, source_target_pairs={{0,2},{1,3},{2,0},{3,1},{4,6},{5,7},{6,4},{7,5},{8,10},{9,11},{10,... | collective-permute-start | bytes 2555912 | tf_op jit(solution)/shard_map/ppermute | solution.py:311
  52.4 1.8 %collective-permute-start.16 = (bf16[832,256]{1,0:T(8,128)(2,1)S(1)}, bf16[832,256]{1,0:T(8,128)(2,1)S(1)}, u32[]{:S(2)}, u32[]{:S(2)}) collective-permute-start(bf16[832,256]{1,0:T(8,128)(2,1)S(1)} %get-tuple-element.55), channel_id=1, source_target_pairs={{0,1},{1,0},{2,3},{3,2},{4,5},{5,4},{6,7},{7,6},{8,9},{9,8},{10,11... | collective-permute-start | bytes 1277960 | tf_op jit(solution)/shard_map/ppermute | solution.py:317
  52.5 2.4 %collective-permute-start.17 = (bf16[832,256]{1,0:T(8,128)(2,1)S(1)}, bf16[832,256]{1,0:T(8,128)(2,1)S(1)}, u32[]{:S(2)}, u32[]{:S(2)}) collective-permute-start(bf16[832,256]{1,0:T(8,128)(2,1)S(1)} %get-tuple-element.56), channel_id=1, source_target_pairs={{0,1},{1,0},{2,3},{3,2},{4,5},{5,4},{6,7},{7,6},{8,9},{9,8},{10,11... | collective-permute-start | bytes 1277960 | tf_op jit(solution)/shard_map/ppermute | solution.py:317
  53.0 2.5 %collective-permute-start.11 = (bf16[416,256]{1,0:T(8,128)(2,1)S(1)}, bf16[416,256]{1,0:T(8,128)(2,1)S(1)}, u32[]{:S(2)}, u32[]{:S(2)}) collective-permute-start(bf16[416,256]{1,0:T(8,128)(2,1)S(1)} %get-tuple-element.50), channel_id=1, source_target_pairs={{0,1},{1,0},{2,3},{3,2},{4,5},{5,4},{6,7},{7,6},{8,9},{9,8},{10,11... | collective-permute-start | bytes 638984 | tf_op jit(solution)/shard_map/ppermute | solution.py:317
  54.8 11.2 %collective-permute-start.19 = (bf16[1664,512]{1,0:T(8,128)(2,1)}, bf16[1664,512]{1,0:T(8,128)(2,1)S(1)}, u32[]{:S(2)}, u32[]{:S(2)}) collective-permute-start(bf16[1664,512]{1,0:T(8,128)(2,1)} %collective-permute-done.15.refs_3_), channel_id=1, source_target_pairs={{0,1},{1,0},{2,3},{3,2},{4,5},{5,4},{6,7},{7,6},{8,9},{9,8},{10,11... | collective-permute-start | bytes 5111816 | tf_op jit(solution)/shard_map/ppermute | solution.py:320
  55.0 5.2 %collective-permute-start.12 = (bf16[416,256]{1,0:T(8,128)(2,1)S(1)}, bf16[416,256]{1,0:T(8,128)(2,1)S(1)}, u32[]{:S(2)}, u32[]{:S(2)}) collective-permute-start(bf16[416,256]{1,0:T(8,128)(2,1)S(1)} %get-tuple-element.51), channel_id=1, source_target_pairs={{0,1},{1,0},{2,3},{3,2},{4,5},{5,4},{6,7},{7,6},{8,9},{9,8},{10,11... | collective-permute-start | bytes 638984 | tf_op jit(solution)/shard_map/ppermute | solution.py:317
  55.3 6.4 %collective-permute-start.13 = (bf16[416,256]{1,0:T(8,128)(2,1)S(1)}, bf16[416,256]{1,0:T(8,128)(2,1)S(1)}, u32[]{:S(2)}, u32[]{:S(2)}) collective-permute-start(bf16[416,256]{1,0:T(8,128)(2,1)S(1)} %get-tuple-element.52), channel_id=1, source_target_pairs={{0,1},{1,0},{2,3},{3,2},{4,5},{5,4},{6,7},{7,6},{8,9},{9,8},{10,11... | collective-permute-start | bytes 638984 | tf_op jit(solution)/shard_map/ppermute | solution.py:317
  55.5 6.2 %collective-permute-start.14 = (bf16[416,256]{1,0:T(8,128)(2,1)S(1)}, bf16[416,256]{1,0:T(8,128)(2,1)S(1)}, u32[]{:S(2)}, u32[]{:S(2)}) collective-permute-start(bf16[416,256]{1,0:T(8,128)(2,1)S(1)} %get-tuple-element.53), channel_id=1, source_target_pairs={{0,1},{1,0},{2,3},{3,2},{4,5},{5,4},{6,7},{7,6},{8,9},{9,8},{10,11... | collective-permute-start | bytes 638984 | tf_op jit(solution)/shard_map/ppermute | solution.py:317
  60.2 26.7 %collective-permute-start.18 = (bf16[1664,256]{1,0:T(8,128)(2,1)}, bf16[1664,256]{1,0:T(8,128)(2,1)}, u32[]{:S(2)}, u32[]{:S(2)}) collective-permute-start(bf16[1664,256]{1,0:T(8,128)(2,1)} %get-tuple-element.63), channel_id=1, source_target_pairs={{0,2},{1,3},{2,0},{3,1},{4,6},{5,7},{6,4},{7,5},{8,10},{9,11},{10,... | collective-permute-start | bytes 2555912 | tf_op jit(solution)/shard_map/ppermute | solution.py:322
  65.1 0.9 copy-start.1
  66.0 20.9 %copy-start = (bf16[2,1664,512]{2,1,0:T(8,128)(2,1)S(1)}, bf16[2,1664,512]{2,1,0:T(8,128)(2,1)}, u32[]{:S(2)}) copy-start(bf16[2,1664,512]{2,1,0:T(8,128)(2,1)} %refs_0_.11) | copy-start | bytes 10223620
  66.0 20.9 %copy-start.2 = (bf16[1664,256]{1,0:T(8,128)(2,1)S(1)}, bf16[1664,256]{1,0:T(8,128)(2,1)}, u32[]{:S(2)}) copy-start(bf16[1664,256]{1,0:T(8,128)(2,1)} %copy-done.1) | copy-start | bytes 2555908

commit v6 on v5

--- a/solution.py
+++ b/solution.py
@@ -44,16 +44,18 @@
 
 
 def call(kernel, name, meta, grid, ins, outs, scratch=(), alias=None, after=(), weight=1, vmem=16):
+    heads = [] if meta is None else [meta]
     ins = list(ins) + [anywhere(a) for a in after]
     read = len(ins) - len(after)
     aliases = {}
     if alias is not None:
-        aliases = {1 + len(ins): len(outs) - 1}
+        aliases = {len(heads) + len(ins): len(outs) - 1}
         ins.append(in_hbm(alias))
     outs = list(outs) + [TOKEN]
 
-    def body(meta_ref, *refs):
+    def body(*refs):
         refs = list(refs)
+        meta_ref = refs.pop(0) if heads else None
         token = refs.pop(len(ins) + len(outs) - 1)
         token[...] = jnp.zeros_like(token)
         kernel(meta_ref, *refs[:read], *refs[len(ins) :])
@@ -61,14 +63,14 @@
     return pl.pallas_call(
         body,
         grid_spec=pltpu.PrefetchScalarGridSpec(
-            num_scalar_prefetch=1, grid=grid, in_specs=[s for _, s in ins], out_specs=[s for _, s in outs], scratch_shapes=list(scratch)
+            num_scalar_prefetch=len(heads), grid=grid, in_specs=[s for _, s in ins], out_specs=[s for _, s in outs], scratch_shapes=list(scratch)
         ),
         out_shape=[s for s, _ in outs],
         input_output_aliases=aliases,
         compiler_params=pltpu.CompilerParams(vmem_limit_bytes=vmem * MIB),
         cost_estimate=pl.CostEstimate(flops=weight, bytes_accessed=1, transcendentals=0),
         name=name,
-    )(meta, *[a for a, _ in ins])
+    )(*heads, *[a for a, _ in ins])
 
 
 def hidden_rows(acts):
@@ -184,7 +186,7 @@
     if keep:
         outs.append((pltpu.VMEM((total * tile, feats), weight.dtype), in_place))
         scratch = [pltpu.SemaphoreType.DMA((total,))]
-    return call(kernel, "partials", meta, (total,), ins, outs, scratch, after=after, weight=weight_of, vmem=8)
+    return call(kernel, "partials", meta if keep else None, (total,), ins, outs, scratch, after=after, weight=weight_of, vmem=8)
 
 
 def turned_slots(meta, slots, each, feats, after=(), weight=1):
@@ -266,7 +268,7 @@
 
 
 def wait_for(meta, after, weight):
-    return call(lambda meta_ref: None, "arrived", meta, (1,), [], [], after=after, weight=weight, vmem=1)[0]
+    return call(lambda meta_ref: None, "arrived", None, (1,), [], [], after=after, weight=weight, vmem=1)[0]
 
 
 ARRIVALS = ((0, 1, 2, 3), (1, 0, 2, 3), (2, 3, 1, 0), (3, 2, 1, 0))

time: 93.5 us -> 93.7 us (level)
  Pallas kernels: 60.3 us -> 58.2 us
  waiting for transfers between devices: 15.6 us -> 17.3 us
    pallas_call x11, Pallas kernels: 58.1 us -> 56 us  [call(): pl.pallas_call(body, grid_spec=pltpu.PrefetchScalarGridSpec(num_scalar_pr...]
    ppermute x1, waiting for transfers between devices: 0.71 us -> 2.35 us  [two_level(): a_far = across_x(a_sum)]
  transfers between devices with their start and end apart: 20 -> 20, of which waited for: 6 -> 6; matrix products, arithmetic and copies ran while one was open for 0% -> 0% of each run, Pallas kernels for 60% -> 58%
where the time goes in v6:
time: 93.7 us; the launch traced here: 92 us
  Pallas kernels  58.2 us (62%)
  waiting for transfers between devices  17.3 us (18%)
  starting transfers between devices  14.7 us (16%)
  local copies, waits for them, and re-layouts  0.94 us (1%)
    pallas_call x11, Pallas kernels, call(): pl.pallas_call(body, grid_spec=pltpu.PrefetchScalarGridSpec(num_scalar_pr...  56 us
    ppermute x2, waiting for transfers between devices, two_level(): near, second = (in_pairs(cotangent), in_middle(cotangent))  7.55 us
    ppermute x2, waiting for transfers between devices, two_level(): third, outer = (in_middle(near), outwards(second))  4.96 us
    ppermute x2, starting transfers between devices, two_level(): near, second = (in_pairs(cotangent), in_middle(cotangent))  3.77 us
    ppermute x10, starting transfers between devices, two_level(): back = [across_core(p) for p in sent]  2.65 us
    ppermute x1, waiting for transfers between devices, two_level(): a_far = across_x(a_sum)  2.35 us
    pallas_call x1, Pallas kernels, hidden_rows(): pl.pallas_call(kernel, in_specs=[spec], out_specs=pl.BlockSpec(memory_spa...  2.22 us
    ppermute x2, starting transfers between devices, two_level(): third, outer = (in_middle(near), outwards(second))  1.97 us
  transfers between devices with their start and end apart: 20, of which 6 were waited for; matrix products, arithmetic and copies ran while one was open for 0% of the time, Pallas kernels for 58%

profile of v6, /device:TPU:0, one launch (start us, length us, event | category | flops | bytes accessed | tf_op | source)
XLA Modules:
  0.0 92.0 jit_solution(18316225437746448795)
XLA Ops:
  0.7 3.1 %collective-permute-start = (bf16[128,2048]{1,0:T(8,128)(2,1)}, bf16[128,2048]{1,0:T(8,128)(2,1)S(1)}, u32[]{:S(2)}, u32[]{:S(2)}) collective-permute-start(bf16[128,2048]{1,0:T(8,128)(2,1)} %refs_1_.10), channel_id=1, source_target_pairs={{0,4},{4,0},{8,12},{12,8},{1,5},{5,1},{9,13},{13,9},{2,6},{6,2},{1... | collective-permute-start | bytes 1572872 | tf_op jit(solution)/shard_map/ppermute | solution.py:302
  3.8 0.7 collective-permute-start.7
  4.5 2.2 %hidden.1.refs_2_ = bf16[1664,512]{1,0:T(8,128)(2,1)S(1)} custom-call(bf16[2,1664,512]{2,1,0:T(8,128)(2,1)} %refs_1_.11), custom_call_target="tpu_custom_call" | custom-call | flops 1 | bytes 1 | tf_op jit(solution)/shard_map/hidden/pallas_call | solution.py:96
  6.8 1.6 %collective-permute-start.15 = (bf16[1664,512]{1,0:T(8,128)(2,1)S(1)}, bf16[1664,512]{1,0:T(8,128)(2,1)}, u32[]{:S(2)}, u32[]{:S(2)}) collective-permute-start(bf16[1664,512]{1,0:T(8,128)(2,1)S(1)} %hidden.1.refs_2_), channel_id=1, source_target_pairs={{0,2},{1,3},{2,0},{3,1},{4,6},{5,7},{6,4},{7,5},{8,10},{9,11},{10,... | collective-permute-start | bytes 5111816 | tf_op jit(solution)/shard_map/ppermute | solution.py:300
  8.4 7.5 %collective-permute-done.refs_2_ = bf16[128,2048]{1,0:T(8,128)(2,1)S(1)} collective-permute-done((bf16[128,2048]{1,0:T(8,128)(2,1)}, bf16[128,2048]{1,0:T(8,128)(2,1)S(1)}, u32[]{:S(2)}, u32[]{:S(2)}) %collective-permute-start) | collective-permute-done | bytes 524320 | tf_op jit(solution)/shard_map/ppermute | solution.py:302
  15.9 0.7 collective-permute-start.8
  16.6 1.3 %collective-permute-start.9 = (bf16[128,2048]{1,0:T(8,128)(2,1)S(1)}, bf16[128,2048]{1,0:T(8,128)(2,1)S(1)}, u32[]{:S(2)}, u32[]{:S(2)}) collective-permute-start(bf16[128,2048]{1,0:T(8,128)(2,1)S(1)} %collective-permute-done.7.refs_1_.refs_3_), channel_id=1, source_target_pairs={{4,0},{8,12},{5,1},{9,13},{6,2},{10,14},{7,3},{11,15},{20,16},{24,... | collective-permute-start | bytes 1572872 | tf_op jit(solution)/shard_map/ppermute | solution.py:303
  17.9 1.4 %turned.1 = (bf16[2048,256]{1,0:T(8,128)(2,1)S(1)}, f32[8,128]{1,0:T(8,128)}) custom-call(s32[5]{0:T(128)S(1)} %fusion.refs_0_, bf16[128,2048]{1,0:T(8,128)(2,1)S(1)} %copy-done.3, bf16[128,2048]{1,0:T(8,128)(2,1)S(1)} %collective-permute-done.refs_2_), custom_call_target="tpu_custom_call" | custom-call | flops 7000000000 | bytes 1 | tf_op jit(solution)/shard_map/turned/pallas_call | solution.py:63
  19.3 8.4 %partials.6 = (bf16[832,256]{1,0:T(8,128)(2,1)S(1)}, bf16[832,256]{1,0:T(8,128)(2,1)S(1)}, bf16[832,256]{1,0:T(8,128)(2,1)S(1)}, bf16[832,256]{1,0:T(8,128)(2,1)...) custom-call(s32[5]{0:T(128)S(1)} %fusion.refs_0_, bf16[6656,2048]{1,0:T(8,128)(2,1)} %refs_1_.9, ...), custom_call_target="tpu_custom_call" | custom-call | flops 1 | bytes 1 | tf_op jit(solution)/shard_map/partials/pallas_call | solution.py:63
  27.9 0.5 collective-permute-start.4
  28.3 5.0 %collective-permute-done.9.refs_2_.refs_4_ = bf16[128,2048]{1,0:T(8,128)(2,1)S(1)} collective-permute-done((bf16[128,2048]{1,0:T(8,128)(2,1)S(1)}, bf16[128,2048]{1,0:T(8,128)(2,1)S(1)}, u32[]{:S(2)}, u32[]{:S(2)}) %collective-permute-start.9) | collective-permute-done | bytes 524320 | tf_op jit(solution)/shard_map/ppermute | solution.py:303
  33.3 1.5 %collective-permute-start.10 = (bf16[128,2048]{1,0:T(8,128)(2,1)S(1)}, bf16[128,2048]{1,0:T(8,128)(2,1)S(1)}, u32[]{:S(2)}, u32[]{:S(2)}) collective-permute-start(bf16[128,2048]{1,0:T(8,128)(2,1)S(1)} %collective-permute-done.8.refs_3_.refs_5_), channel_id=1, source_target_pairs={{4,0},{8,12},{5,1},{9,13},{6,2},{10,14},{7,3},{11,15},{20,16},{24,... | collective-permute-start | bytes 1572872 | tf_op jit(solution)/shard_map/ppermute | solution.py:305
  34.9 0.5 collective-permute-start.2
  35.4 4.9 %partials.7 = (bf16[1664,256]{1,0:T(8,128)(2,1)S(1)}, bf16[1664,2048]{1,0:T(8,128)(2,1)S(1)}, f32[8,128]{1,0:T(8,128)S(1)}) custom-call(s32[5]{0:T(128)S(1)} %fusion.refs_0_, bf16[6656,2048]{1,0:T(8,128)(2,1)} %refs_1_.9, bf16[2048,256]{1,0:T(8,128)(2,1)S(1)} %get-tuple-element.36.refs_2_, bf16[832,256]{1,0:T(8,128)(2,1)S(1)} %collective-permute-done.3.refs_3_, ...), custom_call_target="tpu_custom_call" | custom-call | flops 1 | bytes 1 | tf_op jit(solution)/shard_map/partials/pallas_call | solution.py:63
  40.2 1.6 %collective-permute-start.6 = (bf16[1664,256]{1,0:T(8,128)(2,1)S(1)}, bf16[1664,256]{1,0:T(8,128)(2,1)S(1)}, u32[]{:S(2)}, u32[]{:S(2)}) collective-permute-start(bf16[1664,256]{1,0:T(8,128)(2,1)S(1)} %get-tuple-element.43), channel_id=1, source_target_pairs={{0,2},{1,3},{2,0},{3,1},{4,6},{5,7},{6,4},{7,5},{8,10},{9,11},{10,... | collective-permute-start | bytes 2555912 | tf_op jit(solution)/shard_map/ppermute | solution.py:313
  41.8 4.9 %partials.8 = (f32[1664,256]{1,0:T(8,128)S(1)}, bf16[1664,2048]{1,0:T(8,128)(2,1)S(1)}, f32[8,128]{1,0:T(8,128)S(1)}) custom-call(s32[5]{0:T(128)S(1)} %fusion.refs_0_, bf16[6656,2048]{1,0:T(8,128)(2,1)} %refs_1_.9, bf16[2048,256]{1,0:T(8,128)(2,1)S(1)} %get-tuple-element.36.refs_2_, bf16[832,256]{1,0:T(8,128)(2,1)S(1)} %collective-permute-done.1.refs_3_, ...), custom_call_target="tpu_custom_call" | custom-call | flops 1 | bytes 1 | tf_op jit(solution)/shard_map/partials/pallas_call | solution.py:63
  46.7 0.6 collective-permute-done.10.refs_4_.refs_6_
  47.3 4.5 %partials.9 = (bf16[832,256]{1,0:T(8,128)(2,1)S(1)}, bf16[832,256]{1,0:T(8,128)(2,1)S(1)}, bf16[416,256]{1,0:T(8,128)(2,1)S(1)}, bf16[416,256]{1,0:T(8,128)(2,1)...) custom-call(bf16[3328,2048]{1,0:T(8,128)(2,1)S(1)} %get-tuple-elemen, ...), custom_call_target="tpu_custom_call" | custom-call | flops 1 | bytes 1 | tf_op jit(solution)/shard_map/partials/pallas_call | solution.py:63
  51.9 0.5 collective-permute-start.17
  52.5 1.2 %collective-permute-done.16.refs_2_ = bf16[832,256]{1,0:T(8,128)(2,1)S(1)} collective-permute-done((bf16[832,256]{1,0:T(8,128)(2,1)S(1)}, bf16[832,256]{1,0:T(8,128)(2,1)S(1)}, u32[]{:S(2)}, u32[]{:S(2)}) %collective-permute-start.16) | collective-permute-done | bytes 426016 | tf_op jit(solution)/shard_map/ppermute | solution.py:319
  53.7 0.6 collective-permute-done.17.refs_3_
  54.3 0.1 collective-permute-start.19
  54.4 0.4 collective-permute-start.12
  54.9 0.4 collective-permute-start.14
  55.3 0.7 token_rows.1
  56.0 3.1 %partials.10 = (bf16[1664,256]{1,0:T(8,128)(2,1)}, f32[8,128]{1,0:T(8,128)S(1)}) custom-call(bf16[1664,2048]{1,0:T(8,128)(2,1)S(1)} %get-tuple-element.54.refs_0_, bf16[2048,256]{1,0:T(8,128)(2,1)S(1)} %get-tuple-element.49.refs_1_, bf16[832,256]{1,0:T(8,128)(2,1)S(1)} %collective-permute-done.16.refs_2_, ...), custom_call_target="tpu_custom_call" | custom-call | flops 1 | bytes 1 | tf_op jit(solution)/shard_map/partials/pallas_call | solution.py:63
  59.1 1.5 %collective-permute-start.18 = (bf16[1664,256]{1,0:T(8,128)(2,1)}, bf16[1664,256]{1,0:T(8,128)(2,1)}, u32[]{:S(2)}, u32[]{:S(2)}) collective-permute-start(bf16[1664,256]{1,0:T(8,128)(2,1)} %get-tuple-element.63), channel_id=1, source_target_pairs={{0,2},{1,3},{2,0},{3,1},{4,6},{5,7},{6,4},{7,5},{8,10},{9,11},{10,... | collective-permute-start | bytes 2555912 | tf_op jit(solution)/shard_map/ppermute | solution.py:324
  60.6 2.1 %partials.11 = (f32[1664,256]{1,0:T(8,128)S(1)}, f32[8,128]{1,0:T(8,128)S(1)}) custom-call(bf16[1664,2048]{1,0:T(8,128)(2,1)S(1)} %get-tuple-element.44.refs_0_, bf16[2048,256]{1,0:T(8,128)(2,1)S(1)} %get-tuple-element.49.refs_1_, bf16[416,256]{1,0:T(8,128)(2,1)S(1)} %collective-permute-done.11.refs_2_, ...), custom_call_target="tpu_custom_call" | custom-call | flops 1 | bytes 1 | tf_op jit(solution)/shard_map/partials/pallas_call | solution.py:63
  62.8 2.4 %collective-permute-done.6.refs_1_.refs_3_ = bf16[1664,256]{1,0:T(8,128)(2,1)S(1)} collective-permute-done((bf16[1664,256]{1,0:T(8,128)(2,1)S(1)}, bf16[1664,256]{1,0:T(8,128)(2,1)S(1)}, u32[]{:S(2)}, u32[]{:S(2)}) %collective-permute-start.6) | collective-permute-done | bytes 852000 | tf_op jit(solution)/shard_map/ppermute | solution.py:313
  65.1 0.9 copy-done.1
  66.0 20.9 %weight_grad.1 = (bf16[6656,2048]{1,0:T(8,128)(2,1)}, f32[8,128]{1,0:T(8,128)S(1)}) custom-call(s32[5]{0:T(128)S(1)} %fusion.refs_0_, bf16[512,2048]{1,0:T(8,128)(2,1)S(1)} %get-tuple-element.64.refs_1_, bf16[1664,512]{1,0:T(8,128)(2,1)S(1)} %hidden.1.refs_2_, bf16[1664,512]{1,0:T(8,128)(2,1)} %collective-permute-done.5.refs_5_.refs_3_, ...), custom_call_target="tpu_custom_call" | custom-call | flops 199999995904 | bytes 1 | tf_op jit(solution)/shard_map/weight_grad/pallas_call | solution.py:63
  87.0 5.1 %gate_grad.1 = (bf16[2,1664,512]{2,1,0:T(8,128)(2,1)}, f32[8,128]{1,0:T(8,128)}) custom-call(s32[5]{0:T(128)S(1)} %fusion.refs_0_, bf16[2,1664,512]{2,1,0:T(8,128)(2,1)S(1)} %copy-done, f32[1664,256]{1,0:T(8,128)S(1)} %get-tuple-element.42.refs_2_, bf16[1664,256]{1,0:T(8,128)(2,1)S(1)} %copy-done.2, f32[1664,256]{1,0:T(8,128)S(1)} %get-tuple-element.62.refs_4_, ...), custom_call_target="tpu_custom_call" | custom-call | flops 1 | bytes 1 | tf_op jit(solution)/shard_map/gate_grad/pallas_call | solution.py:63
  (39 shorter events, 0.6 us)
Async XLA Ops:
  0.6 7.7 %copy-start.4 = (s32[5]{0:T(128)S(1)}, s32[5]{0:T(128)}, u32[]{:S(2)}) copy-start(s32[5]{0:T(128)} %constant.27.clone) | copy-start | bytes 64
  0.6 7.7 %copy-start.5 = (s32[5]{0:T(128)S(1)}, s32[5]{0:T(128)}, u32[]{:S(2)}) copy-start(s32[5]{0:T(128)} %constant.26.clone) | copy-start | bytes 64
  0.7 7.7 %copy-start.6 = (s32[5]{0:T(128)S(1)}, s32[5]{0:T(128)}, u32[]{:S(2)}) copy-start(s32[5]{0:T(128)} %constant.25.clone) | copy-start | bytes 64
  0.7 7.7 %copy-start.7 = (s32[5]{0:T(128)S(1)}, s32[5]{0:T(128)}, u32[]{:S(2)}) copy-start(s32[5]{0:T(128)} %constant.24.clone) | copy-start | bytes 64
  0.7 7.7 %copy-start.8 = (s32[5]{0:T(128)S(1)}, s32[5]{0:T(128)}, u32[]{:S(2)}) copy-start(s32[5]{0:T(128)} %constant.23.clone) | copy-start | bytes 64
  0.7 17.2 %copy-start.3 = (bf16[128,2048]{1,0:T(8,128)(2,1)S(1)}, bf16[128,2048]{1,0:T(8,128)(2,1)}, u32[]{:S(2)}) copy-start(bf16[128,2048]{1,0:T(8,128)(2,1)} %refs_1_.10) | copy-start | bytes 1572868
  0.7 15.2 %collective-permute-start = (bf16[128,2048]{1,0:T(8,128)(2,1)}, bf16[128,2048]{1,0:T(8,128)(2,1)S(1)}, u32[]{:S(2)}, u32[]{:S(2)}) collective-permute-start(bf16[128,2048]{1,0:T(8,128)(2,1)} %refs_1_.10), channel_id=1, source_target_pairs={{0,4},{4,0},{8,12},{12,8},{1,5},{5,1},{9,13},{13,9},{2,6},{6,2},{1... | collective-permute-start | bytes 1572872 | tf_op jit(solution)/shard_map/ppermute | solution.py:302
  3.8 12.8 %collective-permute-start.7 = (bf16[128,2048]{1,0:T(8,128)(2,1)}, bf16[128,2048]{1,0:T(8,128)(2,1)S(1)}, u32[]{:S(2)}, u32[]{:S(2)}) collective-permute-start(bf16[128,2048]{1,0:T(8,128)(2,1)} %refs_1_.10), channel_id=1, source_target_pairs={{4,8},{8,4},{5,9},{9,5},{6,10},{10,6},{7,11},{11,7},{20,24},{24,20... | collective-permute-start | bytes 1572872 | tf_op jit(solution)/shard_map/ppermute | solution.py:302
  6.7 28.7 %collective-permute-start.5 = (bf16[1664,512]{1,0:T(8,128)(2,1)S(1)}, bf16[1664,512]{1,0:T(8,128)(2,1)}, u32[]{:S(2)}, u32[]{:S(2)}) collective-permute-start(bf16[1664,512]{1,0:T(8,128)(2,1)S(1)} %hidden.1.refs_2_), channel_id=1, source_target_pairs={{0,1},{1,0},{2,3},{3,2},{4,5},{5,4},{6,7},{7,6},{8,9},{9,8},{10,11... | collective-permute-start | bytes 5111816 | tf_op jit(solution)/shard_map/ppermute | solution.py:300
  6.8 45.7 %collective-permute-start.15 = (bf16[1664,512]{1,0:T(8,128)(2,1)S(1)}, bf16[1664,512]{1,0:T(8,128)(2,1)}, u32[]{:S(2)}, u32[]{:S(2)}) collective-permute-start(bf16[1664,512]{1,0:T(8,128)(2,1)S(1)} %hidden.1.refs_2_), channel_id=1, source_target_pairs={{0,2},{1,3},{2,0},{3,1},{4,6},{5,7},{6,4},{7,5},{8,10},{9,11},{10,... | collective-permute-start | bytes 5111816 | tf_op jit(solution)/shard_map/ppermute | solution.py:300
  15.9 11.9 %collective-permute-start.8 = (bf16[128,2048]{1,0:T(8,128)(2,1)S(1)}, bf16[128,2048]{1,0:T(8,128)(2,1)S(1)}, u32[]{:S(2)}, u32[]{:S(2)}) collective-permute-start(bf16[128,2048]{1,0:T(8,128)(2,1)S(1)} %collective-permute-done.refs_2_), channel_id=1, source_target_pairs={{4,8},{8,4},{5,9},{9,5},{6,10},{10,6},{7,11},{11,7},{20,24},{24,20... | collective-permute-start | bytes 1572872 | tf_op jit(solution)/shard_map/ppermute | solution.py:303
  16.6 16.7 %collective-permute-start.9 = (bf16[128,2048]{1,0:T(8,128)(2,1)S(1)}, bf16[128,2048]{1,0:T(8,128)(2,1)S(1)}, u32[]{:S(2)}, u32[]{:S(2)}) collective-permute-start(bf16[128,2048]{1,0:T(8,128)(2,1)S(1)} %collective-permute-done.7.refs_1_.refs_3_), channel_id=1, source_target_pairs={{4,0},{8,12},{5,1},{9,13},{6,2},{10,14},{7,3},{11,15},{20,16},{24,... | collective-permute-start | bytes 1572872 | tf_op jit(solution)/shard_map/ppermute | solution.py:303
  27.8 7.0 %collective-permute-start.3 = (bf16[832,256]{1,0:T(8,128)(2,1)S(1)}, bf16[832,256]{1,0:T(8,128)(2,1)S(1)}, u32[]{:S(2)}, u32[]{:S(2)}) collective-permute-start(bf16[832,256]{1,0:T(8,128)(2,1)S(1)} %get-tuple-element.39), channel_id=1, source_target_pairs={{0,1},{1,0},{2,3},{3,2},{4,5},{5,4},{6,7},{7,6},{8,9},{9,8},{10,11... | collective-permute-start | bytes 1277960 | tf_op jit(solution)/shard_map/ppermute | solution.py:311
  27.9 7.0 %collective-permute-start.4 = (bf16[832,256]{1,0:T(8,128)(2,1)S(1)}, bf16[832,256]{1,0:T(8,128)(2,1)S(1)}, u32[]{:S(2)}, u32[]{:S(2)}) collective-permute-start(bf16[832,256]{1,0:T(8,128)(2,1)S(1)} %get-tuple-element.40), channel_id=1, source_target_pairs={{0,1},{1,0},{2,3},{3,2},{4,5},{5,4},{6,7},{7,6},{8,9},{9,8},{10,11... | collective-permute-start | bytes 1277960 | tf_op jit(solution)/shard_map/ppermute | solution.py:311
  33.3 14.0 %collective-permute-start.10 = (bf16[128,2048]{1,0:T(8,128)(2,1)S(1)}, bf16[128,2048]{1,0:T(8,128)(2,1)S(1)}, u32[]{:S(2)}, u32[]{:S(2)}) collective-permute-start(bf16[128,2048]{1,0:T(8,128)(2,1)S(1)} %collective-permute-done.8.refs_3_.refs_5_), channel_id=1, source_target_pairs={{4,0},{8,12},{5,1},{9,13},{6,2},{10,14},{7,3},{11,15},{20,16},{24,... | collective-permute-start | bytes 1572872 | tf_op jit(solution)/shard_map/ppermute | solution.py:305
  34.8 7.0 %collective-permute-start.1 = (bf16[832,256]{1,0:T(8,128)(2,1)S(1)}, bf16[832,256]{1,0:T(8,128)(2,1)S(1)}, u32[]{:S(2)}, u32[]{:S(2)}) collective-permute-start(bf16[832,256]{1,0:T(8,128)(2,1)S(1)} %get-tuple-element.37), channel_id=1, source_target_pairs={{0,1},{1,0},{2,3},{3,2},{4,5},{5,4},{6,7},{7,6},{8,9},{9,8},{10,11... | collective-permute-start | bytes 1277960 | tf_op jit(solution)/shard_map/ppermute | solution.py:311
  34.9 6.9 %collective-permute-start.2 = (bf16[832,256]{1,0:T(8,128)(2,1)S(1)}, bf16[832,256]{1,0:T(8,128)(2,1)S(1)}, u32[]{:S(2)}, u32[]{:S(2)}) collective-permute-start(bf16[832,256]{1,0:T(8,128)(2,1)S(1)} %get-tuple-element.38), channel_id=1, source_target_pairs={{0,1},{1,0},{2,3},{3,2},{4,5},{5,4},{6,7},{7,6},{8,9},{9,8},{10,11... | collective-permute-start | bytes 1277960 | tf_op jit(solution)/shard_map/ppermute | solution.py:311
  40.2 24.9 %collective-permute-start.6 = (bf16[1664,256]{1,0:T(8,128)(2,1)S(1)}, bf16[1664,256]{1,0:T(8,128)(2,1)S(1)}, u32[]{:S(2)}, u32[]{:S(2)}) collective-permute-start(bf16[1664,256]{1,0:T(8,128)(2,1)S(1)} %get-tuple-element.43), channel_id=1, source_target_pairs={{0,2},{1,3},{2,0},{3,1},{4,6},{5,7},{6,4},{7,5},{8,10},{9,11},{10,... | collective-permute-start | bytes 2555912 | tf_op jit(solution)/shard_map/ppermute | solution.py:313
  51.8 1.8 %collective-permute-start.16 = (bf16[832,256]{1,0:T(8,128)(2,1)S(1)}, bf16[832,256]{1,0:T(8,128)(2,1)S(1)}, u32[]{:S(2)}, u32[]{:S(2)}) collective-permute-start(bf16[832,256]{1,0:T(8,128)(2,1)S(1)} %get-tuple-element.55), channel_id=1, source_target_pairs={{0,1},{1,0},{2,3},{3,2},{4,5},{5,4},{6,7},{7,6},{8,9},{9,8},{10,11... | collective-permute-start | bytes 1277960 | tf_op jit(solution)/shard_map/ppermute | solution.py:319
  51.9 2.4 %collective-permute-start.17 = (bf16[832,256]{1,0:T(8,128)(2,1)S(1)}, bf16[832,256]{1,0:T(8,128)(2,1)S(1)}, u32[]{:S(2)}, u32[]{:S(2)}) collective-permute-start(bf16[832,256]{1,0:T(8,128)(2,1)S(1)} %get-tuple-element.56), channel_id=1, source_target_pairs={{0,1},{1,0},{2,3},{3,2},{4,5},{5,4},{6,7},{7,6},{8,9},{9,8},{10,11... | collective-permute-start | bytes 1277960 | tf_op jit(solution)/shard_map/ppermute | solution.py:319
  52.4 2.5 %collective-permute-start.11 = (bf16[416,256]{1,0:T(8,128)(2,1)S(1)}, bf16[416,256]{1,0:T(8,128)(2,1)S(1)}, u32[]{:S(2)}, u32[]{:S(2)}) collective-permute-start(bf16[416,256]{1,0:T(8,128)(2,1)S(1)} %get-tuple-element.50), channel_id=1, source_target_pairs={{0,1},{1,0},{2,3},{3,2},{4,5},{5,4},{6,7},{7,6},{8,9},{9,8},{10,11... | collective-permute-start | bytes 638984 | tf_op jit(solution)/shard_map/ppermute | solution.py:319
  54.3 11.8 %collective-permute-start.19 = (bf16[1664,512]{1,0:T(8,128)(2,1)}, bf16[1664,512]{1,0:T(8,128)(2,1)S(1)}, u32[]{:S(2)}, u32[]{:S(2)}) collective-permute-start(bf16[1664,512]{1,0:T(8,128)(2,1)} %collective-permute-done.15.refs_4_), channel_id=1, source_target_pairs={{0,1},{1,0},{2,3},{3,2},{4,5},{5,4},{6,7},{7,6},{8,9},{9,8},{10,11... | collective-permute-start | bytes 5111816 | tf_op jit(solution)/shard_map/ppermute | solution.py:322
  54.4 4.7 %collective-permute-start.12 = (bf16[416,256]{1,0:T(8,128)(2,1)S(1)}, bf16[416,256]{1,0:T(8,128)(2,1)S(1)}, u32[]{:S(2)}, u32[]{:S(2)}) collective-permute-start(bf16[416,256]{1,0:T(8,128)(2,1)S(1)} %get-tuple-element.51), channel_id=1, source_target_pairs={{0,1},{1,0},{2,3},{3,2},{4,5},{5,4},{6,7},{7,6},{8,9},{9,8},{10,11... | collective-permute-start | bytes 638984 | tf_op jit(solution)/shard_map/ppermute | solution.py:319
  54.8 5.8 %collective-permute-start.13 = (bf16[416,256]{1,0:T(8,128)(2,1)S(1)}, bf16[416,256]{1,0:T(8,128)(2,1)S(1)}, u32[]{:S(2)}, u32[]{:S(2)}) collective-permute-start(bf16[416,256]{1,0:T(8,128)(2,1)S(1)} %get-tuple-element.52), channel_id=1, source_target_pairs={{0,1},{1,0},{2,3},{3,2},{4,5},{5,4},{6,7},{7,6},{8,9},{9,8},{10,11... | collective-permute-start | bytes 638984 | tf_op jit(solution)/shard_map/ppermute | solution.py:319
  54.9 5.7 %collective-permute-start.14 = (bf16[416,256]{1,0:T(8,128)(2,1)S(1)}, bf16[416,256]{1,0:T(8,128)(2,1)S(1)}, u32[]{:S(2)}, u32[]{:S(2)}) collective-permute-start(bf16[416,256]{1,0:T(8,128)(2,1)S(1)} %get-tuple-element.53), channel_id=1, source_target_pairs={{0,1},{1,0},{2,3},{3,2},{4,5},{5,4},{6,7},{7,6},{8,9},{9,8},{10,11... | collective-permute-start | bytes 638984 | tf_op jit(solution)/shard_map/ppermute | solution.py:319
  59.1 27.9 %collective-permute-start.18 = (bf16[1664,256]{1,0:T(8,128)(2,1)}, bf16[1664,256]{1,0:T(8,128)(2,1)}, u32[]{:S(2)}, u32[]{:S(2)}) collective-permute-start(bf16[1664,256]{1,0:T(8,128)(2,1)} %get-tuple-element.63), channel_id=1, source_target_pairs={{0,2},{1,3},{2,0},{3,1},{4,6},{5,7},{6,4},{7,5},{8,10},{9,11},{10,... | collective-permute-start | bytes 2555912 | tf_op jit(solution)/shard_map/ppermute | solution.py:324
  65.1 0.9 copy-start.1
  66.0 21.0 %copy-start = (bf16[2,1664,512]{2,1,0:T(8,128)(2,1)S(1)}, bf16[2,1664,512]{2,1,0:T(8,128)(2,1)}, u32[]{:S(2)}) copy-start(bf16[2,1664,512]{2,1,0:T(8,128)(2,1)} %refs_1_.11) | copy-start | bytes 10223620
  66.0 21.0 %copy-start.2 = (bf16[1664,256]{1,0:T(8,128)(2,1)S(1)}, bf16[1664,256]{1,0:T(8,128)(2,1)}, u32[]{:S(2)}) copy-start(bf16[1664,256]{1,0:T(8,128)(2,1)} %copy-done.1) | copy-start | bytes 2555908
